TPU v7x, 32 devices: a whole 2x2x4 slice. The times are simulated.
32 devices in a mesh: role: 2 (over x), dp: 4 (over y, core), vocab: 4 (over z).
Axes of the slice: x: 2, y: 2, z: 4, core: 2. Of those that a mesh axis runs over, the one named last changes fastest.
Arguments:
- hidden: bfloat16 [4096, 1792], P(('role', 'dp'))
- out_weight: bfloat16 [1792, 9728], P(None, 'vocab')
- teacher_logits: bfloat16 [4096, 9728], P(('role', 'dp'), 'vocab')
- token_ids: int32 [4096], P(('role', 'dp')), may hold values from 0 to 9727
- loss_mask: int32 [4096], P(('role', 'dp')), may hold values from 0 to 1
Outputs:
- token_kl: float32 [4096], P(('role', 'dp'))
- chosen_logprob: float32 [4096], P(('role', 'dp'))
- grad_hidden: bfloat16 [4096, 1792], P(('role', 'dp', 'vocab'))
- grad_weight: bfloat16 [1792, 9728], P(('role', 'dp'), 'vocab')
All inputs are finite; a program needn't handle non-finite values.
Results may differ from a plain program's by a relative error of at most 0.02.
Values may be sent and summed in bfloat16 or wider, within the bound.
No kernel may reach another device: no remote copies, remote signals or barrier semaphores. Data moves between devices by JAX's collectives and lax.ppermute only.
A program may use at most 128 MiB of HBM per device.

v0:
```python
import jax
import jax.numpy as jnp
from jax import lax
from jax.sharding import PartitionSpec as P


def from_partner(shard, axis, bit):
    return lax.ppermute(shard, axis, [(i, i ^ 1 << bit) for i in range(lax.axis_size(axis))])


def local(hidden, out_weight, teacher_logits, token_ids, loss_mask):
    shard_width = out_weight.shape[1]
    teacher_tile = from_partner(teacher_logits, "role", 0)
    logits = jnp.dot(hidden, out_weight, preferred_element_type=jnp.float32)
    mask_values = loss_mask.astype(jnp.float32)
    mask_total = jnp.maximum(lax.psum(jnp.sum(mask_values), ("role", "dp")), 1.0)
    columns = lax.axis_index("vocab") * shard_width + lax.iota(jnp.int32, shard_width)
    pick_local = jnp.sum(jnp.where(token_ids[:, None] == columns[None, :], logits, 0.0), axis=1)
    teacher = teacher_tile.astype(jnp.float32)
    logit_gap = logits - teacher
    student_top, teacher_top = lax.pmax(
        (jnp.max(logits, axis=1), jnp.max(teacher, axis=1)), "vocab"
    )
    shifted = jnp.exp(logits - student_top[:, None])
    student_sum, gap_sum, teacher_sum, picked = lax.psum(
        (
            jnp.sum(shifted, axis=1),
            jnp.sum(shifted * logit_gap, axis=1),
            jnp.sum(jnp.exp(teacher - teacher_top[:, None]), axis=1),
            pick_local,
        ),
        "vocab",
    )
    lse_student = student_top + jnp.log(student_sum)
    lse_teacher = teacher_top + jnp.log(teacher_sum)
    lse_diff = lse_student - lse_teacher
    token_kl = gap_sum / student_sum - lse_diff
    chosen_logprob = picked - lse_student
    probs = jnp.exp(logits - lse_student[:, None])
    grad_logits = (
        (mask_values / mask_total)[:, None]
        * probs
        * (logit_gap - lse_diff[:, None] - token_kl[:, None])
    ).astype(jnp.bfloat16)
    block = grad_logits
    grad_hidden = lax.psum_scatter(
        lax.dot_general(
            block, out_weight, (((1,), (1,)), ((), ())), preferred_element_type=jnp.float32
        ).astype(jnp.bfloat16),
        "vocab",
        scatter_dimension=0,
        tiled=True,
    )
    block = hidden
    grad_weight = lax.psum_scatter(
        lax.dot_general(
            block, grad_logits, (((0,), (0,)), ((), ())), preferred_element_type=jnp.float32
        ).astype(jnp.bfloat16),
        ("role", "dp"),
        scatter_dimension=0,
        tiled=True,
    )
    return (token_kl, chosen_logprob, grad_hidden, grad_weight)


def solution(mesh):
    return jax.shard_map(
        local,
        mesh=mesh,
        in_specs=(
            P(("role", "dp"), None),
            P(None, "vocab"),
            P(("role", "dp"), "vocab"),
            P(("role", "dp")),
            P(("role", "dp")),
        ),
        out_specs=(
            P(("role", "dp")),
            P(("role", "dp")),
            P(("role", "dp", "vocab"), None),
            P(("role", "dp"), "vocab"),
        ),
        check_vma=False,
    )
```

profile of v0, /device:TPU:0, one launch (start us, length us, event | category | flops | bytes accessed | tf_op | source)
XLA Modules:
  0.0 246.6 jit_solution(191884829169770630)
XLA Ops:
  7.2 0.0 copy-start
  7.2 0.0 reduce-scatter.5.cloned.1.call-start
  7.2 3.0 %collective-permute-start = (bf16[512,2432]{1,0:T(8,128)(2,1)}, bf16[512,2432]{1,0:T(8,128)(2,1)}, u32[]{:S(2)}, u32[]{:S(2)}) collective-permute-start(bf16[512,2432]{1,0:T(8,128)(2,1)} %param.7), channel_id=1, source_target_pairs={{0,16},{16,0},{1,17},{17,1},{2,18},{18,2},{3,19},{19,3},{4,20},{20... | collective-permute-start | bytes 7471112 | tf_op jit(solution)/shard_map/ppermute | solution.py:8
  10.2 1.3 convert_reduce_fusion
  11.5 62.1 %psum.39 = f32[]{:T(128)} all-reduce(f32[]{:T(128)} %convert_reduce_fusion), channel_id=1, replica_groups=mesh['role'=2,'dp'=4,'vocab'=4] {'role','dp'}, use_global_device_ids=true, to_apply=%region_13.14 | all-reduce | flops 1 | bytes 8 | tf_op jit(solution)/shard_map/psum | solution.py:16
  74.3 0.7 convert_divide_fusion
  75.0 0.0 copy-done
  75.0 0.0 copy-start.1
  75.0 10.2 %fusion.5 = (f32[512]{0:T(512)S(1)}, f32[512,2432]{1,0:T(8,128)}) fusion(bf16[512,1792]{1,0:T(8,128)(2,1)S(1)} %copy-done, bf16[1792,2432]{1,0:T(8,128)(2,1)} %param.6), kind=kOutput, calls=%fused_computation.19 | convolution fusion | flops 4463984128 | bytes 15534080 | tf_op jit(solution)/shard_map/dot_general | solution.py:14
  85.2 0.0 collective-permute-done
  85.2 2.1 reduce_max.24
  87.3 12.0 %all-reduce.1 = (f32[512]{0:T(512)S(1)}, f32[512]{0:T(512)S(1)}) all-reduce(f32[512]{0:T(512)S(1)} %get-tuple-element.26, bf16[512]{0:T(512)(128)(2,1)S(1)} %reduce_max.24), channel_id=1, replica_groups=mesh['role'=2,'dp'=4,'vocab'=4] {'vocab'}, use_global_device_ids=true, to_apply=%region_1.0 | all-reduce | flops 1024 | bytes 7168 | tf_op jit(solution)/shard_map/pmax | solution.py:21
  99.3 0.0 copy-done.1
  99.3 5.0 %multiply_reduce_fusion = (f32[512]{0:T(512)S(1)}, f32[512]{0:T(512)S(1)}, f32[512]{0:T(512)S(1)}, f32[512]{0:T(512)S(1)}) fusion(f32[512,2432]{1,0:T(8,128)} %get-tuple-element.27, bf16[512,2432]{1,0:T(8,128)(2,1)} %collective-permute-done, f32[512]{0:T(512)S(1)} %get-tuple-element.20, s32[2432]{0:T(1024)S(1)} %iota_add_fusion, s32[512]{0:T(512)S(1)} %copy-done.1, ...), kind=kLoop, calls=%fused_computation.8 | loop fusion | flops 13694976 | bytes 7495168 | tf_op jit(solution)/shard_map/reduce_sum | solution.py:28
  104.3 8.5 %all-reduce = (f32[512]{0:T(512)S(1)}, f32[512]{0:T(512)S(1)}, f32[512]{0:T(512)S(1)}, f32[512]{0:T(512)S(1)}) all-reduce(f32[512]{0:T(512)S(1)} %get-tuple-element.13, f32[512]{0:T(512)S(1)} %get-tuple-element.15, f32[512]{0:T(512)S(1)} %get-tuple-element.12, ...), channel_id=1, replica_groups=mesh['role'=2,'dp'=4,'vocab'=4] {'vocab'}, use_global_device_ids=true, to_apply=%region_5.6 | all-reduce | flops 2048 | bytes 16384 | tf_op jit(solution)/shard_map/psum | solution.py:25
  112.8 0.6 fusion.4
  113.4 0.0 copy-start.2
  113.5 12.7 %convolution_convert_fusion.1 = bf16[512,1792]{1,0:T(8,128)(2,1)} fusion(bf16[1792,2432]{1,0:T(8,128)(2,1)} %param.6, f32[512,2432]{1,0:T(8,128)} %get-tuple-element.27, bf16[512,2432]{1,0:T(8,128)(2,1)} %collective-permute-done, f32[512]{0:T(512)S(1)} %get-tuple-element.24, f32[512]{0:T(512)S(1)} %get-tuple-element.25, f32[512]{0:T(512)S(1)} %get-tuple-element.23, ...), kind=kOutput, calls=%fused_computation.11 | convolution fusion | flops 4473618432 | bytes 18030592 | tf_op jit(solution)/shard_map/dot_general | solution.py:47
  126.1 0.0 reduce-scatter.5.cloned.1.call-update
  126.2 0.2 reduce-scatter.7.cloned.1.call-start
  126.4 0.0 copy-done.2
  126.4 12.5 %fusion = bf16[1792,2432]{0,1:T(8,128)(2,1)} fusion(bf16[512,1792]{1,0:T(8,128)(2,1)S(1)} %copy-done, f32[512,2432]{1,0:T(8,128)} %get-tuple-element.27, bf16[512,2432]{1,0:T(8,128)(2,1)} %collective-permute-done, f32[512]{0:T(512)S(1)} %get-tuple-element.24, f32[512]{0:T(512)S(1)} %get-tuple-element.25, f32[512]{0:T(512)S(1)} %get-tuple-element.23, ...), kind=kOutput, calls=%fused_computation.1 | convolution fusion | flops 4477059072 | bytes 18030592 | tf_op jit(solution)/shard_map/dot_general | solution.py:56
  138.9 12.5 %copy.11 = bf16[1792,2432]{1,0:T(8,128)(2,1)} copy(bf16[1792,2432]{0,1:T(8,128)(2,1)} %fusion) | data formatting | bytes 17432576
  151.5 0.0 reduce-scatter.7.cloned.1.call-update
  151.5 12.0 %reduce-scatter.5.cloned.1.call-done = bf16[128,1792]{1,0:T(8,128)(2,1)} async-done(((bf16[512,1792]{1,0:T(8,128)(2,1)}), bf16[128,1792]{1,0:T(8,128)(2,1)}) %reduce-scatter.5.cloned.1.call-update) | async-done | bytes 458768 | tf_op jit(solution)/shard_map/reduce_scatter | solution.py:46
  163.5 76.3 %reduce-scatter.7.cloned.1.call-done = bf16[224,2432]{1,0:T(8,128)(2,1)} async-done(((bf16[1792,2432]{1,0:T(8,128)(2,1)}), bf16[224,2432]{1,0:T(8,128)(2,1)}) %reduce-scatter.7.cloned.1.call-update) | async-done | bytes 1089552
  (2 shorter events, 0.0 us)
Async XLA Ops:
  7.2 67.9 %copy-start = (bf16[512,1792]{1,0:T(8,128)(2,1)S(1)}, bf16[512,1792]{1,0:T(8,128)(2,1)}, u32[]{:S(2)}) copy-start(bf16[512,1792]{1,0:T(8,128)(2,1)} %param.5) | copy-start | bytes 5505028
  7.2 156.3 %reduce-scatter.5.cloned.1.call-start = ((), (), s32[]{:S(2)}) async-start(), calls=%async_computation.2 | async-start | bytes 2293760 | tf_op jit(solution)/shard_map/reduce_scatter | solution.py:46
  7.2 78.0 %collective-permute-start = (bf16[512,2432]{1,0:T(8,128)(2,1)}, bf16[512,2432]{1,0:T(8,128)(2,1)}, u32[]{:S(2)}, u32[]{:S(2)}) collective-permute-start(bf16[512,2432]{1,0:T(8,128)(2,1)} %param.7), channel_id=1, source_target_pairs={{0,16},{16,0},{1,17},{17,1},{2,18},{18,2},{3,19},{19,3},{4,20},{20... | collective-permute-start | bytes 7471112 | tf_op jit(solution)/shard_map/ppermute | solution.py:8
  75.0 24.3 %copy-start.1 = (s32[512]{0:T(512)S(1)}, s32[512]{0:T(512)}, u32[]{:S(2)}) copy-start(s32[512]{0:T(512)} %param.8) | copy-start | bytes 6148
  113.4 13.0 %copy-start.2 = (f32[512]{0:T(512)}, f32[512]{0:T(512)S(1)}, u32[]{:S(2)}) copy-start(f32[512]{0:T(512)S(1)} %get-tuple-element.24) | copy-start | bytes 6148
  126.2 113.6 %reduce-scatter.7.cloned.1.call-start = ((), (), s32[]{:S(2)}) async-start(), calls=%async_computation.3 | async-start | bytes 9805824
Sparse Core Ops, SparseCore 0:
  126.3 37.1 reduce-scatter.4
  167.7 72.0 reduce-scatter.6
where the time goes:
time: 247 us
  waiting for transfers between devices  88.3 us (36%)
  blocking collectives  82.6 us (33%)
  matrix products  35.4 us (14%)
  between operations  14.7 us (6%)
  local copies, waits for them, and re-layouts  12.5 us (5%)
  other arithmetic  9.74 us (4%)
  starting transfers between devices  3.26 us (1%)
    unnamed x3, waiting for transfers between devices  76.3 us
    psum x1, blocking collectives, local(): lax.psum(jnp.sum(mask_values), ('role', 'dp'))  62.1 us
    dot_general x1, matrix products, local(): lax.dot_general(block, out_weight, (((1,), (1,)), ((), ())), preferred_el...  12.7 us
    unnamed x7, local copies, waits for them, and re-layouts  12.5 us
    dot_general x1, matrix products, local(): lax.dot_general(block, grad_logits, (((0,), (0,)), ((), ())), preferred_e...  12.5 us
    reduce_scatter x1, waiting for transfers between devices, local(): lax.psum_scatter(lax.dot_general(block, out_weight, (((1,), (1,)), ((), (...  12 us
    pmax x1, blocking collectives, local(): lax.pmax((jnp.max(logits, axis=1), jnp.max(teacher, axis=1)), 'vocab')  12 us
    dot_general x1, matrix products, local(): logits = jnp.dot(hidden, out_weight, preferred_element_type=jnp.float32)  10.2 us
  transfers between devices with their start and end apart: 3, of which 2 were waited for; matrix products, arithmetic and copies ran while one was open for 15% of the time, Pallas kernels for 0%

commit v1 on v0

v1 whole, which is shorter than its diff:
```python
import functools

import jax
import jax.numpy as jnp
from jax import lax
from jax.experimental import pallas as pl
from jax.experimental.pallas import tpu as pltpu
from jax.sharding import PartitionSpec as P

F32 = jnp.float32
BF16 = jnp.bfloat16
VMEM_LIMIT = 18 * 1024 * 1024
LANES = 128
STEP = 16
LONG = 20_000_000_000
COST = 2_000_000_000
DIGIT = 128
STATS = 8
QUARTERS = 4


def exchange(array, axes, size, partner):
    return lax.ppermute(array, axes, [(i, partner(i)) for i in range(size)])


def xor_swap(array, axis, mask):
    return exchange(array, axis, lax.axis_size(axis), lambda i: i ^ mask)


def shape(dims, dtype):
    return jax.ShapeDtypeStruct(dims, dtype)


def call(kernel, name, outs, arrays, scratch=(), after=(), far=(), aliases=False, flops=1024):
    skip = len(after)
    on_chip = pl.BlockSpec(memory_space=pltpu.VMEM)
    in_hbm = pl.BlockSpec(memory_space=pltpu.HBM)
    return pl.pallas_call(
        lambda *refs: kernel(*refs[skip:]),
        in_specs=[pl.BlockSpec(memory_space=pl.ANY)] * (skip + len(far))
        + [on_chip] * len(arrays),
        out_specs=[on_chip if isinstance(o, jax.ShapeDtypeStruct) else in_hbm for o in outs],
        out_shape=outs,
        scratch_shapes=list(scratch),
        input_output_aliases={skip: 0} if aliases else {},
        compiler_params=pltpu.CompilerParams(vmem_limit_bytes=VMEM_LIMIT),
        cost_estimate=pl.CostEstimate(flops=flops, bytes_accessed=1024, transcendentals=0),
        name=name,
    )(*after, *far, *arrays)


def column_chunks(width, shares):
    bounds = [width // LANES * sum(shares[:i]) // sum(shares) for i in range(len(shares) + 1)]
    return [(a * LANES, (b - a) * LANES) for a, b in zip(bounds, bounds[1:])]


def tiles(start, size, step):
    return [(at, min(step, start + size - at)) for at in range(start, start + size, step)]


def spread(row):
    return jnp.broadcast_to(row, (LANES, row.shape[1])).T


def lane_sum(ref):
    return jnp.sum(ref[...].T, axis=0, keepdims=True)


def fold(row):
    return jnp.concatenate([row[:, at : at + LANES] for at in range(0, row.shape[1], LANES)])


def unfold(values, k, count):
    each = count // LANES
    rows = [values[k * each + i : k * each + i + 1] for i in range(each)]
    return jnp.concatenate(rows, axis=1)


def pad_rows(values, rows):
    return jnp.concatenate([values, jnp.zeros((rows - values.shape[0], LANES), values.dtype)])


def row_steps(total, group):
    block = total // QUARTERS
    inside = block // 2

    def at(i):
        quarter, rest = i * STEP // inside, i * STEP % inside
        here = pl.multiple_of(i * STEP, STEP)
        there = pl.multiple_of(quarter * block + group * inside + rest, STEP)
        return pl.ds(here, STEP), pl.ds(there, STEP)

    return at


def copy_pairs(source, target, parts=4):
    rows = source.shape[0]
    size = max(STEP, -(-rows // parts) // STEP * STEP)
    return [
        (source.at[at : min(at + size, rows), :], target.at[at : min(at + size, rows), :])
        for at in range(0, rows, size)
    ]


def run_copies(pairs, done):
    copies = [pltpu.make_async_copy(*pair, done.at[i]) for i, pair in enumerate(pairs)]
    for copy in copies:
        copy.start()
    for copy in copies:
        copy.wait()


def near_of(index):
    return index ^ (2 if index & 1 else 4)


def far_of(index):
    return index ^ (4 if index & 1 else 2)


def weight_order():
    me = lax.axis_index("role") * 4 + lax.axis_index("dp")
    order = []
    for index in (me ^ 1, me):
        near = 4 - 2 * (index & 1)
        far = 6 - near
        order += [index ^ near ^ far, index ^ near, index ^ far, index]
    return order


def hidden_order(vocab_size):
    order = [lax.axis_index("vocab")]
    bit = vocab_size // 2
    while bit:
        order = [o ^ bit for o in order] + order
        bit //= 2
    return order


def pick_kernel(hidden, *refs, pieces, extra):
    sources, refs = refs[:extra], refs[extra:]
    outs, refs = refs[: len(pieces)], refs[len(pieces) :]
    landed, done = refs[:-1], refs[-1]
    odd = lax.axis_index("vocab") & 1
    block = hidden.shape[0] // QUARTERS
    size = block // 2
    pairs = list(zip(sources, landed))
    for (group, k), out in zip(pieces, outs):
        at = pl.multiple_of((2 * odd + k) * block + group * size, size)
        pairs += copy_pairs(hidden.at[pl.ds(at, size), :], out.at[:, : hidden.shape[1]])
    run_copies(pairs, done)
    if extra:
        ids, mask = (ref[...] for ref in landed)
        rest, terms = ids, []
        for _ in range(3):
            terms.append(rest & (DIGIT - 1))
            rest = rest >> (DIGIT.bit_length() - 1)
        values = jnp.concatenate([fold(v) for v in (*terms, mask)])
        outs[0][:, outs[0].shape[1] - LANES :] = pad_rows(values.astype(F32), size).astype(BF16)


def pick_rows(hidden, pieces, extra=(), after=()):
    rows, features = hidden.shape
    size = rows // QUARTERS // 2
    far = [pltpu.with_memory_space_constraint(a, pltpu.HBM) for a in (hidden, *extra)]
    more = [LANES if extra and i == 0 else 0 for i in range(len(pieces))]
    return call(
        functools.partial(pick_kernel, pieces=pieces, extra=len(extra)),
        "pick_rows",
        [shape((size, features + n), BF16) for n in more],
        [],
        [pltpu.VMEM((1, rows), jnp.int32)] * len(extra)
        + [pltpu.SemaphoreType.DMA((4 * len(pieces) + len(extra),))],
        after,
        far,
        flops=LONG,
    )


def unpack_kernel(packed, piece, side):
    features, count = piece.shape[1], side.shape[1]
    piece[...] = packed[:, :features]
    values = packed[:, features:].astype(F32)
    digits = [unfold(values, k, count) for k in range(4)]
    side[0:1, :] = digits[0] + DIGIT * (digits[1] + DIGIT * digits[2])
    side[1:2, :] = digits[3]


def unpack_rows(packed, rows):
    dims = (packed.shape[0], packed.shape[1] - LANES)
    return call(
        unpack_kernel,
        "unpack_rows",
        [shape(dims, BF16), shape((2, rows), F32)],
        [packed],
    )


def teacher_kernel(teacher, out, top, total):
    rows, width = teacher.shape

    @pl.loop(0, rows // STEP, unroll=2)
    def _(i):
        at = pl.ds(pl.multiple_of(i * STEP, STEP), STEP)
        best = teacher[at, 0:LANES]
        for start, size in tiles(LANES, width - LANES, LANES):
            best = jnp.maximum(best, teacher[at, start : start + size])
        top[at, :] = best.astype(F32)

    top_row = jnp.max(top[...].T, axis=0, keepdims=True)
    top[...] = spread(top_row)

    @pl.loop(0, rows // STEP, unroll=2)
    def _(i):
        at = pl.ds(pl.multiple_of(i * STEP, STEP), STEP)
        shift = top[at, :]
        acc = jnp.zeros((STEP, LANES), F32)
        for start, size in tiles(0, width, LANES):
            acc += jnp.exp(teacher[at, start : start + size].astype(F32) - shift)
        total[at, :] = acc

    out[...] = jnp.concatenate(
        [jnp.zeros((3, rows), F32), top_row, lane_sum(total), jnp.zeros((3, rows), F32)]
    )


def teacher_stats(teacher, after=()):
    rows, width = teacher.shape
    return call(
        teacher_kernel,
        "teacher_stats",
        [shape((STATS, rows), F32)],
        [teacher],
        [pltpu.VMEM((rows, LANES), F32)] * 2,
        after,
        flops=LONG,
    )[0]


def pass_on(array, after):
    outs = [shape(array.shape, array.dtype)]
    return call(lambda *refs: None, "pass_on", outs, [], (), after, [array], True)[0]


def count_kernel(side, mask, out):
    total = jnp.sum(side[1:2, :]) + jnp.sum(mask[...].astype(F32))
    out[...] = jnp.full(out.shape, total)


def sum_kernel(first, second, out):
    out[...] = first[...] + second[...]


def count_rows(side, mask):
    return call(count_kernel, "count_rows", [shape((8, LANES), F32)], [side, mask])[0]


def sum_rows(first, second):
    return call(sum_kernel, "sum_rows", [shape((8, LANES), F32)], [first, second])[0]


def gather_rows(direct, other, rows_in):
    odd = lax.axis_index("vocab") & 1
    half = rows_in.shape[0] // 2
    for first, refs in ((odd, direct), (1 - odd, other)):
        for i, ref in enumerate(refs):
            count = ref.shape[0]
            at = pl.multiple_of(first * half + i * count, count)
            rows_in[pl.ds(at, count), :] = ref[...]


def turn_rows(direct, other, after=()):
    count = len(direct)
    rows, features = 2 * count * direct[0].shape[0], direct[0].shape[1]

    def kernel(*refs):
        out, rows_in, turned = refs[2 * count :]
        gather_rows(refs[:count], refs[count : 2 * count], rows_in)
        turned[...] = rows_in[...].T
        height = features // 8
        for i, block in enumerate(weight_order()):
            at = pl.ds(pl.multiple_of(block * height, STEP), height)
            out[i * height : (i + 1) * height, :] = turned[at, :]

    return call(
        kernel,
        "turn_rows",
        [shape((features, rows), BF16)],
        [*direct, *other],
        [pltpu.VMEM((rows, features), BF16), pltpu.VMEM((features, rows), BF16)],
        after,
    )[0]


def logits_kernel(direct, other, weight, teacher, side, known, *refs):
    group = len(refs) - 8
    first, refs = refs[:group], refs[group:]
    logits, stats, rows_in, top, total, gap, picked, chosen = refs
    rows, width = logits.shape
    vocab = lax.axis_index("vocab")
    gather_rows(direct, other, rows_in)
    value = rows_in[...]

    best = None
    for start, size in tiles(0, width, 2 * LANES):
        tile = jnp.dot(value, weight[:, start : start + size], preferred_element_type=F32)
        logits[:, start : start + size] = tile
        for at in range(0, size, LANES):
            part = tile[:, at : at + LANES]
            best = part if best is None else jnp.maximum(best, part)
    top[...] = spread(jnp.max(best.T, axis=0, keepdims=True))

    ids = side[0:1, :] - (vocab * width).astype(F32)
    chosen[...] = spread(ids) - lax.broadcasted_iota(
        jnp.int32, chosen.shape, 1
    ).astype(F32)
    steps = row_steps(2 * rows, group)
    for ref in (total, gap, picked):
        ref[...] = jnp.zeros(ref.shape, F32)

    @pl.loop(0, rows // STEP, unroll=2)
    def _(i):
        here, there = steps(i)
        shift, wanted = top[here, :], chosen[there, :]
        sums = [jnp.zeros((STEP, LANES), F32)] * 3
        for start, size in tiles(0, width, LANES):
            student = logits[here, start : start + size]
            target = teacher[there, start : start + size].astype(F32)
            share = jnp.exp(student - shift)
            sums[0] += share
            sums[1] += share * (student - target)
            sums[2] += jnp.where(wanted == start, student, 0.0)
        total[there, :], gap[there, :], picked[there, :] = sums

    rows_known = {k: lane_sum(ref) for k, ref in ((1, total), (2, gap), (5, picked))}
    inside = rows // QUARTERS
    for q in range(QUARTERS):
        at = (2 * q + group) * inside
        total[at : at + inside, :] = top[q * inside : (q + 1) * inside, :]
    rows_known[0] = total[...].T[0:1, :]
    stats[...] = known[...]
    for k, row in rows_known.items():
        if first:
            lane = lax.broadcasted_iota(jnp.int32, row.shape, 1)
            row = jnp.where((lane & inside) != 0, row, first[0][k : k + 1, :])
        stats[k : k + 1, :] = row


def group_logits(direct, other, weight, teacher, side, known, first, after=()):
    rows, width = teacher.shape
    features = weight.shape[0]
    count = len(direct)

    def kernel(*refs):
        logits_kernel(refs[:count], refs[count : 2 * count], *refs[2 * count :])

    return call(
        kernel,
        "group_logits",
        [
            shape((rows // 2, width), F32),
            shape((STATS, rows), F32),
        ],
        [*direct, *other, weight, teacher, side, known, *first],
        [pltpu.VMEM((rows // 2, features), BF16)]
        + [pltpu.VMEM((rows // 2, LANES), F32)]
        + [pltpu.VMEM((rows, LANES), F32)] * 4,
        after,
        flops=LONG if first else COST,
    )


def join(parts):
    top = functools.reduce(jnp.maximum, [p[0] for p in parts])
    teacher_top = functools.reduce(jnp.maximum, [p[3] for p in parts])
    scales = [jnp.exp(p[0] - top) for p in parts]
    total = sum(s * p[1] for s, p in zip(scales, parts))
    gap = sum(s * p[2] for s, p in zip(scales, parts))
    teacher_total = sum(jnp.exp(p[3] - teacher_top) * p[4] for p in parts)
    picked = sum(p[5] for p in parts)
    return top, total, gap, teacher_top, teacher_total, picked


def over_vocab(stats, size):
    parts, done = [stats], 1
    while done < size:
        if done > 1:
            joined = join([[p[k] for k in range(6)] for p in parts])
            parts = [jnp.stack(list(joined) + [joined[0]] * (STATS - 6))]
        radix = min(4, size // done)
        parts += [xor_swap(parts[0], "vocab", k * done) for k in reversed(range(1, radix))]
        done *= radix
    return parts


def slope_kernel(*refs, parts):
    stats = refs[:parts]
    side, *counts, teacher, logits_0, logits_1 = refs[parts : parts + 6]
    slope_0, slope_1, tokens, lses, shifts, weights = refs[parts + 6 :]

    top, total, gap, teacher_top, teacher_total, picked = join(
        [[s[k : k + 1, :] for k in range(6)] for s in stats]
    )
    lse = top + jnp.log(total)
    diff = lse - (teacher_top + jnp.log(teacher_total))
    kl = gap / total - diff
    tokens[...] = jnp.concatenate([kl, picked - lse])
    mask_total = counts[0][0:1, 0:1] + counts[1][0:1, 0:1]
    lses[...] = spread(lse)
    shifts[...] = spread(diff + kl)
    weights[...] = spread(side[1:2, :] / jnp.maximum(mask_total, 1.0))
    for group, (logits, slope) in enumerate(((logits_0, slope_0), (logits_1, slope_1))):
        rows, width = logits.shape
        steps = row_steps(2 * rows, group)

        @pl.loop(0, rows // STEP, unroll=2)
        def _(i):
            here, there = steps(i)
            lse, shift, weight = lses[there, :], shifts[there, :], weights[there, :]
            for start, size in tiles(0, width, LANES):
                student = logits[here, start : start + size]
                target = teacher[there, start : start + size].astype(F32)
                value = weight * jnp.exp(student - lse) * (student - target - shift)
                slope[here, start : start + size] = value.astype(BF16)


def slopes_of(stats, side, counts, teacher, logits, after=()):
    rows, width = teacher.shape
    return call(
        functools.partial(slope_kernel, parts=len(stats)),
        "slopes",
        [shape((rows // 2, width), BF16)] * 2 + [shape((2, rows), F32)],
        [*stats, side, *counts, teacher, *logits],
        [pltpu.VMEM((rows, LANES), F32)] * 3,
        after,
    )


def weight_blocks(hidden_t, slopes, first, count, start, size):
    return sum(
        jnp.dot(
            left[first : first + count, :],
            right[:, start : start + size],
            preferred_element_type=F32,
        )
        for left, right in zip(hidden_t, slopes)
    )


def weight_away_kernel(*refs, start):
    hidden_t, slopes, out = refs[:2], refs[2:4], refs[4]
    out[...] = weight_blocks(hidden_t, slopes, 0, out.shape[0], start, out.shape[1]).astype(BF16)


def weight_away(hidden_t, slopes, start, size, after=()):
    features = hidden_t[0].shape[0]
    return call(
        functools.partial(weight_away_kernel, start=start),
        "weight_away",
        [shape((features // 2, size), BF16)],
        [*hidden_t, *slopes],
        (),
        after,
    )[0]


def weight_home_kernel(*refs, start):
    hidden_t, slopes, received, outs = refs[:2], refs[2:4], refs[4], refs[5:]
    count, size = outs[0].shape
    for part, out in enumerate(outs):
        value = weight_blocks(hidden_t, slopes, (2 + part) * count, count, start, size)
        value += received[part * count : (part + 1) * count, :].astype(F32)
        out[...] = value.astype(BF16)


def weight_home(hidden_t, slopes, received, start, after=()):
    count, size = received.shape
    return call(
        functools.partial(weight_home_kernel, start=start),
        "weight_home",
        [shape((count // 2, size), BF16)] * 2,
        [*hidden_t, *slopes, received],
        (),
        after,
    )


def hidden_kernel(*refs, vocab_size):
    *slopes, weight, away, home, rows = refs
    blocks = vocab_size
    height = rows.shape[0] // blocks
    for i, block in enumerate(hidden_order(vocab_size)):
        to = slice(i * height, (i + 1) * height)
        if len(slopes) == 1:
            rows[to, :] = slopes[0][pl.ds(pl.multiple_of(block * height, height), height), :]
        else:
            per = vocab_size // QUARTERS // 2
            at = (block // (2 * per) * per + block % per) * height
            for group, slope in enumerate(slopes):

                @pl.when(block // per % 2 == group)
                def _():
                    rows[to, :] = slope[pl.ds(pl.multiple_of(at, height), height), :]

    value = rows[...]
    middle = away.shape[0]
    for start, size in tiles(0, weight.shape[0], 2 * LANES):
        at = slice(start, start + size)
        result = lax.dot_general(
            value, weight[at, :], (((1,), (1,)), ((), ())), preferred_element_type=F32
        )
        away[:, at] = result[:middle].astype(BF16)
        home[:, at] = result[middle:]


def hidden_blocks(slopes, weight, vocab_size, after=()):
    width = weight.shape[1]
    rows = sum(s.shape[0] for s in slopes)
    dims = (rows // 2, weight.shape[0])
    return call(
        functools.partial(hidden_kernel, vocab_size=vocab_size),
        "hidden_grad",
        [shape(dims, BF16), shape(dims, F32)],
        [*slopes, weight],
        [pltpu.VMEM((rows, width), BF16)],
        after,
    )


def add_kernel(kept, received, *outs):
    count = outs[0].shape[0]
    for i, out in enumerate(outs):
        at = slice(i * count, (i + 1) * count)
        out[...] = (kept[at, :].astype(F32) + received[at, :].astype(F32)).astype(BF16)


def add(kept, received, parts, after=()):
    rows, width = kept.shape
    return call(
        add_kernel,
        "add",
        [shape((rows // parts, width), BF16)] * parts,
        [kept, received],
        (),
        after,
    )


def pack_kernel(kept, received, tokens, out):
    rows, width = kept.shape
    out[:, :width] = (kept[...].astype(F32) + received[...].astype(F32)).astype(BF16)
    rest, terms = tokens[...], []
    for _ in range(3):
        terms.append(rest.astype(BF16).astype(F32))
        rest = rest - terms[-1]
    rows_of = [fold(term[k : k + 1]) for term in terms for k in range(2)]
    room = rows * (out.shape[1] - width) // LANES
    values = pad_rows(jnp.concatenate(rows_of), room).astype(BF16)
    for i in range(room // rows):
        at = width + i * LANES
        out[:, at : at + LANES] = values[i * rows : (i + 1) * rows]


def pack(kept, received, tokens, after=()):
    rows, width = kept.shape
    need = 6 * tokens.shape[1] // LANES
    outs = [shape((rows, width + -(-need // rows) * LANES), BF16)]
    return call(pack_kernel, "pack", outs, [kept, received, tokens], (), after)


def finish_kernel(*refs, start, so_far, tokens):
    refs = refs[so_far:]
    if tokens:
        strip, out, token, *values, done = refs
        count, width = strip.shape[0], out.shape[1]
        folded = jnp.concatenate(
            [strip[:, at : at + LANES] for at in range(width, strip.shape[1], LANES)]
        ).astype(F32)
        for k, value in enumerate(values):
            size = value.shape[1]
            value[...] = sum(unfold(folded, k + 2 * term, size) for term in range(3))
        source, place = strip.at[:, :width], out.at[start : start + count, :]
    elif len(refs) == 4:
        strip, out, token, done = refs
        count = strip.shape[0]
        source, place = strip, out.at[start : start + count, :]
    else:
        kept, received, out, token, source, done = refs
        source[...] = (kept[...].astype(F32) + received[...].astype(F32)).astype(BF16)
        place = out.at[:, start : start + source.shape[1]]
    token[...] = jnp.zeros(token.shape, F32)
    run_copies(copy_pairs(source, place), done)


def finish(parts, dims, start, so_far, after, tokens=0):
    outs = [pltpu.HBM(dims, BF16), shape((8, LANES), F32)]
    outs += [shape((1, tokens), F32)] * 2 if tokens else []
    scratch = [pltpu.VMEM(parts[0].shape, BF16)] if len(parts) == 2 else []
    return call(
        functools.partial(
            finish_kernel, start=start, so_far=len(so_far), tokens=bool(tokens)
        ),
        "finish",
        outs,
        list(parts),
        scratch + [pltpu.SemaphoreType.DMA((8,))],
        after,
        so_far,
        bool(so_far),
    )


def local(hidden, out_weight, teacher_logits, token_ids, loss_mask):
    rows, features = hidden.shape
    width = out_weight.shape[1]
    vocab_size = lax.axis_size("vocab")
    group_axes, group_size = ("role", "dp"), lax.axis_size("role") * lax.axis_size("dp")
    assert lax.axis_size("role") == 2 and lax.axis_size("dp") == 4
    assert vocab_size & (vocab_size - 1) == 0 and vocab_size >= QUARTERS

    ids, mask = token_ids.reshape(1, rows), loss_mask.reshape(1, rows)
    pieces = list(pick_rows(hidden, [(0, 0)]))
    pieces += pick_rows(hidden, [(0, 1), (1, 0), (1, 1)], (ids, mask), after=pieces)
    direct = [xor_swap(piece, "role", 1) for piece in pieces]
    known = teacher_stats(teacher_logits, after=pieces[1:2])
    direct[0] = pass_on(direct[0], [known])
    direct[1], side = unpack_rows(direct[1], rows)
    count = count_rows(side, mask)
    count = sum_rows(count, xor_swap(count, "dp", 1))
    direct[2] = pass_on(direct[2], [count])
    counts = [count, xor_swap(count, "dp", 2)]
    other = [xor_swap(piece, "vocab", 1) for piece in direct]

    logits, hidden_t, stats = [], [], []
    for group in range(2):
        pair = slice(2 * group, 2 * group + 2)
        done = group_logits(
            direct[pair],
            other[pair],
            out_weight,
            teacher_logits,
            side,
            known,
            stats[-1:],
            after=counts[1:] if group else direct[3:],
        )
        for values, value in zip((logits, stats), done):
            values.append(value)
        hidden_t.append(turn_rows(direct[pair], other[pair], after=stats[group:]))
    *slopes, tokens = slopes_of(
        over_vocab(stats[1], vocab_size), side, counts, teacher_logits, logits, hidden_t[1:]
    )

    parts = [[s] for s in slopes] if vocab_size == QUARTERS else [slopes]
    home, hidden_in = [], []

    def hidden_step(last):
        if len(home) < len(parts):
            some = parts[len(home)]
            last, kept = hidden_blocks(some, out_weight, vocab_size, after=[last])
            home.append(kept)
            hidden_in.append(xor_swap(last, "vocab", 1))
        return last

    chunks = column_chunks(width, (7, 6, 6))
    arrived, near = [], []

    def away_step(last):
        last = weight_away(hidden_t, slopes, *chunks[len(arrived)], after=[last])
        arrived.append(exchange(last, group_axes, group_size, lambda i: i ^ 1))
        return last

    def near_step(last):
        k = len(near)
        leaving, last = weight_home(hidden_t, slopes, arrived[k], chunks[k][0], after=[last])
        near.append((last, exchange(leaving, group_axes, group_size, near_of)))
        return last

    far, grad_weight, grad_hidden, returned, outs = [], [], [], [], []

    def far_step(last):
        kept, received = near[len(far)]
        leaving, last = add(kept, received, 2, after=[last])
        far.append((last, exchange(leaving, group_axes, group_size, far_of)))
        return last

    def weight_step(last):
        k = len(grad_weight)
        dims = (features // group_size, width)
        result, last = finish(far[k], dims, chunks[k][0], grad_weight[-1:], [last])
        grad_weight.append(result)
        return last

    halved = []

    def halve_step(last):
        if len(halved) < len(home):
            k = len(halved)
            leaving, last = add(home[k], hidden_in[k], 2, after=[last])
            halved.append((last, xor_swap(leaving, "vocab", 2)))
        return last

    def return_step(last):
        if len(returned) < len(home):
            kept, received = halved[len(returned)]
            bit = 4
            while bit < vocab_size:
                leaving, last = add(kept, received, 2, after=[last])
                kept, received = last, xor_swap(leaving, "vocab", bit)
                bit *= 2
            if returned:
                (last,) = add(kept, received, 1, after=[last])
            else:
                (last,) = pack(kept, received, tokens, after=[last])
            returned.append(xor_swap(last, "role", 1))
        return last

    def strip_step(last):
        if len(grad_hidden) < len(home):
            k = len(grad_hidden)
            strip = returned[k]
            dims = (rows // vocab_size, features)
            start = k * strip.shape[0] if k == 0 else dims[0] // 2
            result, last, *values = finish(
                [strip], dims, start, grad_hidden[-1:], [last], 0 if k else rows
            )
            grad_hidden.append(result)
            outs.extend(values)
        return last

    last = slopes[1]
    for step in (
        away_step,
        away_step,
        away_step,
        near_step,
        hidden_step,
        near_step,
        near_step,
        hidden_step,
        far_step,
        halve_step,
        far_step,
        halve_step,
        return_step,
        weight_step,
        far_step,
        weight_step,
        return_step,
        strip_step,
        weight_step,
        strip_step,
    ):
        last = step(last)

    return outs[0].reshape(rows), outs[1].reshape(rows), grad_hidden[-1], grad_weight[-1]


def solution(mesh):
    return jax.shard_map(
        local,
        mesh=mesh,
        in_specs=(
            P(("role", "dp"), None),
            P(None, "vocab"),
            P(("role", "dp"), "vocab"),
            P(("role", "dp")),
            P(("role", "dp")),
        ),
        out_specs=(
            P(("role", "dp")),
            P(("role", "dp")),
            P(("role", "dp", "vocab"), None),
            P(("role", "dp"), "vocab"),
        ),
        check_vma=False,
    )
```

time: 247 us -> 107 us (0.43)
  blocking collectives: 82.6 us -> 0 us
  waiting for transfers between devices: 88.3 us -> 36.4 us
  matrix products: 35.4 us -> 0 us
  Pallas kernels: 0 us -> 32.8 us
  starting transfers between devices: 3.26 us -> 36 us
  between operations: 14.7 us -> 1.07 us
  local copies, waits for them, and re-layouts: 12.5 us -> 0.02 us
  other arithmetic: 9.74 us -> 0.01 us
    unnamed x3 -> x0, waiting for transfers between devices: 76.3 us -> none
    psum x2 -> x0, blocking collectives: 70.6 us -> none  [the longest x1 62.1 us: local(): lax.psum(jnp.sum(mask_values), ('role', 'dp'))]
    ppermute x1 -> x28, waiting for transfers between devices: 0.01 us -> 36.4 us  [exchange(): return lax.ppermute(array, axes, [(i, partner(i)) for i in range(size)])]
    dot_general x3 -> x0, matrix products: 35.4 us -> none  [the longest x1 12.7 us: local(): lax.dot_general(block, out_weight, (((1,), (1,)), ((), ())), preferred_el...]
    ppermute x1 -> x28, starting transfers between devices: 3 us -> 36 us  [exchange(): return lax.ppermute(array, axes, [(i, partner(i)) for i in range(size)])]
    pallas_call x0 -> x33, Pallas kernels: none -> 32.8 us  [call(): pl.pallas_call(lambda *refs: kernel(*refs[skip:]), in_specs=[pl.BlockSpec...]
    unnamed x7 -> x10, local copies, waits for them, and re-layouts: 12.5 us -> 0.02 us
    reduce_scatter x1 -> x0, waiting for transfers between devices: 12 us -> none  [local(): lax.psum_scatter(lax.dot_general(block, out_weight, (((1,), (1,)), ((), (...]
  transfers between devices with their start and end apart: 3 -> 28, of which waited for: 2 -> 13; matrix products, arithmetic and copies ran while one was open for 15% -> 0% of each run, Pallas kernels for 0% -> 22%
where the time goes in v1:
time: 107 us; the launch traced here: 106 us
  waiting for transfers between devices  36.4 us (34%)
  starting transfers between devices  36 us (34%)
  Pallas kernels  32.8 us (31%)
  between operations  1.07 us (1%)
    ppermute x28, waiting for transfers between devices, exchange(): return lax.ppermute(array, axes, [(i, partner(i)) for i in range(size)])  36.4 us
    ppermute x28, starting transfers between devices, exchange(): return lax.ppermute(array, axes, [(i, partner(i)) for i in range(size)])  36 us
    pallas_call x33, Pallas kernels, call(): pl.pallas_call(lambda *refs: kernel(*refs[skip:]), in_specs=[pl.BlockSpec...  32.8 us
  transfers between devices with their start and end apart: 28, of which 13 were waited for; matrix products, arithmetic and copies ran while one was open for 0% of the time, Pallas kernels for 22%

profile of v1, /device:TPU:0, one launch (start us, length us, event | category | flops | bytes accessed | tf_op | source)
XLA Modules:
  0.0 106.3 jit_solution(5377080262517440650)
XLA Ops:
  1.6 3.0 %collective-permute-start.7 = (bf16[64,1792]{1,0:T(8,128)(2,1)S(1)}, bf16[64,1792]{1,0:T(8,128)(2,1)S(1)}, u32[]{:S(2)}, u32[]{:S(2)}) collective-permute-start(bf16[64,1792]{1,0:T(8,128)(2,1)S(1)} %pick_rows.2.refs_0_), channel_id=1, source_target_pairs={{0,16},{16,0},{1,17},{17,1},{2,18},{18,2},{3,19},{19,3},{4,20},{20... | collective-permute-start | bytes 688136 | tf_op jit(solution)/shard_map/ppermute | solution.py:23
  6.1 2.0 %collective-permute-start.4 = (bf16[64,1792]{1,0:T(8,128)(2,1)S(1)}, bf16[64,1792]{1,0:T(8,128)(2,1)S(1)}, u32[]{:S(2)}, u32[]{:S(2)}) collective-permute-start(bf16[64,1792]{1,0:T(8,128)(2,1)S(1)} %get-tuple-element.50), channel_id=1, source_target_pairs={{0,16},{16,0},{1,17},{17,1},{2,18},{18,2},{3,19},{19,3},{4,20},{20... | collective-permute-start | bytes 688136 | tf_op jit(solution)/shard_map/ppermute | solution.py:23
  8.3 1.9 %teacher_stats.1.refs_0_.refs_8_ = f32[8,512]{1,0:T(8,128)S(1)} custom-call(bf16[64,1920]{1,0:T(8,128)(2,1)S(1)} %get-tuple-element.47.refs_0_, bf16[512,2432]{1,0:T(8,128)(2,1)S(1)} %copy-done), custom_call_target="tpu_custom_call" | custom-call | flops 20000000000 | bytes 1024 | tf_op jit(solution)/shard_map/teacher_stats/pallas_call | solution.py:38
  11.0 2.1 %collective-permute-start.8 = (bf16[64,1792]{1,0:T(8,128)(2,1)S(1)}, bf16[64,1792]{1,0:T(8,128)(2,1)S(1)}, u32[]{:S(2)}, u32[]{:S(2)}) collective-permute-start(bf16[64,1792]{1,0:T(8,128)(2,1)S(1)} %pass_on.3.refs_1_), channel_id=1, source_target_pairs={{0,1},{1,0},{2,3},{3,2},{4,5},{5,4},{6,7},{7,6},{8,9},{9,8},{10,11... | collective-permute-start | bytes 688136 | tf_op jit(solution)/shard_map/ppermute | solution.py:23
  13.2 3.1 %collective-permute-done.refs_0_ = bf16[64,1920]{1,0:T(8,128)(2,1)S(1)} collective-permute-done((bf16[64,1920]{1,0:T(8,128)(2,1)S(1)}, bf16[64,1920]{1,0:T(8,128)(2,1)S(1)}, u32[]{:S(2)}, u32[]{:S(2)}) %collective-permute-start) | collective-permute-done | bytes 245792 | tf_op jit(solution)/shard_map/ppermute | solution.py:23
  16.3 2.2 %collective-permute-start.9 = (bf16[64,1792]{1,0:T(8,128)(2,1)S(1)}, bf16[64,1792]{1,0:T(8,128)(2,1)S(1)}, u32[]{:S(2)}, u32[]{:S(2)}) collective-permute-start(bf16[64,1792]{1,0:T(8,128)(2,1)S(1)} %get-tuple-element.51.refs_2_), channel_id=1, source_target_pairs={{0,1},{1,0},{2,3},{3,2},{4,5},{5,4},{6,7},{7,6},{8,9},{9,8},{10,11... | collective-permute-start | bytes 688136 | tf_op jit(solution)/shard_map/ppermute | solution.py:23
  18.7 2.5 %collective-permute-done.4.refs_0_.refs_2_ = bf16[64,1792]{1,0:T(8,128)(2,1)S(1)} collective-permute-done((bf16[64,1792]{1,0:T(8,128)(2,1)S(1)}, bf16[64,1792]{1,0:T(8,128)(2,1)S(1)}, u32[]{:S(2)}, u32[]{:S(2)}) %collective-permute-start.4) | collective-permute-done | bytes 229408 | tf_op jit(solution)/shard_map/ppermute | solution.py:23
  21.2 2.1 %collective-permute-start.6 = (bf16[64,1792]{1,0:T(8,128)(2,1)S(1)}, bf16[64,1792]{1,0:T(8,128)(2,1)S(1)}, u32[]{:S(2)}, u32[]{:S(2)}) collective-permute-start(bf16[64,1792]{1,0:T(8,128)(2,1)S(1)} %collective-permute-done.4.refs_0_.refs_2_), channel_id=1, source_target_pairs={{0,1},{1,0},{2,3},{3,2},{4,5},{5,4},{6,7},{7,6},{8,9},{9,8},{10,11... | collective-permute-start | bytes 688136 | tf_op jit(solution)/shard_map/ppermute | solution.py:23
  23.4 1.9 %collective-permute-done.3.refs_1_ = bf16[64,1792]{1,0:T(8,128)(2,1)S(1)} collective-permute-done((bf16[64,1792]{1,0:T(8,128)(2,1)S(1)}, bf16[64,1792]{1,0:T(8,128)(2,1)S(1)}, u32[]{:S(2)}, u32[]{:S(2)}) %collective-permute-start.3) | collective-permute-done | bytes 229408 | tf_op jit(solution)/shard_map/ppermute | solution.py:23
  25.3 1.8 %collective-permute-start.5 = (bf16[64,1792]{1,0:T(8,128)(2,1)S(1)}, bf16[64,1792]{1,0:T(8,128)(2,1)S(1)}, u32[]{:S(2)}, u32[]{:S(2)}) collective-permute-start(bf16[64,1792]{1,0:T(8,128)(2,1)S(1)} %pass_on.2.refs_1_), channel_id=1, source_target_pairs={{0,1},{1,0},{2,3},{3,2},{4,5},{5,4},{6,7},{7,6},{8,9},{9,8},{10,11... | collective-permute-start | bytes 688136 | tf_op jit(solution)/shard_map/ppermute | solution.py:23
  27.1 1.5 %collective-permute-start.2 = (f32[8,128]{1,0:T(8,128)S(1)}, f32[8,128]{1,0:T(8,128)S(1)}, u32[]{:S(2)}, u32[]{:S(2)}) collective-permute-start(f32[8,128]{1,0:T(8,128)S(1)} %sum_rows.1.refs_0_.refs_6_), channel_id=1, source_target_pairs={{0,8},{4,12},{8,0},{12,4},{1,9},{5,13},{9,1},{13,5},{2,10},{6,14},... | collective-permute-start | bytes 12296 | tf_op jit(solution)/shard_map/ppermute | solution.py:23
  28.7 4.1 %group_logits.2 = (f32[256,2432]{1,0:T(8,128)S(1)}, f32[8,512]{1,0:T(8,128)S(1)}) custom-call(bf16[64,1792]{1,0:T(8,128)(2,1)S(1)} %collective-permute-done.4.refs_0_.refs_2_, bf16[64,1792]{1,0:T(8,128)(2,1)S(1)} %pass_on.3.refs_1_, bf16[64,1792]{1,0:T(8,128)(2,1)S(1)} %get-tuple-element.51.refs_2_, bf16[64,1792]{1,0:T(8,128)(2,1)S(1)} %collective-permute-done.8.refs_3_, ...), custom_call_target="tpu_custom_call" | custom-call | flops 2000000000 | bytes 1024 | tf_op jit(solution)/shard_map/group_logits/pallas_call | solution.py:38
  32.8 4.1 %group_logits.3 = (f32[256,2432]{1,0:T(8,128)S(1)}, f32[8,512]{1,0:T(8,128)S(1)}) custom-call(f32[8,128]{1,0:T(8,128)S(1)} %collective-permute-done.2.refs_0_.refs_7_, bf16[64,1792]{1,0:T(8,128)(2,1)S(1)} %pass_on.2.refs_1_, bf16[64,1792]{1,0:T(8,128)(2,1)S(1)} %collective-permute-done.4.refs_0_.refs_2_, ...), custom_call_target="tpu_custom_call" | custom-call | flops 20000000000 | bytes 1024 | tf_op jit(solution)/shard_map/group_logits/pallas_call | solution.py:38
  36.8 3.7 %collective-permute-start.10 = (f32[8,512]{1,0:T(8,128)S(1)}, f32[8,512]{1,0:T(8,128)S(1)}, u32[]{:S(2)}, u32[]{:S(2)}) collective-permute-start(f32[8,512]{1,0:T(8,128)S(1)} %get-tuple-element.53.refs_0_.refs_1_), channel_id=1, source_target_pairs={{0,3},{1,2},{2,1},{3,0},{4,7},{5,6},{6,5},{7,4},{8,11},{9,10},{10,... | collective-permute-start | bytes 49160 | tf_op jit(solution)/shard_map/ppermute | solution.py:23
  42.4 2.8 %collective-permute-done.11.refs_3_ = f32[8,512]{1,0:T(8,128)S(1)} collective-permute-done((f32[8,512]{1,0:T(8,128)S(1)}, f32[8,512]{1,0:T(8,128)S(1)}, u32[]{:S(2)}, u32[]{:S(2)}) %collective-permute-start.11) | collective-permute-done | bytes 16416 | tf_op jit(solution)/shard_map/ppermute | solution.py:23
  45.2 2.3 %slopes.1 = (bf16[256,2432]{1,0:T(8,128)(2,1)S(1)}, bf16[256,2432]{1,0:T(8,128)(2,1)S(1)}, f32[2,512]{1,0:T(2,128)S(1)}) custom-call(bf16[1792,256]{1,0:T(8,128)(2,1)S(1)} %turn_rows.2.refs_0_.refs_2_, f32[8,512]{1,0:T(8,128)S(1)} %get-tuple-element.53.refs_0_.refs_1_, f32[8,512]{1,0:T(8,128)S(1)} %collective-permute-done.10.refs_2_, ...), custom_call_target="tpu_custom_call" | custom-call | flops 1024 | bytes 1024 | tf_op jit(solution)/shard_map/slopes/pallas_call | solution.py:38
  53.2 1.6 %collective-permute-start.16 = (bf16[448,896]{1,0:T(8,128)(2,1)S(1)}, bf16[448,896]{1,0:T(8,128)(2,1)S(1)}, u32[]{:S(2)}, u32[]{:S(2)}) collective-permute-start(bf16[448,896]{1,0:T(8,128)(2,1)S(1)} %get-tuple-element.63), channel_id=1, source_target_pairs={{0,16},{4,12},{8,24},{12,4},{16,0},{20,28},{24,8},{28,20},{1,17},{... | collective-permute-start | bytes 2408456 | tf_op jit(solution)/shard_map/ppermute | solution.py:23
  54.8 2.6 %hidden_grad.2 = (bf16[128,1792]{1,0:T(8,128)(2,1)S(1)}, f32[128,1792]{1,0:T(8,128)S(1)}) custom-call(bf16[448,896]{1,0:T(8,128)(2,1)S(1)} %get-tuple-element.58.refs_0_.refs_1_, bf16[256,2432]{1,0:T(8,128)(2,1)S(1)} %get-tuple-element.57.refs_3_.refs_1_, bf16[1792,2432]{1,0:T(8,128)(2,1)S(1)} %bitcast.5), custom_call_target="tpu_custom_call" | custom-call | flops 1024 | bytes 1024 | tf_op jit(solution)/shard_map/hidden_grad/pallas_call | solution.py:38
  59.8 1.6 %collective-permute-start.22 = (bf16[448,768]{1,0:T(8,128)(2,1)S(1)}, bf16[448,768]{1,0:T(8,128)(2,1)S(1)}, u32[]{:S(2)}, u32[]{:S(2)}) collective-permute-start(bf16[448,768]{1,0:T(8,128)(2,1)S(1)} %get-tuple-element.75), channel_id=1, source_target_pairs={{0,16},{4,12},{8,24},{12,4},{16,0},{20,28},{24,8},{28,20},{1,17},{... | collective-permute-start | bytes 2064392 | tf_op jit(solution)/shard_map/ppermute | solution.py:23
  61.4 2.6 %hidden_grad.3 = (bf16[128,1792]{1,0:T(8,128)(2,1)S(1)}, f32[128,1792]{1,0:T(8,128)S(1)}) custom-call(bf16[448,768]{1,0:T(8,128)(2,1)S(1)} %get-tuple-element.61.refs_0_.refs_1_, bf16[256,2432]{1,0:T(8,128)(2,1)S(1)} %get-tuple-element.56.refs_0_.refs_4_.refs_1_, bf16[1792,2432]{1,0:T(8,128)(2,1)S(1)} %bitcast.5), custom_call_target="tpu_custom_call" | custom-call | flops 1024 | bytes 1024 | tf_op jit(solution)/shard_map/hidden_grad/pallas_call | solution.py:38
  63.9 2.1 %collective-permute-start.19 = (bf16[128,1792]{1,0:T(8,128)(2,1)S(1)}, bf16[128,1792]{1,0:T(8,128)(2,1)S(1)}, u32[]{:S(2)}, u32[]{:S(2)}) collective-permute-start(bf16[128,1792]{1,0:T(8,128)(2,1)S(1)} %get-tuple-element.62.refs_0_), channel_id=1, source_target_pairs={{0,1},{1,0},{2,3},{3,2},{4,5},{5,4},{6,7},{7,6},{8,9},{9,8},{10,11... | collective-permute-start | bytes 1376264 | tf_op jit(solution)/shard_map/ppermute | solution.py:23
  66.2 1.6 %collective-permute-start.21 = (bf16[224,896]{1,0:T(8,128)(2,1)S(1)}, bf16[224,896]{1,0:T(8,128)(2,1)S(1)}, u32[]{:S(2)}, u32[]{:S(2)}) collective-permute-start(bf16[224,896]{1,0:T(8,128)(2,1)S(1)} %get-tuple-element.73), channel_id=1, source_target_pairs={{0,8},{4,20},{8,0},{12,28},{16,24},{20,4},{24,16},{28,12},{1,9},{5... | collective-permute-start | bytes 1204232 | tf_op jit(solution)/shard_map/ppermute | solution.py:23
  67.8 4.5 %collective-permute-done.17.refs_2_ = bf16[128,1792]{1,0:T(8,128)(2,1)S(1)} collective-permute-done((bf16[128,1792]{1,0:T(8,128)(2,1)S(1)}, bf16[128,1792]{1,0:T(8,128)(2,1)S(1)}, u32[]{:S(2)}, u32[]{:S(2)}) %collective-permute-start.17) | collective-permute-done | bytes 458784 | tf_op jit(solution)/shard_map/ppermute | solution.py:23
  72.4 2.1 %collective-permute-start.20 = (bf16[64,1792]{1,0:T(8,128)(2,1)S(1)}, bf16[64,1792]{1,0:T(8,128)(2,1)S(1)}, u32[]{:S(2)}, u32[]{:S(2)}) collective-permute-start(bf16[64,1792]{1,0:T(8,128)(2,1)S(1)} %get-tuple-element.71), channel_id=1, source_target_pairs={{0,2},{1,3},{2,0},{3,1},{4,6},{5,7},{6,4},{7,5},{8,10},{9,11},{10,... | collective-permute-start | bytes 688136 | tf_op jit(solution)/shard_map/ppermute | solution.py:23
  74.5 2.6 %collective-permute-done.18.refs_2_ = bf16[448,768]{1,0:T(8,128)(2,1)S(1)} collective-permute-done((bf16[448,768]{1,0:T(8,128)(2,1)S(1)}, bf16[448,768]{1,0:T(8,128)(2,1)S(1)}, u32[]{:S(2)}, u32[]{:S(2)}) %collective-permute-start.18) | collective-permute-done | bytes 688160 | tf_op jit(solution)/shard_map/ppermute | solution.py:23
  77.3 1.6 %collective-permute-start.23 = (bf16[224,768]{1,0:T(8,128)(2,1)S(1)}, bf16[224,768]{1,0:T(8,128)(2,1)S(1)}, u32[]{:S(2)}, u32[]{:S(2)}) collective-permute-start(bf16[224,768]{1,0:T(8,128)(2,1)S(1)} %get-tuple-element.78), channel_id=1, source_target_pairs={{0,8},{4,20},{8,0},{12,28},{16,24},{20,4},{24,16},{28,12},{1,9},{5... | collective-permute-start | bytes 1032200 | tf_op jit(solution)/shard_map/ppermute | solution.py:23
  78.9 6.7 %collective-permute-done.19.refs_2_ = bf16[128,1792]{1,0:T(8,128)(2,1)S(1)} collective-permute-done((bf16[128,1792]{1,0:T(8,128)(2,1)S(1)}, bf16[128,1792]{1,0:T(8,128)(2,1)S(1)}, u32[]{:S(2)}, u32[]{:S(2)}) %collective-permute-start.19) | collective-permute-done | bytes 458784 | tf_op jit(solution)/shard_map/ppermute | solution.py:23
  88.4 1.6 %collective-permute-start.26 = (bf16[224,768]{1,0:T(8,128)(2,1)S(1)}, bf16[224,768]{1,0:T(8,128)(2,1)S(1)}, u32[]{:S(2)}, u32[]{:S(2)}) collective-permute-start(bf16[224,768]{1,0:T(8,128)(2,1)S(1)} %get-tuple-element.85), channel_id=1, source_target_pairs={{0,8},{4,20},{8,0},{12,28},{16,24},{20,4},{24,16},{28,12},{1,9},{5... | collective-permute-start | bytes 1032200 | tf_op jit(solution)/shard_map/ppermute | solution.py:23
  89.9 1.5 %collective-permute-start.25 = (bf16[64,1920]{1,0:T(8,128)(2,1)S(1)}, bf16[64,1920]{1,0:T(8,128)(2,1)S(1)}, u32[]{:S(2)}, u32[]{:S(2)}) collective-permute-start(bf16[64,1920]{1,0:T(8,128)(2,1)S(1)} %pack.1.refs_0_), channel_id=1, source_target_pairs={{0,16},{16,0},{1,17},{17,1},{2,18},{18,2},{3,19},{19,3},{4,20},{20... | collective-permute-start | bytes 737288 | tf_op jit(solution)/shard_map/ppermute | solution.py:23
  92.3 4.9 %collective-permute-done.24.refs_2_ = bf16[64,1792]{1,0:T(8,128)(2,1)S(1)} collective-permute-done((bf16[64,1792]{1,0:T(8,128)(2,1)S(1)}, bf16[64,1792]{1,0:T(8,128)(2,1)S(1)}, u32[]{:S(2)}, u32[]{:S(2)}) %collective-permute-start.24) | collective-permute-done | bytes 229408 | tf_op jit(solution)/shard_map/ppermute | solution.py:23
  97.3 1.5 %collective-permute-start.27 = (bf16[64,1792]{1,0:T(8,128)(2,1)S(1)}, bf16[64,1792]{1,0:T(8,128)(2,1)S(1)}, u32[]{:S(2)}, u32[]{:S(2)}) collective-permute-start(bf16[64,1792]{1,0:T(8,128)(2,1)S(1)} %add.11.refs_0_), channel_id=1, source_target_pairs={{0,16},{16,0},{1,17},{17,1},{2,18},{18,2},{3,19},{19,3},{4,20},{20... | collective-permute-start | bytes 688136 | tf_op jit(solution)/shard_map/ppermute | solution.py:23
  101.0 3.8 %collective-permute-done.27.refs_2_ = bf16[64,1792]{1,0:T(8,128)(2,1)S(1)} collective-permute-done((bf16[64,1792]{1,0:T(8,128)(2,1)S(1)}, bf16[64,1792]{1,0:T(8,128)(2,1)S(1)}, u32[]{:S(2)}, u32[]{:S(2)}) %collective-permute-start.27) | collective-permute-done | bytes 229408 | tf_op jit(solution)/shard_map/ppermute | solution.py:23
  (68 shorter events, 21.3 us)
Async XLA Ops:
  1.6 9.4 %collective-permute-start.7 = (bf16[64,1792]{1,0:T(8,128)(2,1)S(1)}, bf16[64,1792]{1,0:T(8,128)(2,1)S(1)}, u32[]{:S(2)}, u32[]{:S(2)}) collective-permute-start(bf16[64,1792]{1,0:T(8,128)(2,1)S(1)} %pick_rows.2.refs_0_), channel_id=1, source_target_pairs={{0,16},{16,0},{1,17},{17,1},{2,18},{18,2},{3,19},{19,3},{4,20},{20... | collective-permute-start | bytes 688136 | tf_op jit(solution)/shard_map/ppermute | solution.py:23
  6.0 10.3 %collective-permute-start = (bf16[64,1920]{1,0:T(8,128)(2,1)S(1)}, bf16[64,1920]{1,0:T(8,128)(2,1)S(1)}, u32[]{:S(2)}, u32[]{:S(2)}) collective-permute-start(bf16[64,1920]{1,0:T(8,128)(2,1)S(1)} %get-tuple-element.47.refs_0_), channel_id=1, source_target_pairs={{0,16},{16,0},{1,17},{17,1},{2,18},{18,2},{3,19},{19,3},{4,20},{20... | collective-permute-start | bytes 737288 | tf_op jit(solution)/shard_map/ppermute | solution.py:23
  6.1 15.1 %collective-permute-start.4 = (bf16[64,1792]{1,0:T(8,128)(2,1)S(1)}, bf16[64,1792]{1,0:T(8,128)(2,1)S(1)}, u32[]{:S(2)}, u32[]{:S(2)}) collective-permute-start(bf16[64,1792]{1,0:T(8,128)(2,1)S(1)} %get-tuple-element.50), channel_id=1, source_target_pairs={{0,16},{16,0},{1,17},{17,1},{2,18},{18,2},{3,19},{19,3},{4,20},{20... | collective-permute-start | bytes 688136 | tf_op jit(solution)/shard_map/ppermute | solution.py:23
  8.1 20.5 %slice-start = ((s8[8716288]{0:T(1024)(128)(4,1)}), s8[4194304]{0:T(1024)(128)(4,1)S(1)}, s32[]{:S(2)}) async-start(s8[8716288]{0:T(1024)(128)(4,1)} %bitcast.4), calls=%async_computation | async-start | bytes 8388608
  8.1 10.4 %copy-start.1 = (s32[512]{0:T(512)S(1)}, s32[512]{0:T(512)}, u32[]{:S(2)}) copy-start(s32[512]{0:T(512)} %param.9) | copy-start | bytes 6148
  8.1 20.5 %slice-start.1 = ((s8[8716288]{0:T(1024)(128)(4,1)}), s8[4194304]{0:T(1024)(128)(4,1)S(1)}, s32[]{:S(2)}) async-start(s8[8716288]{0:T(1024)(128)(4,1)} %bitcast.4), calls=%async_computation.1 | async-start | bytes 8388608
  8.1 20.5 %slice-start.2 = ((s8[8716288]{0:T(1024)(128)(4,1)}), s8[327680]{0:T(1024)(128)(4,1)S(1)}, s32[]{:S(2)}) async-start(s8[8716288]{0:T(1024)(128)(4,1)} %bitcast.4), calls=%async_computation.2 | async-start | bytes 655360
  8.1 17.2 %collective-permute-start.3 = (bf16[64,1792]{1,0:T(8,128)(2,1)S(1)}, bf16[64,1792]{1,0:T(8,128)(2,1)S(1)}, u32[]{:S(2)}, u32[]{:S(2)}) collective-permute-start(bf16[64,1792]{1,0:T(8,128)(2,1)S(1)} %get-tuple-element.49), channel_id=1, source_target_pairs={{0,16},{16,0},{1,17},{17,1},{2,18},{18,2},{3,19},{19,3},{4,20},{20... | collective-permute-start | bytes 688136 | tf_op jit(solution)/shard_map/ppermute | solution.py:23
  11.0 17.6 %collective-permute-start.8 = (bf16[64,1792]{1,0:T(8,128)(2,1)S(1)}, bf16[64,1792]{1,0:T(8,128)(2,1)S(1)}, u32[]{:S(2)}, u32[]{:S(2)}) collective-permute-start(bf16[64,1792]{1,0:T(8,128)(2,1)S(1)} %pass_on.3.refs_1_), channel_id=1, source_target_pairs={{0,1},{1,0},{2,3},{3,2},{4,5},{5,4},{6,7},{7,6},{8,9},{9,8},{10,11... | collective-permute-start | bytes 688136 | tf_op jit(solution)/shard_map/ppermute | solution.py:23
  16.3 12.3 %collective-permute-start.9 = (bf16[64,1792]{1,0:T(8,128)(2,1)S(1)}, bf16[64,1792]{1,0:T(8,128)(2,1)S(1)}, u32[]{:S(2)}, u32[]{:S(2)}) collective-permute-start(bf16[64,1792]{1,0:T(8,128)(2,1)S(1)} %get-tuple-element.51.refs_2_), channel_id=1, source_target_pairs={{0,1},{1,0},{2,3},{3,2},{4,5},{5,4},{6,7},{7,6},{8,9},{9,8},{10,11... | collective-permute-start | bytes 688136 | tf_op jit(solution)/shard_map/ppermute | solution.py:23
  18.7 4.7 %collective-permute-start.1 = (f32[8,128]{1,0:T(8,128)S(1)}, f32[8,128]{1,0:T(8,128)S(1)}, u32[]{:S(2)}, u32[]{:S(2)}) collective-permute-start(f32[8,128]{1,0:T(8,128)S(1)} %count_rows.1.refs_0_), channel_id=1, source_target_pairs={{0,4},{4,0},{8,12},{12,8},{1,5},{5,1},{9,13},{13,9},{2,6},{6,2},{1... | collective-permute-start | bytes 12296 | tf_op jit(solution)/shard_map/ppermute | solution.py:23
  21.2 11.5 %collective-permute-start.6 = (bf16[64,1792]{1,0:T(8,128)(2,1)S(1)}, bf16[64,1792]{1,0:T(8,128)(2,1)S(1)}, u32[]{:S(2)}, u32[]{:S(2)}) collective-permute-start(bf16[64,1792]{1,0:T(8,128)(2,1)S(1)} %collective-permute-done.4.refs_0_.refs_2_), channel_id=1, source_target_pairs={{0,1},{1,0},{2,3},{3,2},{4,5},{5,4},{6,7},{7,6},{8,9},{9,8},{10,11... | collective-permute-start | bytes 688136 | tf_op jit(solution)/shard_map/ppermute | solution.py:23
  25.3 7.5 %collective-permute-start.5 = (bf16[64,1792]{1,0:T(8,128)(2,1)S(1)}, bf16[64,1792]{1,0:T(8,128)(2,1)S(1)}, u32[]{:S(2)}, u32[]{:S(2)}) collective-permute-start(bf16[64,1792]{1,0:T(8,128)(2,1)S(1)} %pass_on.2.refs_1_), channel_id=1, source_target_pairs={{0,1},{1,0},{2,3},{3,2},{4,5},{5,4},{6,7},{7,6},{8,9},{9,8},{10,11... | collective-permute-start | bytes 688136 | tf_op jit(solution)/shard_map/ppermute | solution.py:23
  27.1 5.6 %collective-permute-start.2 = (f32[8,128]{1,0:T(8,128)S(1)}, f32[8,128]{1,0:T(8,128)S(1)}, u32[]{:S(2)}, u32[]{:S(2)}) collective-permute-start(f32[8,128]{1,0:T(8,128)S(1)} %sum_rows.1.refs_0_.refs_6_), channel_id=1, source_target_pairs={{0,8},{4,12},{8,0},{12,4},{1,9},{5,13},{9,1},{13,5},{2,10},{6,14},... | collective-permute-start | bytes 12296 | tf_op jit(solution)/shard_map/ppermute | solution.py:23
  36.8 5.6 %collective-permute-start.10 = (f32[8,512]{1,0:T(8,128)S(1)}, f32[8,512]{1,0:T(8,128)S(1)}, u32[]{:S(2)}, u32[]{:S(2)}) collective-permute-start(f32[8,512]{1,0:T(8,128)S(1)} %get-tuple-element.53.refs_0_.refs_1_), channel_id=1, source_target_pairs={{0,3},{1,2},{2,1},{3,0},{4,7},{5,6},{6,5},{7,4},{8,11},{9,10},{10,... | collective-permute-start | bytes 49160 | tf_op jit(solution)/shard_map/ppermute | solution.py:23
  40.5 4.6 %collective-permute-start.11 = (f32[8,512]{1,0:T(8,128)S(1)}, f32[8,512]{1,0:T(8,128)S(1)}, u32[]{:S(2)}, u32[]{:S(2)}) collective-permute-start(f32[8,512]{1,0:T(8,128)S(1)} %get-tuple-element.53.refs_0_.refs_1_), channel_id=1, source_target_pairs={{0,2},{1,3},{2,0},{3,1},{4,6},{5,7},{6,4},{7,5},{8,10},{9,11},{10,... | collective-permute-start | bytes 49160 | tf_op jit(solution)/shard_map/ppermute | solution.py:23
  40.5 4.6 %collective-permute-start.12 = (f32[8,512]{1,0:T(8,128)S(1)}, f32[8,512]{1,0:T(8,128)S(1)}, u32[]{:S(2)}, u32[]{:S(2)}) collective-permute-start(f32[8,512]{1,0:T(8,128)S(1)} %get-tuple-element.53.refs_0_.refs_1_), channel_id=1, source_target_pairs={{0,1},{1,0},{2,3},{3,2},{4,5},{5,4},{6,7},{7,6},{8,9},{9,8},{10,11... | collective-permute-start | bytes 49160 | tf_op jit(solution)/shard_map/ppermute | solution.py:23
  48.6 3.5 %collective-permute-start.13 = (bf16[896,896]{1,0:T(8,128)(2,1)S(1)}, bf16[896,896]{1,0:T(8,128)(2,1)S(1)}, u32[]{:S(2)}, u32[]{:S(2)}) collective-permute-start(bf16[896,896]{1,0:T(8,128)(2,1)S(1)} %weight_away.3.refs_0_), channel_id=1, source_target_pairs={{0,4},{4,0},{8,12},{12,8},{16,20},{20,16},{24,28},{28,24},{1,5},{5... | collective-permute-start | bytes 4816904 | tf_op jit(solution)/shard_map/ppermute | solution.py:23
  49.5 7.8 %collective-permute-start.14 = (bf16[896,768]{1,0:T(8,128)(2,1)S(1)}, bf16[896,768]{1,0:T(8,128)(2,1)S(1)}, u32[]{:S(2)}, u32[]{:S(2)}) collective-permute-start(bf16[896,768]{1,0:T(8,128)(2,1)S(1)} %weight_away.4.refs_0_), channel_id=1, source_target_pairs={{0,4},{4,0},{8,12},{12,8},{16,20},{20,16},{24,28},{28,24},{1,5},{5... | collective-permute-start | bytes 4128776 | tf_op jit(solution)/shard_map/ppermute | solution.py:23
  51.0 7.9 %collective-permute-start.15 = (bf16[896,768]{1,0:T(8,128)(2,1)S(1)}, bf16[896,768]{1,0:T(8,128)(2,1)S(1)}, u32[]{:S(2)}, u32[]{:S(2)}) collective-permute-start(bf16[896,768]{1,0:T(8,128)(2,1)S(1)} %weight_away.5.refs_0_), channel_id=1, source_target_pairs={{0,4},{4,0},{8,12},{12,8},{16,20},{20,16},{24,28},{28,24},{1,5},{5... | collective-permute-start | bytes 4128776 | tf_op jit(solution)/shard_map/ppermute | solution.py:23
  53.2 12.8 %collective-permute-start.16 = (bf16[448,896]{1,0:T(8,128)(2,1)S(1)}, bf16[448,896]{1,0:T(8,128)(2,1)S(1)}, u32[]{:S(2)}, u32[]{:S(2)}) collective-permute-start(bf16[448,896]{1,0:T(8,128)(2,1)S(1)} %get-tuple-element.63), channel_id=1, source_target_pairs={{0,16},{4,12},{8,24},{12,4},{16,0},{20,28},{24,8},{28,20},{1,17},{... | collective-permute-start | bytes 2408456 | tf_op jit(solution)/shard_map/ppermute | solution.py:23
  58.3 18.9 %collective-permute-start.18 = (bf16[448,768]{1,0:T(8,128)(2,1)S(1)}, bf16[448,768]{1,0:T(8,128)(2,1)S(1)}, u32[]{:S(2)}, u32[]{:S(2)}) collective-permute-start(bf16[448,768]{1,0:T(8,128)(2,1)S(1)} %get-tuple-element.67), channel_id=1, source_target_pairs={{0,16},{4,12},{8,24},{12,4},{16,0},{20,28},{24,8},{28,20},{1,17},{... | collective-permute-start | bytes 2064392 | tf_op jit(solution)/shard_map/ppermute | solution.py:23
  58.9 13.4 %collective-permute-start.17 = (bf16[128,1792]{1,0:T(8,128)(2,1)S(1)}, bf16[128,1792]{1,0:T(8,128)(2,1)S(1)}, u32[]{:S(2)}, u32[]{:S(2)}) collective-permute-start(bf16[128,1792]{1,0:T(8,128)(2,1)S(1)} %get-tuple-element.59.refs_0_), channel_id=1, source_target_pairs={{0,1},{1,0},{2,3},{3,2},{4,5},{5,4},{6,7},{7,6},{8,9},{9,8},{10,11... | collective-permute-start | bytes 1376264 | tf_op jit(solution)/shard_map/ppermute | solution.py:23
  59.8 28.4 %collective-permute-start.22 = (bf16[448,768]{1,0:T(8,128)(2,1)S(1)}, bf16[448,768]{1,0:T(8,128)(2,1)S(1)}, u32[]{:S(2)}, u32[]{:S(2)}) collective-permute-start(bf16[448,768]{1,0:T(8,128)(2,1)S(1)} %get-tuple-element.75), channel_id=1, source_target_pairs={{0,16},{4,12},{8,24},{12,4},{16,0},{20,28},{24,8},{28,20},{1,17},{... | collective-permute-start | bytes 2064392 | tf_op jit(solution)/shard_map/ppermute | solution.py:23
  63.9 21.7 %collective-permute-start.19 = (bf16[128,1792]{1,0:T(8,128)(2,1)S(1)}, bf16[128,1792]{1,0:T(8,128)(2,1)S(1)}, u32[]{:S(2)}, u32[]{:S(2)}) collective-permute-start(bf16[128,1792]{1,0:T(8,128)(2,1)S(1)} %get-tuple-element.62.refs_0_), channel_id=1, source_target_pairs={{0,1},{1,0},{2,3},{3,2},{4,5},{5,4},{6,7},{7,6},{8,9},{9,8},{10,11... | collective-permute-start | bytes 1376264 | tf_op jit(solution)/shard_map/ppermute | solution.py:23
  66.2 19.7 %collective-permute-start.21 = (bf16[224,896]{1,0:T(8,128)(2,1)S(1)}, bf16[224,896]{1,0:T(8,128)(2,1)S(1)}, u32[]{:S(2)}, u32[]{:S(2)}) collective-permute-start(bf16[224,896]{1,0:T(8,128)(2,1)S(1)} %get-tuple-element.73), channel_id=1, source_target_pairs={{0,8},{4,20},{8,0},{12,28},{16,24},{20,4},{24,16},{28,12},{1,9},{5... | collective-permute-start | bytes 1204232 | tf_op jit(solution)/shard_map/ppermute | solution.py:23
  72.4 13.4 %collective-permute-start.20 = (bf16[64,1792]{1,0:T(8,128)(2,1)S(1)}, bf16[64,1792]{1,0:T(8,128)(2,1)S(1)}, u32[]{:S(2)}, u32[]{:S(2)}) collective-permute-start(bf16[64,1792]{1,0:T(8,128)(2,1)S(1)} %get-tuple-element.71), channel_id=1, source_target_pairs={{0,2},{1,3},{2,0},{3,1},{4,6},{5,7},{6,4},{7,5},{8,10},{9,11},{10,... | collective-permute-start | bytes 688136 | tf_op jit(solution)/shard_map/ppermute | solution.py:23
  77.3 14.1 %collective-permute-start.23 = (bf16[224,768]{1,0:T(8,128)(2,1)S(1)}, bf16[224,768]{1,0:T(8,128)(2,1)S(1)}, u32[]{:S(2)}, u32[]{:S(2)}) collective-permute-start(bf16[224,768]{1,0:T(8,128)(2,1)S(1)} %get-tuple-element.78), channel_id=1, source_target_pairs={{0,8},{4,20},{8,0},{12,28},{16,24},{20,4},{24,16},{28,12},{1,9},{5... | collective-permute-start | bytes 1032200 | tf_op jit(solution)/shard_map/ppermute | solution.py:23
  85.7 11.5 %collective-permute-start.24 = (bf16[64,1792]{1,0:T(8,128)(2,1)S(1)}, bf16[64,1792]{1,0:T(8,128)(2,1)S(1)}, u32[]{:S(2)}, u32[]{:S(2)}) collective-permute-start(bf16[64,1792]{1,0:T(8,128)(2,1)S(1)} %get-tuple-element.80), channel_id=1, source_target_pairs={{0,2},{1,3},{2,0},{3,1},{4,6},{5,7},{6,4},{7,5},{8,10},{9,11},{10,... | collective-permute-start | bytes 688136 | tf_op jit(solution)/shard_map/ppermute | solution.py:23
  88.4 11.8 %collective-permute-start.26 = (bf16[224,768]{1,0:T(8,128)(2,1)S(1)}, bf16[224,768]{1,0:T(8,128)(2,1)S(1)}, u32[]{:S(2)}, u32[]{:S(2)}) collective-permute-start(bf16[224,768]{1,0:T(8,128)(2,1)S(1)} %get-tuple-element.85), channel_id=1, source_target_pairs={{0,8},{4,20},{8,0},{12,28},{16,24},{20,4},{24,16},{28,12},{1,9},{5... | collective-permute-start | bytes 1032200 | tf_op jit(solution)/shard_map/ppermute | solution.py:23
  89.9 8.9 %collective-permute-start.25 = (bf16[64,1920]{1,0:T(8,128)(2,1)S(1)}, bf16[64,1920]{1,0:T(8,128)(2,1)S(1)}, u32[]{:S(2)}, u32[]{:S(2)}) collective-permute-start(bf16[64,1920]{1,0:T(8,128)(2,1)S(1)} %pack.1.refs_0_), channel_id=1, source_target_pairs={{0,16},{16,0},{1,17},{17,1},{2,18},{18,2},{3,19},{19,3},{4,20},{20... | collective-permute-start | bytes 737288 | tf_op jit(solution)/shard_map/ppermute | solution.py:23
  97.3 7.6 %collective-permute-start.27 = (bf16[64,1792]{1,0:T(8,128)(2,1)S(1)}, bf16[64,1792]{1,0:T(8,128)(2,1)S(1)}, u32[]{:S(2)}, u32[]{:S(2)}) collective-permute-start(bf16[64,1792]{1,0:T(8,128)(2,1)S(1)} %add.11.refs_0_), channel_id=1, source_target_pairs={{0,16},{16,0},{1,17},{17,1},{2,18},{18,2},{3,19},{19,3},{4,20},{20... | collective-permute-start | bytes 688136 | tf_op jit(solution)/shard_map/ppermute | solution.py:23
  (1 other events, 3.7 us)

commit v2 on v1

--- a/solution.py
+++ b/solution.py
@@ -15,6 +15,7 @@
 LONG = 20_000_000_000
 COST = 2_000_000_000
 DIGIT = 128
+BAND = 32
 STATS = 8
 QUARTERS = 4
 
@@ -301,39 +302,50 @@
     gather_rows(direct, other, rows_in)
     value = rows_in[...]
 
-    best = None
+    ids = side[0:1, :] - (vocab * width).astype(F32)
+    chosen[...] = spread(ids) - lax.broadcasted_iota(jnp.int32, chosen.shape, 1).astype(F32)
+    for ref in (total, gap, picked):
+        ref[...] = jnp.zeros(ref.shape, F32)
+    inside = rows // QUARTERS
     for start, size in tiles(0, width, 2 * LANES):
         tile = jnp.dot(value, weight[:, start : start + size], preferred_element_type=F32)
         logits[:, start : start + size] = tile
-        for at in range(0, size, LANES):
-            part = tile[:, at : at + LANES]
-            best = part if best is None else jnp.maximum(best, part)
-    top[...] = spread(jnp.max(best.T, axis=0, keepdims=True))
-
-    ids = side[0:1, :] - (vocab * width).astype(F32)
-    chosen[...] = spread(ids) - lax.broadcasted_iota(
-        jnp.int32, chosen.shape, 1
-    ).astype(F32)
-    steps = row_steps(2 * rows, group)
-    for ref in (total, gap, picked):
-        ref[...] = jnp.zeros(ref.shape, F32)
-
-    @pl.loop(0, rows // STEP, unroll=2)
-    def _(i):
-        here, there = steps(i)
-        shift, wanted = top[here, :], chosen[there, :]
-        sums = [jnp.zeros((STEP, LANES), F32)] * 3
-        for start, size in tiles(0, width, LANES):
-            student = logits[here, start : start + size]
-            target = teacher[there, start : start + size].astype(F32)
-            share = jnp.exp(student - shift)
-            sums[0] += share
-            sums[1] += share * (student - target)
-            sums[2] += jnp.where(wanted == start, student, 0.0)
-        total[there, :], gap[there, :], picked[there, :] = sums
+        columns = range(start, start + size, LANES)
+        for at in range(0, rows, BAND):
+            here = slice(at, at + BAND)
+            from_row = (at // inside * 2 + group) * inside + at % inside
+            there = slice(from_row, from_row + BAND)
+            students = [tile[here, c - start : c - start + LANES] for c in columns]
+            best = functools.reduce(jnp.maximum, students)
+            if start:
+                last = top[here, :]
+                best = jnp.maximum(best, last)
+                scale = jnp.exp(last - best)
+                sums = [total[there, :] * scale, gap[there, :] * scale]
+                hit = picked[there, :]
+            else:
+                sums, hit = [0.0, 0.0], 0.0
+            top[here, :] = best
+            wanted = chosen[there, :]
+            for c, student in zip(columns, students):
+                target = teacher[there, c : c + LANES].astype(F32)
+                share = jnp.exp(student - best)
+                sums = [sums[0] + share, sums[1] + share * (student - target)]
+                hit = hit + jnp.where(wanted == c, student, 0.0)
+            total[there, :], gap[there, :], picked[there, :] = *sums, hit
+
+    top_row = jnp.max(top[...].T, axis=0, keepdims=True)
+    whole_top = spread(top_row)
+    for at in range(0, rows, inside):
+        here = slice(at, at + inside)
+        from_row = (at // inside * 2 + group) * inside
+        there = slice(from_row, from_row + inside)
+        scale = jnp.exp(top[here, :] - whole_top[here, :])
+        total[there, :] = total[there, :] * scale
+        gap[there, :] = gap[there, :] * scale
+        top[here, :] = whole_top[here, :]
 
     rows_known = {k: lane_sum(ref) for k, ref in ((1, total), (2, gap), (5, picked))}
-    inside = rows // QUARTERS
     for q in range(QUARTERS):
         at = (2 * q + group) * inside
         total[at : at + inside, :] = top[q * inside : (q + 1) * inside, :]
@@ -381,23 +393,23 @@
     return top, total, gap, teacher_top, teacher_total, picked
 
 
+def join_kernel(first, second, out):
+    rows = join([[p[k : k + 1, :] for k in range(6)] for p in (first, second)])
+    out[...] = jnp.concatenate([*rows, rows[0], rows[0]])
+
+
 def over_vocab(stats, size):
-    parts, done = [stats], 1
-    while done < size:
-        if done > 1:
-            joined = join([[p[k] for k in range(6)] for p in parts])
-            parts = [jnp.stack(list(joined) + [joined[0]] * (STATS - 6))]
-        radix = min(4, size // done)
-        parts += [xor_swap(parts[0], "vocab", k * done) for k in reversed(range(1, radix))]
-        done *= radix
-    return parts
-
-
-def slope_kernel(*refs, parts):
-    stats = refs[:parts]
-    side, *counts, teacher, logits_0, logits_1 = refs[parts : parts + 6]
-    slope_0, slope_1, tokens, lses, shifts, weights = refs[parts + 6 :]
-
+    distance = 1
+    while distance * 2 < size:
+        received = xor_swap(stats, "vocab", distance)
+        (stats,) = call(
+            join_kernel, "join_stats", [shape(stats.shape, F32)], [stats, received]
+        )
+        distance *= 2
+    return [stats, xor_swap(stats, "vocab", distance)]
+
+
+def row_kernel(stats, side, counts, tokens, lses, shifts, weights):
     top, total, gap, teacher_top, teacher_total, picked = join(
         [[s[k : k + 1, :] for k in range(6)] for s in stats]
     )
@@ -409,29 +421,55 @@
     lses[...] = spread(lse)
     shifts[...] = spread(diff + kl)
     weights[...] = spread(side[1:2, :] / jnp.maximum(mask_total, 1.0))
-    for group, (logits, slope) in enumerate(((logits_0, slope_0), (logits_1, slope_1))):
-        rows, width = logits.shape
+
+
+def slope_kernel(lses, shifts, weights, teacher, *refs, start):
+    for group, (logits, slope) in enumerate(zip(refs[:2], refs[2:])):
+        rows, width = slope.shape
         steps = row_steps(2 * rows, group)
 
         @pl.loop(0, rows // STEP, unroll=2)
         def _(i):
             here, there = steps(i)
             lse, shift, weight = lses[there, :], shifts[there, :], weights[there, :]
-            for start, size in tiles(0, width, LANES):
-                student = logits[here, start : start + size]
-                target = teacher[there, start : start + size].astype(F32)
+            for at, size in tiles(0, width, LANES):
+                student = logits[here, start + at : start + at + size]
+                target = teacher[there, start + at : start + at + size].astype(F32)
                 value = weight * jnp.exp(student - lse) * (student - target - shift)
-                slope[here, start : start + size] = value.astype(BF16)
-
-
-def slopes_of(stats, side, counts, teacher, logits, after=()):
-    rows, width = teacher.shape
-    return call(
-        functools.partial(slope_kernel, parts=len(stats)),
+                slope[here, at : at + size] = value.astype(BF16)
+
+
+def first_slopes(stats, side, counts, teacher, logits, size, after=()):
+    rows = teacher.shape[0]
+    parts = len(stats)
+
+    def kernel(*refs):
+        before, (slope_0, slope_1, *after) = refs[: parts + 6], refs[parts + 6 :]
+        side, first, second, teacher, *logits = before[parts:]
+        row_kernel(before[:parts], side, (first, second), *after)
+        slope_kernel(*after[1:], teacher, *logits, slope_0, slope_1, start=0)
+
+    *slopes, tokens, lses, shifts, weights = call(
+        kernel,
         "slopes",
-        [shape((rows // 2, width), BF16)] * 2 + [shape((2, rows), F32)],
+        [shape((rows // 2, size), BF16)] * 2
+        + [shape((2, rows), F32)]
+        + [shape((rows, LANES), F32)] * 3,
         [*stats, side, *counts, teacher, *logits],
-        [pltpu.VMEM((rows, LANES), F32)] * 3,
+        (),
+        after,
+    )
+    return slopes, tokens, (lses, shifts, weights)
+
+
+def more_slopes(columns, teacher, logits, start, size, after=()):
+    rows = teacher.shape[0]
+    return call(
+        functools.partial(slope_kernel, start=start),
+        "slopes",
+        [shape((rows // 2, size), BF16)] * 2,
+        [*columns, teacher, *logits],
+        (),
         after,
     )
 
@@ -485,22 +523,28 @@
     )
 
 
-def hidden_kernel(*refs, vocab_size):
+def hidden_kernel(*refs, vocab_size, groups):
     *slopes, weight, away, home, rows = refs
     blocks = vocab_size
     height = rows.shape[0] // blocks
-    for i, block in enumerate(hidden_order(vocab_size)):
-        to = slice(i * height, (i + 1) * height)
-        if len(slopes) == 1:
-            rows[to, :] = slopes[0][pl.ds(pl.multiple_of(block * height, height), height), :]
-        else:
+    begin = 0
+    for at_part in range(0, len(slopes), groups):
+        part = slopes[at_part : at_part + groups]
+        columns = slice(begin, begin + part[0].shape[1])
+        begin = columns.stop
+        for i, block in enumerate(hidden_order(vocab_size)):
+            to = slice(i * height, (i + 1) * height)
+            if groups == 1:
+                at = pl.multiple_of(block * height, height)
+                rows[to, columns] = part[0][pl.ds(at, height), :]
+                continue
             per = vocab_size // QUARTERS // 2
-            at = (block // (2 * per) * per + block % per) * height
-            for group, slope in enumerate(slopes):
+            at = pl.multiple_of((block // (2 * per) * per + block % per) * height, height)
+            for group, slope in enumerate(part):
 
                 @pl.when(block // per % 2 == group)
                 def _():
-                    rows[to, :] = slope[pl.ds(pl.multiple_of(at, height), height), :]
+                    rows[to, columns] = slope[pl.ds(at, height), :]
 
     value = rows[...]
     middle = away.shape[0]
@@ -515,13 +559,13 @@
 
 def hidden_blocks(slopes, weight, vocab_size, after=()):
     width = weight.shape[1]
-    rows = sum(s.shape[0] for s in slopes)
+    rows = sum(s.shape[0] for s in slopes[0])
     dims = (rows // 2, weight.shape[0])
     return call(
-        functools.partial(hidden_kernel, vocab_size=vocab_size),
+        functools.partial(hidden_kernel, vocab_size=vocab_size, groups=len(slopes[0])),
         "hidden_grad",
         [shape(dims, BF16), shape(dims, F32)],
-        [*slopes, weight],
+        [*sum(slopes, []), weight],
         [pltpu.VMEM((rows, width), BF16)],
         after,
     )
@@ -568,42 +612,35 @@
     return call(pack_kernel, "pack", outs, [kept, received, tokens], (), after)
 
 
-def finish_kernel(*refs, start, so_far, tokens):
-    refs = refs[so_far:]
-    if tokens:
-        strip, out, token, *values, done = refs
-        count, width = strip.shape[0], out.shape[1]
-        folded = jnp.concatenate(
-            [strip[:, at : at + LANES] for at in range(width, strip.shape[1], LANES)]
-        ).astype(F32)
-        for k, value in enumerate(values):
-            size = value.shape[1]
-            value[...] = sum(unfold(folded, k + 2 * term, size) for term in range(3))
-        source, place = strip.at[:, :width], out.at[start : start + count, :]
-    elif len(refs) == 4:
-        strip, out, token, done = refs
-        count = strip.shape[0]
-        source, place = strip, out.at[start : start + count, :]
-    else:
-        kept, received, out, token, source, done = refs
-        source[...] = (kept[...].astype(F32) + received[...].astype(F32)).astype(BF16)
-        place = out.at[:, start : start + source.shape[1]]
+def tokens_kernel(strip, *values, width):
+    folded = jnp.concatenate(
+        [strip[:, at : at + LANES] for at in range(width, strip.shape[1], LANES)]
+    ).astype(F32)
+    for k, value in enumerate(values):
+        size = value.shape[1]
+        value[...] = sum(unfold(folded, k + 2 * term, size) for term in range(3))
+
+
+def tokens_of(strip, rows, width, after):
+    outs = [shape((1, rows), F32)] * 2
+    kernel = functools.partial(tokens_kernel, width=width)
+    return call(kernel, "tokens_of", outs, [strip], (), after)
+
+
+def finish_kernel(*refs, start, so_far):
+    kept, received, out, token, source, done = refs[so_far:]
+    source[...] = (kept[...].astype(F32) + received[...].astype(F32)).astype(BF16)
     token[...] = jnp.zeros(token.shape, F32)
-    run_copies(copy_pairs(source, place), done)
-
-
-def finish(parts, dims, start, so_far, after, tokens=0):
-    outs = [pltpu.HBM(dims, BF16), shape((8, LANES), F32)]
-    outs += [shape((1, tokens), F32)] * 2 if tokens else []
-    scratch = [pltpu.VMEM(parts[0].shape, BF16)] if len(parts) == 2 else []
-    return call(
-        functools.partial(
-            finish_kernel, start=start, so_far=len(so_far), tokens=bool(tokens)
-        ),
+    run_copies(copy_pairs(source, out.at[:, start : start + source.shape[1]]), done)
+
+
+def finish(parts, dims, start, so_far, after):
+    return call(
+        functools.partial(finish_kernel, start=start, so_far=len(so_far)),
         "finish",
-        outs,
+        [pltpu.HBM(dims, BF16), shape((8, LANES), F32)],
         list(parts),
-        scratch + [pltpu.SemaphoreType.DMA((8,))],
+        [pltpu.VMEM(parts[0].shape, BF16), pltpu.SemaphoreType.DMA((8,))],
         after,
         so_far,
         bool(so_far),
@@ -619,15 +656,16 @@
     assert vocab_size & (vocab_size - 1) == 0 and vocab_size >= QUARTERS
 
     ids, mask = token_ids.reshape(1, rows), loss_mask.reshape(1, rows)
-    pieces = list(pick_rows(hidden, [(0, 0)]))
-    pieces += pick_rows(hidden, [(0, 1), (1, 0), (1, 1)], (ids, mask), after=pieces)
+    pieces = []
+    for k, piece in enumerate([(0, 0), (0, 1), (1, 0), (1, 1)]):
+        pieces += pick_rows(hidden, [piece], (ids, mask) if k == 1 else (), after=pieces[-1:])
     direct = [xor_swap(piece, "role", 1) for piece in pieces]
-    known = teacher_stats(teacher_logits, after=pieces[1:2])
+    known = teacher_stats(teacher_logits, after=pieces[3:])
     direct[0] = pass_on(direct[0], [known])
     direct[1], side = unpack_rows(direct[1], rows)
     count = count_rows(side, mask)
     count = sum_rows(count, xor_swap(count, "dp", 1))
-    direct[2] = pass_on(direct[2], [count])
+    direct[3] = pass_on(direct[3], [count])
     counts = [count, xor_swap(count, "dp", 2)]
     other = [xor_swap(piece, "vocab", 1) for piece in direct]
 
@@ -647,36 +685,51 @@
         for values, value in zip((logits, stats), done):
             values.append(value)
         hidden_t.append(turn_rows(direct[pair], other[pair], after=stats[group:]))
-    *slopes, tokens = slopes_of(
-        over_vocab(stats[1], vocab_size), side, counts, teacher_logits, logits, hidden_t[1:]
-    )
-
-    parts = [[s] for s in slopes] if vocab_size == QUARTERS else [slopes]
+    chunks = column_chunks(width, (7, 6, 6))
+    split = chunks[1][0]
+    slopes, tokens, columns = first_slopes(
+        over_vocab(stats[1], vocab_size), side, counts, teacher_logits, logits, split, hidden_t[1:]
+    )
+    ranges = [(0, list(slopes))]
+    last = slopes[1]
+
+    def slope_step(last):
+        slopes = more_slopes(columns, teacher_logits, logits, split, width - split, after=[last])
+        ranges.append((split, list(slopes)))
+        return slopes[1]
+
+    by_group = vocab_size == QUARTERS
     home, hidden_in = [], []
 
     def hidden_step(last):
-        if len(home) < len(parts):
-            some = parts[len(home)]
+        k = len(home)
+        if k == 0 or by_group:
+            some = [s[k : k + 1] if by_group else s for _, s in ranges]
             last, kept = hidden_blocks(some, out_weight, vocab_size, after=[last])
             home.append(kept)
             hidden_in.append(xor_swap(last, "vocab", 1))
         return last
 
-    chunks = column_chunks(width, (7, 6, 6))
     arrived, near = [], []
 
+    def chunk_of(k):
+        start, size = chunks[k]
+        begin, slopes = ranges[min(k, 1)]
+        return slopes, start - begin, size
+
     def away_step(last):
-        last = weight_away(hidden_t, slopes, *chunks[len(arrived)], after=[last])
+        last = weight_away(hidden_t, *chunk_of(len(arrived)), after=[last])
         arrived.append(exchange(last, group_axes, group_size, lambda i: i ^ 1))
         return last
 
     def near_step(last):
         k = len(near)
-        leaving, last = weight_home(hidden_t, slopes, arrived[k], chunks[k][0], after=[last])
+        slopes, start, _ = chunk_of(k)
+        leaving, last = weight_home(hidden_t, slopes, arrived[k], start, after=[last])
         near.append((last, exchange(leaving, group_axes, group_size, near_of)))
         return last
 
-    far, grad_weight, grad_hidden, returned, outs = [], [], [], [], []
+    far, grad_weight, returned, outs = [], [], [], []
 
     def far_step(last):
         kept, received = near[len(far)]
@@ -715,45 +768,26 @@
             returned.append(xor_swap(last, "role", 1))
         return last
 
-    def strip_step(last):
-        if len(grad_hidden) < len(home):
-            k = len(grad_hidden)
-            strip = returned[k]
-            dims = (rows // vocab_size, features)
-            start = k * strip.shape[0] if k == 0 else dims[0] // 2
-            result, last, *values = finish(
-                [strip], dims, start, grad_hidden[-1:], [last], 0 if k else rows
-            )
-            grad_hidden.append(result)
-            outs.extend(values)
-        return last
-
-    last = slopes[1]
-    for step in (
-        away_step,
-        away_step,
-        away_step,
-        near_step,
-        hidden_step,
-        near_step,
-        near_step,
-        hidden_step,
-        far_step,
-        halve_step,
-        far_step,
-        halve_step,
-        return_step,
-        weight_step,
-        far_step,
-        weight_step,
-        return_step,
-        strip_step,
-        weight_step,
-        strip_step,
-    ):
-        last = step(last)
-
-    return outs[0].reshape(rows), outs[1].reshape(rows), grad_hidden[-1], grad_weight[-1]
+    def tokens_step(last):
+        outs.extend(tokens_of(returned[0], rows, features, [last]))
+        return outs[0]
+
+    steps = {
+        "s": slope_step,
+        "a": away_step,
+        "n": near_step,
+        "h": hidden_step,
+        "f": far_step,
+        "v": halve_step,
+        "r": return_step,
+        "w": weight_step,
+        "t": tokens_step,
+    }
+    for name in "asaanhnnhfvrfvwfwrtw":
+        last = steps[name](last)
+
+    grad_hidden = jnp.concatenate([r[:, :features] for r in returned])
+    return outs[0].reshape(rows), outs[1].reshape(rows), grad_hidden, grad_weight[-1]
 
 
 def solution(mesh):

time: 107 us -> 108 us (level)
  starting transfers between devices: 36 us -> 37.8 us
  waiting for transfers between devices: 36.4 us -> 34.7 us
    ppermute x28 -> x27, starting transfers between devices: 36 us -> 37.8 us  [exchange(): return lax.ppermute(array, axes, [(i, partner(i)) for i in range(size)])]
    ppermute x28 -> x27, waiting for transfers between devices: 36.4 us -> 34.7 us  [exchange(): return lax.ppermute(array, axes, [(i, partner(i)) for i in range(size)])]
    pallas_call x33 -> x36, Pallas kernels: 32.8 us -> 32.3 us  [call(): pl.pallas_call(lambda *refs: kernel(*refs[skip:]), in_specs=[pl.BlockSpec...]
  transfers between devices with their start and end apart: 28 -> 27, of which waited for: 13 -> 12; matrix products, arithmetic and copies ran while one was open for 0% -> 0% of each run, Pallas kernels for 22% -> 24%
where the time goes in v2:
time: 108 us; the launch traced here: 107 us
  starting transfers between devices  37.8 us (35%)
  waiting for transfers between devices  34.7 us (32%)
  Pallas kernels  32.3 us (30%)
    ppermute x27, starting transfers between devices, exchange(): return lax.ppermute(array, axes, [(i, partner(i)) for i in range(size)])  37.8 us
    ppermute x27, waiting for transfers between devices, exchange(): return lax.ppermute(array, axes, [(i, partner(i)) for i in range(size)])  34.7 us
    pallas_call x36, Pallas kernels, call(): pl.pallas_call(lambda *refs: kernel(*refs[skip:]), in_specs=[pl.BlockSpec...  32.3 us
  transfers between devices with their start and end apart: 27, of which 12 were waited for; matrix products, arithmetic and copies ran while one was open for 0% of the time, Pallas kernels for 24%

profile of v2, /device:TPU:0, one launch (start us, length us, event | category | flops | bytes accessed | tf_op | source)
XLA Modules:
  0.0 107.2 jit_solution(7818324281382574288)
XLA Ops:
  1.6 3.0 %collective-permute-start.7 = (bf16[64,1792]{1,0:T(8,128)(2,1)S(1)}, bf16[64,1792]{1,0:T(8,128)(2,1)S(1)}, u32[]{:S(2)}, u32[]{:S(2)}) collective-permute-start(bf16[64,1792]{1,0:T(8,128)(2,1)S(1)} %pick_rows.4.refs_0_), channel_id=1, source_target_pairs={{0,16},{16,0},{1,17},{17,1},{2,18},{18,2},{3,19},{19,3},{4,20},{20... | collective-permute-start | bytes 688136 | tf_op jit(solution)/shard_map/ppermute | solution.py:24
  6.6 2.1 %collective-permute-start.3 = (bf16[64,1792]{1,0:T(8,128)(2,1)S(1)}, bf16[64,1792]{1,0:T(8,128)(2,1)S(1)}, u32[]{:S(2)}, u32[]{:S(2)}) collective-permute-start(bf16[64,1792]{1,0:T(8,128)(2,1)S(1)} %pick_rows.6.refs_0_), channel_id=1, source_target_pairs={{0,16},{16,0},{1,17},{17,1},{2,18},{18,2},{3,19},{19,3},{4,20},{20... | collective-permute-start | bytes 688136 | tf_op jit(solution)/shard_map/ppermute | solution.py:24
  9.9 1.9 %teacher_stats.1.refs_0_.refs_8_ = f32[8,512]{1,0:T(8,128)S(1)} custom-call(bf16[64,1792]{1,0:T(8,128)(2,1)S(1)} %pick_rows.7.refs_0_, bf16[512,2432]{1,0:T(8,128)(2,1)S(1)} %copy-done), custom_call_target="tpu_custom_call" | custom-call | flops 20000000000 | bytes 1024 | tf_op jit(solution)/shard_map/teacher_stats/pallas_call | solution.py:39
  11.9 2.1 %collective-permute-start.8 = (bf16[64,1792]{1,0:T(8,128)(2,1)S(1)}, bf16[64,1792]{1,0:T(8,128)(2,1)S(1)}, u32[]{:S(2)}, u32[]{:S(2)}) collective-permute-start(bf16[64,1792]{1,0:T(8,128)(2,1)S(1)} %pass_on.3.refs_1_), channel_id=1, source_target_pairs={{0,1},{1,0},{2,3},{3,2},{4,5},{5,4},{6,7},{7,6},{8,9},{9,8},{10,11... | collective-permute-start | bytes 688136 | tf_op jit(solution)/shard_map/ppermute | solution.py:24
  14.0 2.2 %collective-permute-done.refs_0_ = bf16[64,1920]{1,0:T(8,128)(2,1)S(1)} collective-permute-done((bf16[64,1920]{1,0:T(8,128)(2,1)S(1)}, bf16[64,1920]{1,0:T(8,128)(2,1)S(1)}, u32[]{:S(2)}, u32[]{:S(2)}) %collective-permute-start) | collective-permute-done | bytes 245792 | tf_op jit(solution)/shard_map/ppermute | solution.py:24
  16.3 2.2 %collective-permute-start.9 = (bf16[64,1792]{1,0:T(8,128)(2,1)S(1)}, bf16[64,1792]{1,0:T(8,128)(2,1)S(1)}, u32[]{:S(2)}, u32[]{:S(2)}) collective-permute-start(bf16[64,1792]{1,0:T(8,128)(2,1)S(1)} %get-tuple-element.46.refs_2_), channel_id=1, source_target_pairs={{0,1},{1,0},{2,3},{3,2},{4,5},{5,4},{6,7},{7,6},{8,9},{9,8},{10,11... | collective-permute-start | bytes 688136 | tf_op jit(solution)/shard_map/ppermute | solution.py:24
  18.7 2.5 %collective-permute-done.3.refs_1_ = bf16[64,1792]{1,0:T(8,128)(2,1)S(1)} collective-permute-done((bf16[64,1792]{1,0:T(8,128)(2,1)S(1)}, bf16[64,1792]{1,0:T(8,128)(2,1)S(1)}, u32[]{:S(2)}, u32[]{:S(2)}) %collective-permute-start.3) | collective-permute-done | bytes 229408 | tf_op jit(solution)/shard_map/ppermute | solution.py:24
  21.2 2.1 %collective-permute-start.5 = (bf16[64,1792]{1,0:T(8,128)(2,1)S(1)}, bf16[64,1792]{1,0:T(8,128)(2,1)S(1)}, u32[]{:S(2)}, u32[]{:S(2)}) collective-permute-start(bf16[64,1792]{1,0:T(8,128)(2,1)S(1)} %collective-permute-done.3.refs_1_), channel_id=1, source_target_pairs={{0,1},{1,0},{2,3},{3,2},{4,5},{5,4},{6,7},{7,6},{8,9},{9,8},{10,11... | collective-permute-start | bytes 688136 | tf_op jit(solution)/shard_map/ppermute | solution.py:24
  23.4 1.9 %collective-permute-done.4.refs_1_ = bf16[64,1792]{1,0:T(8,128)(2,1)S(1)} collective-permute-done((bf16[64,1792]{1,0:T(8,128)(2,1)S(1)}, bf16[64,1792]{1,0:T(8,128)(2,1)S(1)}, u32[]{:S(2)}, u32[]{:S(2)}) %collective-permute-start.4) | collective-permute-done | bytes 229408 | tf_op jit(solution)/shard_map/ppermute | solution.py:24
  25.3 1.8 %collective-permute-start.6 = (bf16[64,1792]{1,0:T(8,128)(2,1)S(1)}, bf16[64,1792]{1,0:T(8,128)(2,1)S(1)}, u32[]{:S(2)}, u32[]{:S(2)}) collective-permute-start(bf16[64,1792]{1,0:T(8,128)(2,1)S(1)} %pass_on.2.refs_0_.refs_2_), channel_id=1, source_target_pairs={{0,1},{1,0},{2,3},{3,2},{4,5},{5,4},{6,7},{7,6},{8,9},{9,8},{10,11... | collective-permute-start | bytes 688136 | tf_op jit(solution)/shard_map/ppermute | solution.py:24
  27.1 1.5 %collective-permute-start.2 = (f32[8,128]{1,0:T(8,128)S(1)}, f32[8,128]{1,0:T(8,128)S(1)}, u32[]{:S(2)}, u32[]{:S(2)}) collective-permute-start(f32[8,128]{1,0:T(8,128)S(1)} %sum_rows.1.refs_0_.refs_4_), channel_id=1, source_target_pairs={{0,8},{4,12},{8,0},{12,4},{1,9},{5,13},{9,1},{13,5},{2,10},{6,14},... | collective-permute-start | bytes 12296 | tf_op jit(solution)/shard_map/ppermute | solution.py:24
  28.7 3.6 %group_logits.2 = (f32[256,2432]{1,0:T(8,128)S(1)}, f32[8,512]{1,0:T(8,128)S(1)}) custom-call(bf16[64,1792]{1,0:T(8,128)(2,1)S(1)} %pass_on.2.refs_0_.refs_2_, bf16[64,1792]{1,0:T(8,128)(2,1)S(1)} %pass_on.3.refs_1_, bf16[64,1792]{1,0:T(8,128)(2,1)S(1)} %get-tuple-element.46.refs_2_, bf16[64,1792]{1,0:T(8,128)(2,1)S(1)} %collective-permute-done.8.refs_3_, ...), custom_call_target="tpu_custom_call" | custom-call | flops 2000000000 | bytes 1024 | tf_op jit(solution)/shard_map/group_logits/pallas_call | solution.py:39
  33.3 3.6 %group_logits.3 = (f32[256,2432]{1,0:T(8,128)S(1)}, f32[8,512]{1,0:T(8,128)S(1)}) custom-call(f32[8,128]{1,0:T(8,128)S(1)} %collective-permute-done.2.refs_0_.refs_5_, bf16[64,1792]{1,0:T(8,128)(2,1)S(1)} %collective-permute-done.3.refs_1_, bf16[64,1792]{1,0:T(8,128)(2,1)S(1)} %pass_on.2.refs_0_.refs_2_, ...), custom_call_target="tpu_custom_call" | custom-call | flops 20000000000 | bytes 1024 | tf_op jit(solution)/shard_map/group_logits/pallas_call | solution.py:39
  36.9 1.8 %collective-permute-start.10 = (f32[8,512]{1,0:T(8,128)S(1)}, f32[8,512]{1,0:T(8,128)S(1)}, u32[]{:S(2)}, u32[]{:S(2)}) collective-permute-start(f32[8,512]{1,0:T(8,128)S(1)} %get-tuple-element.48.refs_0_), channel_id=1, source_target_pairs={{0,1},{1,0},{2,3},{3,2},{4,5},{5,4},{6,7},{7,6},{8,9},{9,8},{10,11... | collective-permute-start | bytes 49160 | tf_op jit(solution)/shard_map/ppermute | solution.py:24
  38.7 2.0 %collective-permute-done.10.refs_1_ = f32[8,512]{1,0:T(8,128)S(1)} collective-permute-done((f32[8,512]{1,0:T(8,128)S(1)}, f32[8,512]{1,0:T(8,128)S(1)}, u32[]{:S(2)}, u32[]{:S(2)}) %collective-permute-start.10) | collective-permute-done | bytes 16416 | tf_op jit(solution)/shard_map/ppermute | solution.py:24
  40.7 2.8 %collective-permute-start.11 = (f32[8,512]{1,0:T(8,128)S(1)}, f32[8,512]{1,0:T(8,128)S(1)}, u32[]{:S(2)}, u32[]{:S(2)}) collective-permute-start(f32[8,512]{1,0:T(8,128)S(1)} %join_stats.1.refs_1_), channel_id=1, source_target_pairs={{0,2},{1,3},{2,0},{3,1},{4,6},{5,7},{6,4},{7,5},{8,10},{9,11},{10,... | collective-permute-start | bytes 49160 | tf_op jit(solution)/shard_map/ppermute | solution.py:24
  47.7 1.4 %slopes.3 = (bf16[256,1536]{1,0:T(8,128)(2,1)S(1)}, bf16[256,1536]{1,0:T(8,128)(2,1)S(1)}) custom-call(bf16[896,896]{1,0:T(8,128)(2,1)S(1)} %weight_away.3.refs_0_, f32[512,128]{1,0:T(8,128)S(1)} %get-tuple-element.53.refs_1_, f32[512,128]{1,0:T(8,128)S(1)} %get-tuple-element.54.refs_2_, f32[512,128]{1,0:T(8,128)S(1)} %get-tuple-element.55.refs_3_, ...), custom_call_target="tpu_custom_call" | custom-call | flops 1024 | bytes 1024 | tf_op jit(solution)/shard_map/slopes/pallas_call | solution.py:39
  51.5 1.1 %weight_home.3 = (bf16[448,896]{1,0:T(8,128)(2,1)S(1)}, bf16[448,896]{1,0:T(8,128)(2,1)S(1)}) custom-call(bf16[896,768]{1,0:T(8,128)(2,1)S(1)} %weight_away.5.refs_0_, bf16[1792,256]{1,0:T(8,128)(2,1)S(1)} %turn_rows.3.refs_1_, bf16[1792,256]{1,0:T(8,128)(2,1)S(1)} %turn_rows.2.refs_0_.refs_2_, bf16[256,896]{1,0:T(8,128)(2,1)S(1)} %get-tuple-element.52.refs_3_.refs_1_, ...), custom_call_target="tpu_custom_call" | custom-call | flops 1024 | bytes 1024 | tf_op jit(solution)/shard_map/weight_home/pallas_call | solution.py:39
  52.7 1.7 %collective-permute-start.15 = (bf16[448,896]{1,0:T(8,128)(2,1)S(1)}, bf16[448,896]{1,0:T(8,128)(2,1)S(1)}, u32[]{:S(2)}, u32[]{:S(2)}) collective-permute-start(bf16[448,896]{1,0:T(8,128)(2,1)S(1)} %get-tuple-element.63), channel_id=1, source_target_pairs={{0,16},{4,12},{8,24},{12,4},{16,0},{20,28},{24,8},{28,20},{1,17},{... | collective-permute-start | bytes 2408456 | tf_op jit(solution)/shard_map/ppermute | solution.py:24
  54.4 2.6 %hidden_grad.2 = (bf16[128,1792]{1,0:T(8,128)(2,1)S(1)}, f32[128,1792]{1,0:T(8,128)S(1)}) custom-call(bf16[448,896]{1,0:T(8,128)(2,1)S(1)} %get-tuple-element.58.refs_0_.refs_1_, bf16[256,896]{1,0:T(8,128)(2,1)S(1)} %get-tuple-element.52.refs_3_.refs_1_, bf16[256,1536]{1,0:T(8,128)(2,1)S(1)} %get-tuple-element.57.refs_3_.refs_2_, bf16[1792,2432]{1,0:T(8,128)(2,1)S(1)} %bitcast.5), custom_call_target="tpu_custom_call" | custom-call | flops 1024 | bytes 1024 | tf_op jit(solution)/shard_map/hidden_grad/pallas_call | solution.py:39
  57.0 1.7 %collective-permute-start.16 = (bf16[128,1792]{1,0:T(8,128)(2,1)S(1)}, bf16[128,1792]{1,0:T(8,128)(2,1)S(1)}, u32[]{:S(2)}, u32[]{:S(2)}) collective-permute-start(bf16[128,1792]{1,0:T(8,128)(2,1)S(1)} %get-tuple-element.59.refs_0_), channel_id=1, source_target_pairs={{0,1},{1,0},{2,3},{3,2},{4,5},{5,4},{6,7},{7,6},{8,9},{9,8},{10,11... | collective-permute-start | bytes 1376264 | tf_op jit(solution)/shard_map/ppermute | solution.py:24
  61.1 1.6 %collective-permute-start.21 = (bf16[448,768]{1,0:T(8,128)(2,1)S(1)}, bf16[448,768]{1,0:T(8,128)(2,1)S(1)}, u32[]{:S(2)}, u32[]{:S(2)}) collective-permute-start(bf16[448,768]{1,0:T(8,128)(2,1)S(1)} %get-tuple-element.75), channel_id=1, source_target_pairs={{0,16},{4,12},{8,24},{12,4},{16,0},{20,28},{24,8},{28,20},{1,17},{... | collective-permute-start | bytes 2064392 | tf_op jit(solution)/shard_map/ppermute | solution.py:24
  62.6 2.6 %hidden_grad.3 = (bf16[128,1792]{1,0:T(8,128)(2,1)S(1)}, f32[128,1792]{1,0:T(8,128)S(1)}) custom-call(bf16[448,768]{1,0:T(8,128)(2,1)S(1)} %get-tuple-element.61.refs_0_.refs_1_, bf16[256,896]{1,0:T(8,128)(2,1)S(1)} %get-tuple-element.51.refs_0_.refs_4_.refs_1_, bf16[256,1536]{1,0:T(8,128)(2,1)S(1)} %get-tuple-element.56.refs_0_.refs_4_.refs_2_, ...), custom_call_target="tpu_custom_call" | custom-call | flops 1024 | bytes 1024 | tf_op jit(solution)/shard_map/hidden_grad/pallas_call | solution.py:39
  65.9 4.5 %collective-permute-done.16.refs_2_ = bf16[128,1792]{1,0:T(8,128)(2,1)S(1)} collective-permute-done((bf16[128,1792]{1,0:T(8,128)(2,1)S(1)}, bf16[128,1792]{1,0:T(8,128)(2,1)S(1)}, u32[]{:S(2)}, u32[]{:S(2)}) %collective-permute-start.16) | collective-permute-done | bytes 458784 | tf_op jit(solution)/shard_map/ppermute | solution.py:24
  70.5 2.7 %collective-permute-start.17 = (bf16[64,1792]{1,0:T(8,128)(2,1)S(1)}, bf16[64,1792]{1,0:T(8,128)(2,1)S(1)}, u32[]{:S(2)}, u32[]{:S(2)}) collective-permute-start(bf16[64,1792]{1,0:T(8,128)(2,1)S(1)} %get-tuple-element.67), channel_id=1, source_target_pairs={{0,2},{1,3},{2,0},{3,1},{4,6},{5,7},{6,4},{7,5},{8,10},{9,11},{10,... | collective-permute-start | bytes 688136 | tf_op jit(solution)/shard_map/ppermute | solution.py:24
  73.1 1.6 %collective-permute-start.20 = (bf16[224,896]{1,0:T(8,128)(2,1)S(1)}, bf16[224,896]{1,0:T(8,128)(2,1)S(1)}, u32[]{:S(2)}, u32[]{:S(2)}) collective-permute-start(bf16[224,896]{1,0:T(8,128)(2,1)S(1)} %get-tuple-element.73), channel_id=1, source_target_pairs={{0,8},{4,20},{8,0},{12,28},{16,24},{20,4},{24,16},{28,12},{1,9},{5... | collective-permute-start | bytes 1204232 | tf_op jit(solution)/shard_map/ppermute | solution.py:24
  74.7 8.8 %collective-permute-done.17.refs_2_ = bf16[64,1792]{1,0:T(8,128)(2,1)S(1)} collective-permute-done((bf16[64,1792]{1,0:T(8,128)(2,1)S(1)}, bf16[64,1792]{1,0:T(8,128)(2,1)S(1)}, u32[]{:S(2)}, u32[]{:S(2)}) %collective-permute-start.17) | collective-permute-done | bytes 229408 | tf_op jit(solution)/shard_map/ppermute | solution.py:24
  84.5 3.4 %collective-permute-start.23 = (bf16[64,1792]{1,0:T(8,128)(2,1)S(1)}, bf16[64,1792]{1,0:T(8,128)(2,1)S(1)}, u32[]{:S(2)}, u32[]{:S(2)}) collective-permute-start(bf16[64,1792]{1,0:T(8,128)(2,1)S(1)} %get-tuple-element.80), channel_id=1, source_target_pairs={{0,2},{1,3},{2,0},{3,1},{4,6},{5,7},{6,4},{7,5},{8,10},{9,11},{10,... | collective-permute-start | bytes 688136 | tf_op jit(solution)/shard_map/ppermute | solution.py:24
  89.0 1.6 %collective-permute-start.26 = (bf16[224,768]{1,0:T(8,128)(2,1)S(1)}, bf16[224,768]{1,0:T(8,128)(2,1)S(1)}, u32[]{:S(2)}, u32[]{:S(2)}) collective-permute-start(bf16[224,768]{1,0:T(8,128)(2,1)S(1)} %get-tuple-element.84), channel_id=1, source_target_pairs={{0,8},{4,20},{8,0},{12,28},{16,24},{20,4},{24,16},{28,12},{1,9},{5... | collective-permute-start | bytes 1032200 | tf_op jit(solution)/shard_map/ppermute | solution.py:24
  92.5 6.5 %collective-permute-done.23.refs_2_ = bf16[64,1792]{1,0:T(8,128)(2,1)S(1)} collective-permute-done((bf16[64,1792]{1,0:T(8,128)(2,1)S(1)}, bf16[64,1792]{1,0:T(8,128)(2,1)S(1)}, u32[]{:S(2)}, u32[]{:S(2)}) %collective-permute-start.23) | collective-permute-done | bytes 229408 | tf_op jit(solution)/shard_map/ppermute | solution.py:24
  100.8 1.5 %finish.5 = (bf16[224,2432]{1,0:T(8,128)(2,1)}, f32[8,128]{1,0:T(8,128)}) custom-call(f32[1,512]{1,0:T(1,128)S(1)} %copy-done.2, bf16[224,2432]{1,0:T(8,128)(2,1)} %get-tuple-element.83.refs_1_, bf16[224,768]{1,0:T(8,128)(2,1)S(1)} %get-tuple-element.76.refs_0_.refs_2_, ...), custom_call_target="tpu_custom_call", output_to_operand_aliasing={{0}: (1, {})} | custom-call | flops 1024 | bytes 1024 | tf_op jit(solution)/shard_map/finish/pallas_call | solution.py:39
  102.3 4.2 %collective-permute-done.25 = bf16[64,1792]{1,0:T(8,128)(2,1)S(1)} collective-permute-done((bf16[64,1792]{1,0:T(8,128)(2,1)S(1)}, bf16[64,1792]{1,0:T(8,128)(2,1)S(1)}, u32[]{:S(2)}, u32[]{:S(2)}) %collective-permute-start.25) | collective-permute-done | bytes 229408 | tf_op jit(solution)/shard_map/ppermute | solution.py:24
  (73 shorter events, 21.7 us)
Async XLA Ops:
  1.6 10.3 %collective-permute-start.7 = (bf16[64,1792]{1,0:T(8,128)(2,1)S(1)}, bf16[64,1792]{1,0:T(8,128)(2,1)S(1)}, u32[]{:S(2)}, u32[]{:S(2)}) collective-permute-start(bf16[64,1792]{1,0:T(8,128)(2,1)S(1)} %pick_rows.4.refs_0_), channel_id=1, source_target_pairs={{0,16},{16,0},{1,17},{17,1},{2,18},{18,2},{3,19},{19,3},{4,20},{20... | collective-permute-start | bytes 688136 | tf_op jit(solution)/shard_map/ppermute | solution.py:24
  5.6 10.7 %collective-permute-start = (bf16[64,1920]{1,0:T(8,128)(2,1)S(1)}, bf16[64,1920]{1,0:T(8,128)(2,1)S(1)}, u32[]{:S(2)}, u32[]{:S(2)}) collective-permute-start(bf16[64,1920]{1,0:T(8,128)(2,1)S(1)} %pick_rows.5.refs_0_), channel_id=1, source_target_pairs={{0,16},{16,0},{1,17},{17,1},{2,18},{18,2},{3,19},{19,3},{4,20},{20... | collective-permute-start | bytes 737288 | tf_op jit(solution)/shard_map/ppermute | solution.py:24
  6.6 3.3 %copy-start = (bf16[512,2432]{1,0:T(8,128)(2,1)S(1)}, bf16[512,2432]{1,0:T(8,128)(2,1)}, u32[]{:S(2)}) copy-start(bf16[512,2432]{1,0:T(8,128)(2,1)} %refs_4_.1) | copy-start | bytes 7471108
  6.6 14.6 %collective-permute-start.3 = (bf16[64,1792]{1,0:T(8,128)(2,1)S(1)}, bf16[64,1792]{1,0:T(8,128)(2,1)S(1)}, u32[]{:S(2)}, u32[]{:S(2)}) collective-permute-start(bf16[64,1792]{1,0:T(8,128)(2,1)S(1)} %pick_rows.6.refs_0_), channel_id=1, source_target_pairs={{0,16},{16,0},{1,17},{17,1},{2,18},{18,2},{3,19},{19,3},{4,20},{20... | collective-permute-start | bytes 688136 | tf_op jit(solution)/shard_map/ppermute | solution.py:24
  8.7 19.9 %slice-start = ((s8[8716288]{0:T(1024)(128)(4,1)}), s8[4194304]{0:T(1024)(128)(4,1)S(1)}, s32[]{:S(2)}) async-start(s8[8716288]{0:T(1024)(128)(4,1)} %bitcast.4), calls=%async_computation | async-start | bytes 8388608
  8.7 19.9 %slice-start.1 = ((s8[8716288]{0:T(1024)(128)(4,1)}), s8[4194304]{0:T(1024)(128)(4,1)S(1)}, s32[]{:S(2)}) async-start(s8[8716288]{0:T(1024)(128)(4,1)} %bitcast.4), calls=%async_computation.1 | async-start | bytes 8388608
  9.8 8.7 %copy-start.1 = (s32[512]{0:T(512)S(1)}, s32[512]{0:T(512)}, u32[]{:S(2)}) copy-start(s32[512]{0:T(512)} %param.9) | copy-start | bytes 6148
  9.8 18.8 %slice-start.2 = ((s8[8716288]{0:T(1024)(128)(4,1)}), s8[327680]{0:T(1024)(128)(4,1)S(1)}, s32[]{:S(2)}) async-start(s8[8716288]{0:T(1024)(128)(4,1)} %bitcast.4), calls=%async_computation.2 | async-start | bytes 655360
  9.8 15.5 %collective-permute-start.4 = (bf16[64,1792]{1,0:T(8,128)(2,1)S(1)}, bf16[64,1792]{1,0:T(8,128)(2,1)S(1)}, u32[]{:S(2)}, u32[]{:S(2)}) collective-permute-start(bf16[64,1792]{1,0:T(8,128)(2,1)S(1)} %pick_rows.7.refs_0_), channel_id=1, source_target_pairs={{0,16},{16,0},{1,17},{17,1},{2,18},{18,2},{3,19},{19,3},{4,20},{20... | collective-permute-start | bytes 688136 | tf_op jit(solution)/shard_map/ppermute | solution.py:24
  11.9 16.7 %collective-permute-start.8 = (bf16[64,1792]{1,0:T(8,128)(2,1)S(1)}, bf16[64,1792]{1,0:T(8,128)(2,1)S(1)}, u32[]{:S(2)}, u32[]{:S(2)}) collective-permute-start(bf16[64,1792]{1,0:T(8,128)(2,1)S(1)} %pass_on.3.refs_1_), channel_id=1, source_target_pairs={{0,1},{1,0},{2,3},{3,2},{4,5},{5,4},{6,7},{7,6},{8,9},{9,8},{10,11... | collective-permute-start | bytes 688136 | tf_op jit(solution)/shard_map/ppermute | solution.py:24
  16.3 12.3 %collective-permute-start.9 = (bf16[64,1792]{1,0:T(8,128)(2,1)S(1)}, bf16[64,1792]{1,0:T(8,128)(2,1)S(1)}, u32[]{:S(2)}, u32[]{:S(2)}) collective-permute-start(bf16[64,1792]{1,0:T(8,128)(2,1)S(1)} %get-tuple-element.46.refs_2_), channel_id=1, source_target_pairs={{0,1},{1,0},{2,3},{3,2},{4,5},{5,4},{6,7},{7,6},{8,9},{9,8},{10,11... | collective-permute-start | bytes 688136 | tf_op jit(solution)/shard_map/ppermute | solution.py:24
  18.7 4.7 %collective-permute-start.1 = (f32[8,128]{1,0:T(8,128)S(1)}, f32[8,128]{1,0:T(8,128)S(1)}, u32[]{:S(2)}, u32[]{:S(2)}) collective-permute-start(f32[8,128]{1,0:T(8,128)S(1)} %count_rows.1.refs_0_), channel_id=1, source_target_pairs={{0,4},{4,0},{8,12},{12,8},{1,5},{5,1},{9,13},{13,9},{2,6},{6,2},{1... | collective-permute-start | bytes 12296 | tf_op jit(solution)/shard_map/ppermute | solution.py:24
  21.2 11.1 %collective-permute-start.5 = (bf16[64,1792]{1,0:T(8,128)(2,1)S(1)}, bf16[64,1792]{1,0:T(8,128)(2,1)S(1)}, u32[]{:S(2)}, u32[]{:S(2)}) collective-permute-start(bf16[64,1792]{1,0:T(8,128)(2,1)S(1)} %collective-permute-done.3.refs_1_), channel_id=1, source_target_pairs={{0,1},{1,0},{2,3},{3,2},{4,5},{5,4},{6,7},{7,6},{8,9},{9,8},{10,11... | collective-permute-start | bytes 688136 | tf_op jit(solution)/shard_map/ppermute | solution.py:24
  25.3 8.0 %collective-permute-start.6 = (bf16[64,1792]{1,0:T(8,128)(2,1)S(1)}, bf16[64,1792]{1,0:T(8,128)(2,1)S(1)}, u32[]{:S(2)}, u32[]{:S(2)}) collective-permute-start(bf16[64,1792]{1,0:T(8,128)(2,1)S(1)} %pass_on.2.refs_0_.refs_2_), channel_id=1, source_target_pairs={{0,1},{1,0},{2,3},{3,2},{4,5},{5,4},{6,7},{7,6},{8,9},{9,8},{10,11... | collective-permute-start | bytes 688136 | tf_op jit(solution)/shard_map/ppermute | solution.py:24
  27.1 5.2 %collective-permute-start.2 = (f32[8,128]{1,0:T(8,128)S(1)}, f32[8,128]{1,0:T(8,128)S(1)}, u32[]{:S(2)}, u32[]{:S(2)}) collective-permute-start(f32[8,128]{1,0:T(8,128)S(1)} %sum_rows.1.refs_0_.refs_4_), channel_id=1, source_target_pairs={{0,8},{4,12},{8,0},{12,4},{1,9},{5,13},{9,1},{13,5},{2,10},{6,14},... | collective-permute-start | bytes 12296 | tf_op jit(solution)/shard_map/ppermute | solution.py:24
  36.9 3.8 %collective-permute-start.10 = (f32[8,512]{1,0:T(8,128)S(1)}, f32[8,512]{1,0:T(8,128)S(1)}, u32[]{:S(2)}, u32[]{:S(2)}) collective-permute-start(f32[8,512]{1,0:T(8,128)S(1)} %get-tuple-element.48.refs_0_), channel_id=1, source_target_pairs={{0,1},{1,0},{2,3},{3,2},{4,5},{5,4},{6,7},{7,6},{8,9},{9,8},{10,11... | collective-permute-start | bytes 49160 | tf_op jit(solution)/shard_map/ppermute | solution.py:24
  40.7 4.7 %collective-permute-start.11 = (f32[8,512]{1,0:T(8,128)S(1)}, f32[8,512]{1,0:T(8,128)S(1)}, u32[]{:S(2)}, u32[]{:S(2)}) collective-permute-start(f32[8,512]{1,0:T(8,128)S(1)} %join_stats.1.refs_1_), channel_id=1, source_target_pairs={{0,2},{1,3},{2,0},{3,1},{4,6},{5,7},{6,4},{7,5},{8,10},{9,11},{10,... | collective-permute-start | bytes 49160 | tf_op jit(solution)/shard_map/ppermute | solution.py:24
  47.7 3.9 %collective-permute-start.12 = (bf16[896,896]{1,0:T(8,128)(2,1)S(1)}, bf16[896,896]{1,0:T(8,128)(2,1)S(1)}, u32[]{:S(2)}, u32[]{:S(2)}) collective-permute-start(bf16[896,896]{1,0:T(8,128)(2,1)S(1)} %weight_away.3.refs_0_), channel_id=1, source_target_pairs={{0,4},{4,0},{8,12},{12,8},{16,20},{20,16},{24,28},{28,24},{1,5},{5... | collective-permute-start | bytes 4816904 | tf_op jit(solution)/shard_map/ppermute | solution.py:24
  50.0 8.6 %collective-permute-start.13 = (bf16[896,768]{1,0:T(8,128)(2,1)S(1)}, bf16[896,768]{1,0:T(8,128)(2,1)S(1)}, u32[]{:S(2)}, u32[]{:S(2)}) collective-permute-start(bf16[896,768]{1,0:T(8,128)(2,1)S(1)} %weight_away.4.refs_0_), channel_id=1, source_target_pairs={{0,4},{4,0},{8,12},{12,8},{16,20},{20,16},{24,28},{28,24},{1,5},{5... | collective-permute-start | bytes 4128776 | tf_op jit(solution)/shard_map/ppermute | solution.py:24
  51.4 8.7 %collective-permute-start.14 = (bf16[896,768]{1,0:T(8,128)(2,1)S(1)}, bf16[896,768]{1,0:T(8,128)(2,1)S(1)}, u32[]{:S(2)}, u32[]{:S(2)}) collective-permute-start(bf16[896,768]{1,0:T(8,128)(2,1)S(1)} %weight_away.5.refs_0_), channel_id=1, source_target_pairs={{0,4},{4,0},{8,12},{12,8},{16,20},{20,16},{24,28},{28,24},{1,5},{5... | collective-permute-start | bytes 4128776 | tf_op jit(solution)/shard_map/ppermute | solution.py:24
  52.7 13.1 %collective-permute-start.15 = (bf16[448,896]{1,0:T(8,128)(2,1)S(1)}, bf16[448,896]{1,0:T(8,128)(2,1)S(1)}, u32[]{:S(2)}, u32[]{:S(2)}) collective-permute-start(bf16[448,896]{1,0:T(8,128)(2,1)S(1)} %get-tuple-element.63), channel_id=1, source_target_pairs={{0,16},{4,12},{8,24},{12,4},{16,0},{20,28},{24,8},{28,20},{1,17},{... | collective-permute-start | bytes 2408456 | tf_op jit(solution)/shard_map/ppermute | solution.py:24
  57.0 13.4 %collective-permute-start.16 = (bf16[128,1792]{1,0:T(8,128)(2,1)S(1)}, bf16[128,1792]{1,0:T(8,128)(2,1)S(1)}, u32[]{:S(2)}, u32[]{:S(2)}) collective-permute-start(bf16[128,1792]{1,0:T(8,128)(2,1)S(1)} %get-tuple-element.59.refs_0_), channel_id=1, source_target_pairs={{0,1},{1,0},{2,3},{3,2},{4,5},{5,4},{6,7},{7,6},{8,9},{9,8},{10,11... | collective-permute-start | bytes 1376264 | tf_op jit(solution)/shard_map/ppermute | solution.py:24
  59.5 24.1 %collective-permute-start.18 = (bf16[448,768]{1,0:T(8,128)(2,1)S(1)}, bf16[448,768]{1,0:T(8,128)(2,1)S(1)}, u32[]{:S(2)}, u32[]{:S(2)}) collective-permute-start(bf16[448,768]{1,0:T(8,128)(2,1)S(1)} %get-tuple-element.69), channel_id=1, source_target_pairs={{0,16},{4,12},{8,24},{12,4},{16,0},{20,28},{24,8},{28,20},{1,17},{... | collective-permute-start | bytes 2064392 | tf_op jit(solution)/shard_map/ppermute | solution.py:24
  61.1 27.8 %collective-permute-start.21 = (bf16[448,768]{1,0:T(8,128)(2,1)S(1)}, bf16[448,768]{1,0:T(8,128)(2,1)S(1)}, u32[]{:S(2)}, u32[]{:S(2)}) collective-permute-start(bf16[448,768]{1,0:T(8,128)(2,1)S(1)} %get-tuple-element.75), channel_id=1, source_target_pairs={{0,16},{4,12},{8,24},{12,4},{16,0},{20,28},{24,8},{28,20},{1,17},{... | collective-permute-start | bytes 2064392 | tf_op jit(solution)/shard_map/ppermute | solution.py:24
  65.2 19.2 %collective-permute-start.19 = (bf16[128,1792]{1,0:T(8,128)(2,1)S(1)}, bf16[128,1792]{1,0:T(8,128)(2,1)S(1)}, u32[]{:S(2)}, u32[]{:S(2)}) collective-permute-start(bf16[128,1792]{1,0:T(8,128)(2,1)S(1)} %get-tuple-element.62.refs_0_), channel_id=1, source_target_pairs={{0,1},{1,0},{2,3},{3,2},{4,5},{5,4},{6,7},{7,6},{8,9},{9,8},{10,11... | collective-permute-start | bytes 1376264 | tf_op jit(solution)/shard_map/ppermute | solution.py:24
  70.5 13.1 %collective-permute-start.17 = (bf16[64,1792]{1,0:T(8,128)(2,1)S(1)}, bf16[64,1792]{1,0:T(8,128)(2,1)S(1)}, u32[]{:S(2)}, u32[]{:S(2)}) collective-permute-start(bf16[64,1792]{1,0:T(8,128)(2,1)S(1)} %get-tuple-element.67), channel_id=1, source_target_pairs={{0,2},{1,3},{2,0},{3,1},{4,6},{5,7},{6,4},{7,5},{8,10},{9,11},{10,... | collective-permute-start | bytes 688136 | tf_op jit(solution)/shard_map/ppermute | solution.py:24
  73.1 14.8 %collective-permute-start.20 = (bf16[224,896]{1,0:T(8,128)(2,1)S(1)}, bf16[224,896]{1,0:T(8,128)(2,1)S(1)}, u32[]{:S(2)}, u32[]{:S(2)}) collective-permute-start(bf16[224,896]{1,0:T(8,128)(2,1)S(1)} %get-tuple-element.73), channel_id=1, source_target_pairs={{0,8},{4,20},{8,0},{12,28},{16,24},{20,4},{24,16},{28,12},{1,9},{5... | collective-permute-start | bytes 1204232 | tf_op jit(solution)/shard_map/ppermute | solution.py:24
  83.8 7.8 %collective-permute-start.22 = (bf16[224,768]{1,0:T(8,128)(2,1)S(1)}, bf16[224,768]{1,0:T(8,128)(2,1)S(1)}, u32[]{:S(2)}, u32[]{:S(2)}) collective-permute-start(bf16[224,768]{1,0:T(8,128)(2,1)S(1)} %get-tuple-element.78), channel_id=1, source_target_pairs={{0,8},{4,20},{8,0},{12,28},{16,24},{20,4},{24,16},{28,12},{1,9},{5... | collective-permute-start | bytes 1032200 | tf_op jit(solution)/shard_map/ppermute | solution.py:24
  84.5 14.5 %collective-permute-start.23 = (bf16[64,1792]{1,0:T(8,128)(2,1)S(1)}, bf16[64,1792]{1,0:T(8,128)(2,1)S(1)}, u32[]{:S(2)}, u32[]{:S(2)}) collective-permute-start(bf16[64,1792]{1,0:T(8,128)(2,1)S(1)} %get-tuple-element.80), channel_id=1, source_target_pairs={{0,2},{1,3},{2,0},{3,1},{4,6},{5,7},{6,4},{7,5},{8,10},{9,11},{10,... | collective-permute-start | bytes 688136 | tf_op jit(solution)/shard_map/ppermute | solution.py:24
  89.0 11.1 %collective-permute-start.26 = (bf16[224,768]{1,0:T(8,128)(2,1)S(1)}, bf16[224,768]{1,0:T(8,128)(2,1)S(1)}, u32[]{:S(2)}, u32[]{:S(2)}) collective-permute-start(bf16[224,768]{1,0:T(8,128)(2,1)S(1)} %get-tuple-element.84), channel_id=1, source_target_pairs={{0,8},{4,20},{8,0},{12,28},{16,24},{20,4},{24,16},{28,12},{1,9},{5... | collective-permute-start | bytes 1032200 | tf_op jit(solution)/shard_map/ppermute | solution.py:24
  90.6 8.9 %collective-permute-start.24 = (bf16[64,1920]{1,0:T(8,128)(2,1)S(1)}, bf16[64,1920]{1,0:T(8,128)(2,1)S(1)}, u32[]{:S(2)}, u32[]{:S(2)}) collective-permute-start(bf16[64,1920]{1,0:T(8,128)(2,1)S(1)} %pack.1.refs_0_), channel_id=1, source_target_pairs={{0,16},{16,0},{1,17},{17,1},{2,18},{18,2},{3,19},{19,3},{4,20},{20... | collective-permute-start | bytes 737288 | tf_op jit(solution)/shard_map/ppermute | solution.py:24
  99.0 7.4 %collective-permute-start.25 = (bf16[64,1792]{1,0:T(8,128)(2,1)S(1)}, bf16[64,1792]{1,0:T(8,128)(2,1)S(1)}, u32[]{:S(2)}, u32[]{:S(2)}) collective-permute-start(bf16[64,1792]{1,0:T(8,128)(2,1)S(1)} %add.11.refs_0_), channel_id=1, source_target_pairs={{0,16},{16,0},{1,17},{17,1},{2,18},{18,2},{3,19},{19,3},{4,20},{20... | collective-permute-start | bytes 688136 | tf_op jit(solution)/shard_map/ppermute | solution.py:24
  (1 other events, 0.7 us)

commit v3 on v2

--- a/solution.py
+++ b/solution.py
@@ -393,23 +393,23 @@
     return top, total, gap, teacher_top, teacher_total, picked
 
 
-def join_kernel(first, second, out):
-    rows = join([[p[k : k + 1, :] for k in range(6)] for p in (first, second)])
-    out[...] = jnp.concatenate([*rows, rows[0], rows[0]])
-
-
 def over_vocab(stats, size):
-    distance = 1
-    while distance * 2 < size:
-        received = xor_swap(stats, "vocab", distance)
-        (stats,) = call(
-            join_kernel, "join_stats", [shape(stats.shape, F32)], [stats, received]
-        )
-        distance *= 2
-    return [stats, xor_swap(stats, "vocab", distance)]
-
-
-def row_kernel(stats, side, counts, tokens, lses, shifts, weights):
+    parts, done = [stats], 1
+    while done < size:
+        if done > 1:
+            joined = join([[p[k] for k in range(6)] for p in parts])
+            parts = [jnp.stack(list(joined) + [joined[0]] * (STATS - 6))]
+        radix = min(4, size // done)
+        parts += [xor_swap(parts[0], "vocab", k * done) for k in reversed(range(1, radix))]
+        done *= radix
+    return parts
+
+
+def slope_kernel(*refs, parts):
+    stats = refs[:parts]
+    side, *counts, teacher, logits_0, logits_1 = refs[parts : parts + 6]
+    slope_0, slope_1, tokens, lses, shifts, weights = refs[parts + 6 :]
+
     top, total, gap, teacher_top, teacher_total, picked = join(
         [[s[k : k + 1, :] for k in range(6)] for s in stats]
     )
@@ -421,55 +421,29 @@
     lses[...] = spread(lse)
     shifts[...] = spread(diff + kl)
     weights[...] = spread(side[1:2, :] / jnp.maximum(mask_total, 1.0))
-
-
-def slope_kernel(lses, shifts, weights, teacher, *refs, start):
-    for group, (logits, slope) in enumerate(zip(refs[:2], refs[2:])):
-        rows, width = slope.shape
+    for group, (logits, slope) in enumerate(((logits_0, slope_0), (logits_1, slope_1))):
+        rows, width = logits.shape
         steps = row_steps(2 * rows, group)
 
         @pl.loop(0, rows // STEP, unroll=2)
         def _(i):
             here, there = steps(i)
             lse, shift, weight = lses[there, :], shifts[there, :], weights[there, :]
-            for at, size in tiles(0, width, LANES):
-                student = logits[here, start + at : start + at + size]
-                target = teacher[there, start + at : start + at + size].astype(F32)
+            for start, size in tiles(0, width, LANES):
+                student = logits[here, start : start + size]
+                target = teacher[there, start : start + size].astype(F32)
                 value = weight * jnp.exp(student - lse) * (student - target - shift)
-                slope[here, at : at + size] = value.astype(BF16)
-
-
-def first_slopes(stats, side, counts, teacher, logits, size, after=()):
-    rows = teacher.shape[0]
-    parts = len(stats)
-
-    def kernel(*refs):
-        before, (slope_0, slope_1, *after) = refs[: parts + 6], refs[parts + 6 :]
-        side, first, second, teacher, *logits = before[parts:]
-        row_kernel(before[:parts], side, (first, second), *after)
-        slope_kernel(*after[1:], teacher, *logits, slope_0, slope_1, start=0)
-
-    *slopes, tokens, lses, shifts, weights = call(
-        kernel,
+                slope[here, start : start + size] = value.astype(BF16)
+
+
+def slopes_of(stats, side, counts, teacher, logits, after=()):
+    rows, width = teacher.shape
+    return call(
+        functools.partial(slope_kernel, parts=len(stats)),
         "slopes",
-        [shape((rows // 2, size), BF16)] * 2
-        + [shape((2, rows), F32)]
-        + [shape((rows, LANES), F32)] * 3,
+        [shape((rows // 2, width), BF16)] * 2 + [shape((2, rows), F32)],
         [*stats, side, *counts, teacher, *logits],
-        (),
-        after,
-    )
-    return slopes, tokens, (lses, shifts, weights)
-
-
-def more_slopes(columns, teacher, logits, start, size, after=()):
-    rows = teacher.shape[0]
-    return call(
-        functools.partial(slope_kernel, start=start),
-        "slopes",
-        [shape((rows // 2, size), BF16)] * 2,
-        [*columns, teacher, *logits],
-        (),
+        [pltpu.VMEM((rows, LANES), F32)] * 3,
         after,
     )
 
@@ -523,28 +497,22 @@
     )
 
 
-def hidden_kernel(*refs, vocab_size, groups):
+def hidden_kernel(*refs, vocab_size):
     *slopes, weight, away, home, rows = refs
     blocks = vocab_size
     height = rows.shape[0] // blocks
-    begin = 0
-    for at_part in range(0, len(slopes), groups):
-        part = slopes[at_part : at_part + groups]
-        columns = slice(begin, begin + part[0].shape[1])
-        begin = columns.stop
-        for i, block in enumerate(hidden_order(vocab_size)):
-            to = slice(i * height, (i + 1) * height)
-            if groups == 1:
-                at = pl.multiple_of(block * height, height)
-                rows[to, columns] = part[0][pl.ds(at, height), :]
-                continue
+    for i, block in enumerate(hidden_order(vocab_size)):
+        to = slice(i * height, (i + 1) * height)
+        if len(slopes) == 1:
+            rows[to, :] = slopes[0][pl.ds(pl.multiple_of(block * height, height), height), :]
+        else:
             per = vocab_size // QUARTERS // 2
-            at = pl.multiple_of((block // (2 * per) * per + block % per) * height, height)
-            for group, slope in enumerate(part):
+            at = (block // (2 * per) * per + block % per) * height
+            for group, slope in enumerate(slopes):
 
                 @pl.when(block // per % 2 == group)
                 def _():
-                    rows[to, columns] = slope[pl.ds(at, height), :]
+                    rows[to, :] = slope[pl.ds(pl.multiple_of(at, height), height), :]
 
     value = rows[...]
     middle = away.shape[0]
@@ -559,13 +527,13 @@
 
 def hidden_blocks(slopes, weight, vocab_size, after=()):
     width = weight.shape[1]
-    rows = sum(s.shape[0] for s in slopes[0])
+    rows = sum(s.shape[0] for s in slopes)
     dims = (rows // 2, weight.shape[0])
     return call(
-        functools.partial(hidden_kernel, vocab_size=vocab_size, groups=len(slopes[0])),
+        functools.partial(hidden_kernel, vocab_size=vocab_size),
         "hidden_grad",
         [shape(dims, BF16), shape(dims, F32)],
-        [*sum(slopes, []), weight],
+        [*slopes, weight],
         [pltpu.VMEM((rows, width), BF16)],
         after,
     )
@@ -656,16 +624,15 @@
     assert vocab_size & (vocab_size - 1) == 0 and vocab_size >= QUARTERS
 
     ids, mask = token_ids.reshape(1, rows), loss_mask.reshape(1, rows)
-    pieces = []
-    for k, piece in enumerate([(0, 0), (0, 1), (1, 0), (1, 1)]):
-        pieces += pick_rows(hidden, [piece], (ids, mask) if k == 1 else (), after=pieces[-1:])
+    pieces = list(pick_rows(hidden, [(0, 0)]))
+    pieces += pick_rows(hidden, [(0, 1), (1, 0), (1, 1)], (ids, mask), after=pieces)
     direct = [xor_swap(piece, "role", 1) for piece in pieces]
-    known = teacher_stats(teacher_logits, after=pieces[3:])
+    known = teacher_stats(teacher_logits, after=pieces[1:2])
     direct[0] = pass_on(direct[0], [known])
     direct[1], side = unpack_rows(direct[1], rows)
     count = count_rows(side, mask)
     count = sum_rows(count, xor_swap(count, "dp", 1))
-    direct[3] = pass_on(direct[3], [count])
+    direct[2] = pass_on(direct[2], [count])
     counts = [count, xor_swap(count, "dp", 2)]
     other = [xor_swap(piece, "vocab", 1) for piece in direct]
 
@@ -685,47 +652,32 @@
         for values, value in zip((logits, stats), done):
             values.append(value)
         hidden_t.append(turn_rows(direct[pair], other[pair], after=stats[group:]))
-    chunks = column_chunks(width, (7, 6, 6))
-    split = chunks[1][0]
-    slopes, tokens, columns = first_slopes(
-        over_vocab(stats[1], vocab_size), side, counts, teacher_logits, logits, split, hidden_t[1:]
-    )
-    ranges = [(0, list(slopes))]
-    last = slopes[1]
-
-    def slope_step(last):
-        slopes = more_slopes(columns, teacher_logits, logits, split, width - split, after=[last])
-        ranges.append((split, list(slopes)))
-        return slopes[1]
-
-    by_group = vocab_size == QUARTERS
+    *slopes, tokens = slopes_of(
+        over_vocab(stats[1], vocab_size), side, counts, teacher_logits, logits, hidden_t[1:]
+    )
+
+    parts = [[s] for s in slopes] if vocab_size == QUARTERS else [slopes]
     home, hidden_in = [], []
 
     def hidden_step(last):
-        k = len(home)
-        if k == 0 or by_group:
-            some = [s[k : k + 1] if by_group else s for _, s in ranges]
+        if len(home) < len(parts):
+            some = parts[len(home)]
             last, kept = hidden_blocks(some, out_weight, vocab_size, after=[last])
             home.append(kept)
             hidden_in.append(xor_swap(last, "vocab", 1))
         return last
 
+    chunks = column_chunks(width, (7, 6, 6))
     arrived, near = [], []
 
-    def chunk_of(k):
-        start, size = chunks[k]
-        begin, slopes = ranges[min(k, 1)]
-        return slopes, start - begin, size
-
     def away_step(last):
-        last = weight_away(hidden_t, *chunk_of(len(arrived)), after=[last])
+        last = weight_away(hidden_t, slopes, *chunks[len(arrived)], after=[last])
         arrived.append(exchange(last, group_axes, group_size, lambda i: i ^ 1))
         return last
 
     def near_step(last):
         k = len(near)
-        slopes, start, _ = chunk_of(k)
-        leaving, last = weight_home(hidden_t, slopes, arrived[k], start, after=[last])
+        leaving, last = weight_home(hidden_t, slopes, arrived[k], chunks[k][0], after=[last])
         near.append((last, exchange(leaving, group_axes, group_size, near_of)))
         return last
 
@@ -772,8 +724,8 @@
         outs.extend(tokens_of(returned[0], rows, features, [last]))
         return outs[0]
 
+    last = slopes[1]
     steps = {
-        "s": slope_step,
         "a": away_step,
         "n": near_step,
         "h": hidden_step,
@@ -783,8 +735,9 @@
         "w": weight_step,
         "t": tokens_step,
     }
-    for name in "asaanhnnhfvrfvwfwrtw":
-        last = steps[name](last)
+    for name in "aaanhnnhfvrfvfwwrtw":
+        step = steps[name]
+        last = step(last)
 
     grad_hidden = jnp.concatenate([r[:, :features] for r in returned])
     return outs[0].reshape(rows), outs[1].reshape(rows), grad_hidden, grad_weight[-1]

time: 108 us -> 105 us (0.972)
  Pallas kernels: 32.3 us -> 30.4 us
    pallas_call x36 -> x32, Pallas kernels: 32.3 us -> 30.4 us  [call(): pl.pallas_call(lambda *refs: kernel(*refs[skip:]), in_specs=[pl.BlockSpec...]
    ppermute x27 -> x28, waiting for transfers between devices: 34.7 us -> 33.7 us  [exchange(): return lax.ppermute(array, axes, [(i, partner(i)) for i in range(size)])]
    ppermute x27 -> x28, starting transfers between devices: 37.8 us -> 38.4 us  [exchange(): return lax.ppermute(array, axes, [(i, partner(i)) for i in range(size)])]
  transfers between devices with their start and end apart: 27 -> 28, of which waited for: 12 -> 13; matrix products, arithmetic and copies ran while one was open for 0% -> 0% of each run, Pallas kernels for 24% -> 21%
where the time goes in v3:
time: 105 us
  starting transfers between devices  38.4 us (37%)
  waiting for transfers between devices  33.7 us (32%)
  Pallas kernels  30.4 us (29%)
    ppermute x28, starting transfers between devices, exchange(): return lax.ppermute(array, axes, [(i, partner(i)) for i in range(size)])  38.4 us
    ppermute x28, waiting for transfers between devices, exchange(): return lax.ppermute(array, axes, [(i, partner(i)) for i in range(size)])  33.7 us
    pallas_call x32, Pallas kernels, call(): pl.pallas_call(lambda *refs: kernel(*refs[skip:]), in_specs=[pl.BlockSpec...  30.4 us
  transfers between devices with their start and end apart: 28, of which 13 were waited for; matrix products, arithmetic and copies ran while one was open for 0% of the time, Pallas kernels for 21%

profile of v3, /device:TPU:0, one launch (start us, length us, event | category | flops | bytes accessed | tf_op | source)
XLA Modules:
  0.0 105.0 jit_solution(4964710295504584362)
XLA Ops:
  1.6 3.0 %collective-permute-start.7 = (bf16[64,1792]{1,0:T(8,128)(2,1)S(1)}, bf16[64,1792]{1,0:T(8,128)(2,1)S(1)}, u32[]{:S(2)}, u32[]{:S(2)}) collective-permute-start(bf16[64,1792]{1,0:T(8,128)(2,1)S(1)} %pick_rows.2.refs_0_), channel_id=1, source_target_pairs={{0,16},{16,0},{1,17},{17,1},{2,18},{18,2},{3,19},{19,3},{4,20},{20... | collective-permute-start | bytes 688136 | tf_op jit(solution)/shard_map/ppermute | solution.py:24
  4.6 1.4 %pick_rows.3 = (bf16[64,1920]{1,0:T(8,128)(2,1)S(1)}, bf16[64,1792]{1,0:T(8,128)(2,1)S(1)}, bf16[64,1792]{1,0:T(8,128)(2,1)S(1)}) custom-call(bf16[64,1792]{1,0:T(8,128)(2,1)S(1)} %pick_rows.2.refs_0_, bf16[512,1792]{1,0:T(8,128)(2,1)} %refs_1_.2, s32[1,512]{1,0:T(1,128)} %bitcast.9, s32[1,512]{1,0:T(1,128)} %bitcast.6), custom_call_target="tpu_custom_call" | custom-call | flops 20000000000 | bytes 1024 | tf_op jit(solution)/shard_map/pick_rows/pallas_call | solution.py:39
  6.1 2.0 %collective-permute-start.4 = (bf16[64,1792]{1,0:T(8,128)(2,1)S(1)}, bf16[64,1792]{1,0:T(8,128)(2,1)S(1)}, u32[]{:S(2)}, u32[]{:S(2)}) collective-permute-start(bf16[64,1792]{1,0:T(8,128)(2,1)S(1)} %get-tuple-element.46), channel_id=1, source_target_pairs={{0,16},{16,0},{1,17},{17,1},{2,18},{18,2},{3,19},{19,3},{4,20},{20... | collective-permute-start | bytes 688136 | tf_op jit(solution)/shard_map/ppermute | solution.py:24
  8.3 1.9 %teacher_stats.1.refs_0_.refs_8_ = f32[8,512]{1,0:T(8,128)S(1)} custom-call(bf16[64,1920]{1,0:T(8,128)(2,1)S(1)} %get-tuple-element.43.refs_0_, bf16[512,2432]{1,0:T(8,128)(2,1)S(1)} %copy-done), custom_call_target="tpu_custom_call" | custom-call | flops 20000000000 | bytes 1024 | tf_op jit(solution)/shard_map/teacher_stats/pallas_call | solution.py:39
  11.0 2.1 %collective-permute-start.8 = (bf16[64,1792]{1,0:T(8,128)(2,1)S(1)}, bf16[64,1792]{1,0:T(8,128)(2,1)S(1)}, u32[]{:S(2)}, u32[]{:S(2)}) collective-permute-start(bf16[64,1792]{1,0:T(8,128)(2,1)S(1)} %pass_on.3.refs_1_), channel_id=1, source_target_pairs={{0,1},{1,0},{2,3},{3,2},{4,5},{5,4},{6,7},{7,6},{8,9},{9,8},{10,11... | collective-permute-start | bytes 688136 | tf_op jit(solution)/shard_map/ppermute | solution.py:24
  13.2 3.1 %collective-permute-done.refs_0_ = bf16[64,1920]{1,0:T(8,128)(2,1)S(1)} collective-permute-done((bf16[64,1920]{1,0:T(8,128)(2,1)S(1)}, bf16[64,1920]{1,0:T(8,128)(2,1)S(1)}, u32[]{:S(2)}, u32[]{:S(2)}) %collective-permute-start) | collective-permute-done | bytes 245792 | tf_op jit(solution)/shard_map/ppermute | solution.py:24
  16.3 2.2 %collective-permute-start.9 = (bf16[64,1792]{1,0:T(8,128)(2,1)S(1)}, bf16[64,1792]{1,0:T(8,128)(2,1)S(1)}, u32[]{:S(2)}, u32[]{:S(2)}) collective-permute-start(bf16[64,1792]{1,0:T(8,128)(2,1)S(1)} %get-tuple-element.47.refs_2_), channel_id=1, source_target_pairs={{0,1},{1,0},{2,3},{3,2},{4,5},{5,4},{6,7},{7,6},{8,9},{9,8},{10,11... | collective-permute-start | bytes 688136 | tf_op jit(solution)/shard_map/ppermute | solution.py:24
  18.7 2.5 %collective-permute-done.4.refs_0_.refs_2_ = bf16[64,1792]{1,0:T(8,128)(2,1)S(1)} collective-permute-done((bf16[64,1792]{1,0:T(8,128)(2,1)S(1)}, bf16[64,1792]{1,0:T(8,128)(2,1)S(1)}, u32[]{:S(2)}, u32[]{:S(2)}) %collective-permute-start.4) | collective-permute-done | bytes 229408 | tf_op jit(solution)/shard_map/ppermute | solution.py:24
  21.2 2.1 %collective-permute-start.6 = (bf16[64,1792]{1,0:T(8,128)(2,1)S(1)}, bf16[64,1792]{1,0:T(8,128)(2,1)S(1)}, u32[]{:S(2)}, u32[]{:S(2)}) collective-permute-start(bf16[64,1792]{1,0:T(8,128)(2,1)S(1)} %collective-permute-done.4.refs_0_.refs_2_), channel_id=1, source_target_pairs={{0,1},{1,0},{2,3},{3,2},{4,5},{5,4},{6,7},{7,6},{8,9},{9,8},{10,11... | collective-permute-start | bytes 688136 | tf_op jit(solution)/shard_map/ppermute | solution.py:24
  23.4 1.9 %collective-permute-done.3.refs_1_ = bf16[64,1792]{1,0:T(8,128)(2,1)S(1)} collective-permute-done((bf16[64,1792]{1,0:T(8,128)(2,1)S(1)}, bf16[64,1792]{1,0:T(8,128)(2,1)S(1)}, u32[]{:S(2)}, u32[]{:S(2)}) %collective-permute-start.3) | collective-permute-done | bytes 229408 | tf_op jit(solution)/shard_map/ppermute | solution.py:24
  25.3 1.8 %collective-permute-start.5 = (bf16[64,1792]{1,0:T(8,128)(2,1)S(1)}, bf16[64,1792]{1,0:T(8,128)(2,1)S(1)}, u32[]{:S(2)}, u32[]{:S(2)}) collective-permute-start(bf16[64,1792]{1,0:T(8,128)(2,1)S(1)} %pass_on.2.refs_1_), channel_id=1, source_target_pairs={{0,1},{1,0},{2,3},{3,2},{4,5},{5,4},{6,7},{7,6},{8,9},{9,8},{10,11... | collective-permute-start | bytes 688136 | tf_op jit(solution)/shard_map/ppermute | solution.py:24
  27.1 1.5 %collective-permute-start.2 = (f32[8,128]{1,0:T(8,128)S(1)}, f32[8,128]{1,0:T(8,128)S(1)}, u32[]{:S(2)}, u32[]{:S(2)}) collective-permute-start(f32[8,128]{1,0:T(8,128)S(1)} %sum_rows.1.refs_0_.refs_6_), channel_id=1, source_target_pairs={{0,8},{4,12},{8,0},{12,4},{1,9},{5,13},{9,1},{13,5},{2,10},{6,14},... | collective-permute-start | bytes 12296 | tf_op jit(solution)/shard_map/ppermute | solution.py:24
  28.7 3.6 %group_logits.2 = (f32[256,2432]{1,0:T(8,128)S(1)}, f32[8,512]{1,0:T(8,128)S(1)}) custom-call(bf16[64,1792]{1,0:T(8,128)(2,1)S(1)} %collective-permute-done.4.refs_0_.refs_2_, bf16[64,1792]{1,0:T(8,128)(2,1)S(1)} %pass_on.3.refs_1_, bf16[64,1792]{1,0:T(8,128)(2,1)S(1)} %get-tuple-element.47.refs_2_, bf16[64,1792]{1,0:T(8,128)(2,1)S(1)} %collective-permute-done.8.refs_3_, ...), custom_call_target="tpu_custom_call" | custom-call | flops 2000000000 | bytes 1024 | tf_op jit(solution)/shard_map/group_logits/pallas_call | solution.py:39
  32.4 3.6 %group_logits.3 = (f32[256,2432]{1,0:T(8,128)S(1)}, f32[8,512]{1,0:T(8,128)S(1)}) custom-call(f32[8,128]{1,0:T(8,128)S(1)} %collective-permute-done.2.refs_0_.refs_7_, bf16[64,1792]{1,0:T(8,128)(2,1)S(1)} %pass_on.2.refs_1_, bf16[64,1792]{1,0:T(8,128)(2,1)S(1)} %collective-permute-done.4.refs_0_.refs_2_, ...), custom_call_target="tpu_custom_call" | custom-call | flops 20000000000 | bytes 1024 | tf_op jit(solution)/shard_map/group_logits/pallas_call | solution.py:39
  36.0 4.1 %collective-permute-start.10 = (f32[8,512]{1,0:T(8,128)S(1)}, f32[8,512]{1,0:T(8,128)S(1)}, u32[]{:S(2)}, u32[]{:S(2)}) collective-permute-start(f32[8,512]{1,0:T(8,128)S(1)} %get-tuple-element.49.refs_0_.refs_1_), channel_id=1, source_target_pairs={{0,3},{1,2},{2,1},{3,0},{4,7},{5,6},{6,5},{7,4},{8,11},{9,10},{10,... | collective-permute-start | bytes 49160 | tf_op jit(solution)/shard_map/ppermute | solution.py:24
  41.8 2.9 %collective-permute-done.11.refs_3_ = f32[8,512]{1,0:T(8,128)S(1)} collective-permute-done((f32[8,512]{1,0:T(8,128)S(1)}, f32[8,512]{1,0:T(8,128)S(1)}, u32[]{:S(2)}, u32[]{:S(2)}) %collective-permute-start.11) | collective-permute-done | bytes 16416 | tf_op jit(solution)/shard_map/ppermute | solution.py:24
  44.7 2.3 %slopes.1 = (bf16[256,2432]{1,0:T(8,128)(2,1)S(1)}, bf16[256,2432]{1,0:T(8,128)(2,1)S(1)}, f32[2,512]{1,0:T(2,128)S(1)}) custom-call(bf16[1792,256]{1,0:T(8,128)(2,1)S(1)} %turn_rows.2.refs_0_.refs_2_, f32[8,512]{1,0:T(8,128)S(1)} %get-tuple-element.49.refs_0_.refs_1_, f32[8,512]{1,0:T(8,128)S(1)} %collective-permute-done.10.refs_2_, ...), custom_call_target="tpu_custom_call" | custom-call | flops 1024 | bytes 1024 | tf_op jit(solution)/shard_map/slopes/pallas_call | solution.py:39
  52.8 1.6 %collective-permute-start.16 = (bf16[448,896]{1,0:T(8,128)(2,1)S(1)}, bf16[448,896]{1,0:T(8,128)(2,1)S(1)}, u32[]{:S(2)}, u32[]{:S(2)}) collective-permute-start(bf16[448,896]{1,0:T(8,128)(2,1)S(1)} %get-tuple-element.59), channel_id=1, source_target_pairs={{0,16},{4,12},{8,24},{12,4},{16,0},{20,28},{24,8},{28,20},{1,17},{... | collective-permute-start | bytes 2408456 | tf_op jit(solution)/shard_map/ppermute | solution.py:24
  54.4 2.6 %hidden_grad.2 = (bf16[128,1792]{1,0:T(8,128)(2,1)S(1)}, f32[128,1792]{1,0:T(8,128)S(1)}) custom-call(bf16[448,896]{1,0:T(8,128)(2,1)S(1)} %get-tuple-element.54.refs_0_.refs_1_, bf16[256,2432]{1,0:T(8,128)(2,1)S(1)} %get-tuple-element.53.refs_3_.refs_1_, bf16[1792,2432]{1,0:T(8,128)(2,1)S(1)} %bitcast.5), custom_call_target="tpu_custom_call" | custom-call | flops 1024 | bytes 1024 | tf_op jit(solution)/shard_map/hidden_grad/pallas_call | solution.py:39
  59.4 1.6 %collective-permute-start.21 = (bf16[448,768]{1,0:T(8,128)(2,1)S(1)}, bf16[448,768]{1,0:T(8,128)(2,1)S(1)}, u32[]{:S(2)}, u32[]{:S(2)}) collective-permute-start(bf16[448,768]{1,0:T(8,128)(2,1)S(1)} %get-tuple-element.69), channel_id=1, source_target_pairs={{0,16},{4,12},{8,24},{12,4},{16,0},{20,28},{24,8},{28,20},{1,17},{... | collective-permute-start | bytes 2064392 | tf_op jit(solution)/shard_map/ppermute | solution.py:24
  61.0 2.6 %hidden_grad.3 = (bf16[128,1792]{1,0:T(8,128)(2,1)S(1)}, f32[128,1792]{1,0:T(8,128)S(1)}) custom-call(bf16[448,768]{1,0:T(8,128)(2,1)S(1)} %get-tuple-element.57.refs_0_.refs_1_, bf16[256,2432]{1,0:T(8,128)(2,1)S(1)} %get-tuple-element.52.refs_0_.refs_4_.refs_1_, bf16[1792,2432]{1,0:T(8,128)(2,1)S(1)} %bitcast.5), custom_call_target="tpu_custom_call" | custom-call | flops 1024 | bytes 1024 | tf_op jit(solution)/shard_map/hidden_grad/pallas_call | solution.py:39
  63.6 2.1 %collective-permute-start.20 = (bf16[128,1792]{1,0:T(8,128)(2,1)S(1)}, bf16[128,1792]{1,0:T(8,128)(2,1)S(1)}, u32[]{:S(2)}, u32[]{:S(2)}) collective-permute-start(bf16[128,1792]{1,0:T(8,128)(2,1)S(1)} %get-tuple-element.58.refs_0_), channel_id=1, source_target_pairs={{0,1},{1,0},{2,3},{3,2},{4,5},{5,4},{6,7},{7,6},{8,9},{9,8},{10,11... | collective-permute-start | bytes 1376264 | tf_op jit(solution)/shard_map/ppermute | solution.py:24
  65.8 4.6 %collective-permute-done.17.refs_2_ = bf16[128,1792]{1,0:T(8,128)(2,1)S(1)} collective-permute-done((bf16[128,1792]{1,0:T(8,128)(2,1)S(1)}, bf16[128,1792]{1,0:T(8,128)(2,1)S(1)}, u32[]{:S(2)}, u32[]{:S(2)}) %collective-permute-start.17) | collective-permute-done | bytes 458784 | tf_op jit(solution)/shard_map/ppermute | solution.py:24
  70.5 2.1 %collective-permute-start.18 = (bf16[64,1792]{1,0:T(8,128)(2,1)S(1)}, bf16[64,1792]{1,0:T(8,128)(2,1)S(1)}, u32[]{:S(2)}, u32[]{:S(2)}) collective-permute-start(bf16[64,1792]{1,0:T(8,128)(2,1)S(1)} %get-tuple-element.63), channel_id=1, source_target_pairs={{0,2},{1,3},{2,0},{3,1},{4,6},{5,7},{6,4},{7,5},{8,10},{9,11},{10,... | collective-permute-start | bytes 688136 | tf_op jit(solution)/shard_map/ppermute | solution.py:24
  72.6 2.1 %collective-permute-start.22 = (bf16[224,896]{1,0:T(8,128)(2,1)S(1)}, bf16[224,896]{1,0:T(8,128)(2,1)S(1)}, u32[]{:S(2)}, u32[]{:S(2)}) collective-permute-start(bf16[224,896]{1,0:T(8,128)(2,1)S(1)} %get-tuple-element.71), channel_id=1, source_target_pairs={{0,8},{4,20},{8,0},{12,28},{16,24},{20,4},{24,16},{28,12},{1,9},{5... | collective-permute-start | bytes 1204232 | tf_op jit(solution)/shard_map/ppermute | solution.py:24
  74.7 7.2 %collective-permute-done.18.refs_2_ = bf16[64,1792]{1,0:T(8,128)(2,1)S(1)} collective-permute-done((bf16[64,1792]{1,0:T(8,128)(2,1)S(1)}, bf16[64,1792]{1,0:T(8,128)(2,1)S(1)}, u32[]{:S(2)}, u32[]{:S(2)}) %collective-permute-start.18) | collective-permute-done | bytes 229408 | tf_op jit(solution)/shard_map/ppermute | solution.py:24
  82.1 4.6 %collective-permute-start.23 = (bf16[224,768]{1,0:T(8,128)(2,1)S(1)}, bf16[224,768]{1,0:T(8,128)(2,1)S(1)}, u32[]{:S(2)}, u32[]{:S(2)}) collective-permute-start(bf16[224,768]{1,0:T(8,128)(2,1)S(1)} %get-tuple-element.74), channel_id=1, source_target_pairs={{0,8},{4,20},{8,0},{12,28},{16,24},{20,4},{24,16},{28,12},{1,9},{5... | collective-permute-start | bytes 1032200 | tf_op jit(solution)/shard_map/ppermute | solution.py:24
  88.0 1.2 %collective-permute-start.25 = (bf16[64,1920]{1,0:T(8,128)(2,1)S(1)}, bf16[64,1920]{1,0:T(8,128)(2,1)S(1)}, u32[]{:S(2)}, u32[]{:S(2)}) collective-permute-start(bf16[64,1920]{1,0:T(8,128)(2,1)S(1)} %pack.1.refs_0_), channel_id=1, source_target_pairs={{0,16},{16,0},{1,17},{17,1},{2,18},{18,2},{3,19},{19,3},{4,20},{20... | collective-permute-start | bytes 737288 | tf_op jit(solution)/shard_map/ppermute | solution.py:24
  90.1 1.8 %collective-permute-done.23.refs_3_ = bf16[224,768]{1,0:T(8,128)(2,1)S(1)} collective-permute-done((bf16[224,768]{1,0:T(8,128)(2,1)S(1)}, bf16[224,768]{1,0:T(8,128)(2,1)S(1)}, u32[]{:S(2)}, u32[]{:S(2)}) %collective-permute-start.23) | collective-permute-done | bytes 344096 | tf_op jit(solution)/shard_map/ppermute | solution.py:24
  92.8 5.2 %collective-permute-done.24.refs_2_ = bf16[64,1792]{1,0:T(8,128)(2,1)S(1)} collective-permute-done((bf16[64,1792]{1,0:T(8,128)(2,1)S(1)}, bf16[64,1792]{1,0:T(8,128)(2,1)S(1)}, u32[]{:S(2)}, u32[]{:S(2)}) %collective-permute-start.24) | collective-permute-done | bytes 229408 | tf_op jit(solution)/shard_map/ppermute | solution.py:24
  100.4 1.5 %finish.5 = (bf16[224,2432]{1,0:T(8,128)(2,1)}, f32[8,128]{1,0:T(8,128)}) custom-call(f32[1,512]{1,0:T(1,128)S(1)} %copy-done.2, bf16[224,2432]{1,0:T(8,128)(2,1)} %get-tuple-element.79.refs_1_, bf16[224,768]{1,0:T(8,128)(2,1)S(1)} %get-tuple-element.70.refs_0_.refs_2_, ...), custom_call_target="tpu_custom_call", output_to_operand_aliasing={{0}: (1, {})} | custom-call | flops 1024 | bytes 1024 | tf_op jit(solution)/shard_map/finish/pallas_call | solution.py:39
  101.9 2.3 %collective-permute-done.26 = bf16[64,1792]{1,0:T(8,128)(2,1)S(1)} collective-permute-done((bf16[64,1792]{1,0:T(8,128)(2,1)S(1)}, bf16[64,1792]{1,0:T(8,128)(2,1)S(1)}, u32[]{:S(2)}, u32[]{:S(2)}) %collective-permute-start.26) | collective-permute-done | bytes 229408 | tf_op jit(solution)/shard_map/ppermute | solution.py:24
  (71 shorter events, 18.9 us)
Async XLA Ops:
  1.6 9.4 %collective-permute-start.7 = (bf16[64,1792]{1,0:T(8,128)(2,1)S(1)}, bf16[64,1792]{1,0:T(8,128)(2,1)S(1)}, u32[]{:S(2)}, u32[]{:S(2)}) collective-permute-start(bf16[64,1792]{1,0:T(8,128)(2,1)S(1)} %pick_rows.2.refs_0_), channel_id=1, source_target_pairs={{0,16},{16,0},{1,17},{17,1},{2,18},{18,2},{3,19},{19,3},{4,20},{20... | collective-permute-start | bytes 688136 | tf_op jit(solution)/shard_map/ppermute | solution.py:24
  6.0 10.3 %collective-permute-start = (bf16[64,1920]{1,0:T(8,128)(2,1)S(1)}, bf16[64,1920]{1,0:T(8,128)(2,1)S(1)}, u32[]{:S(2)}, u32[]{:S(2)}) collective-permute-start(bf16[64,1920]{1,0:T(8,128)(2,1)S(1)} %get-tuple-element.43.refs_0_), channel_id=1, source_target_pairs={{0,16},{16,0},{1,17},{17,1},{2,18},{18,2},{3,19},{19,3},{4,20},{20... | collective-permute-start | bytes 737288 | tf_op jit(solution)/shard_map/ppermute | solution.py:24
  6.1 15.1 %collective-permute-start.4 = (bf16[64,1792]{1,0:T(8,128)(2,1)S(1)}, bf16[64,1792]{1,0:T(8,128)(2,1)S(1)}, u32[]{:S(2)}, u32[]{:S(2)}) collective-permute-start(bf16[64,1792]{1,0:T(8,128)(2,1)S(1)} %get-tuple-element.46), channel_id=1, source_target_pairs={{0,16},{16,0},{1,17},{17,1},{2,18},{18,2},{3,19},{19,3},{4,20},{20... | collective-permute-start | bytes 688136 | tf_op jit(solution)/shard_map/ppermute | solution.py:24
  8.1 20.5 %slice-start = ((s8[8716288]{0:T(1024)(128)(4,1)}), s8[4194304]{0:T(1024)(128)(4,1)S(1)}, s32[]{:S(2)}) async-start(s8[8716288]{0:T(1024)(128)(4,1)} %bitcast.4), calls=%async_computation | async-start | bytes 8388608
  8.1 10.4 %copy-start.1 = (s32[512]{0:T(512)S(1)}, s32[512]{0:T(512)}, u32[]{:S(2)}) copy-start(s32[512]{0:T(512)} %param.9) | copy-start | bytes 6148
  8.1 20.5 %slice-start.1 = ((s8[8716288]{0:T(1024)(128)(4,1)}), s8[4194304]{0:T(1024)(128)(4,1)S(1)}, s32[]{:S(2)}) async-start(s8[8716288]{0:T(1024)(128)(4,1)} %bitcast.4), calls=%async_computation.1 | async-start | bytes 8388608
  8.1 20.5 %slice-start.2 = ((s8[8716288]{0:T(1024)(128)(4,1)}), s8[327680]{0:T(1024)(128)(4,1)S(1)}, s32[]{:S(2)}) async-start(s8[8716288]{0:T(1024)(128)(4,1)} %bitcast.4), calls=%async_computation.2 | async-start | bytes 655360
  8.1 17.2 %collective-permute-start.3 = (bf16[64,1792]{1,0:T(8,128)(2,1)S(1)}, bf16[64,1792]{1,0:T(8,128)(2,1)S(1)}, u32[]{:S(2)}, u32[]{:S(2)}) collective-permute-start(bf16[64,1792]{1,0:T(8,128)(2,1)S(1)} %get-tuple-element.45), channel_id=1, source_target_pairs={{0,16},{16,0},{1,17},{17,1},{2,18},{18,2},{3,19},{19,3},{4,20},{20... | collective-permute-start | bytes 688136 | tf_op jit(solution)/shard_map/ppermute | solution.py:24
  11.0 17.6 %collective-permute-start.8 = (bf16[64,1792]{1,0:T(8,128)(2,1)S(1)}, bf16[64,1792]{1,0:T(8,128)(2,1)S(1)}, u32[]{:S(2)}, u32[]{:S(2)}) collective-permute-start(bf16[64,1792]{1,0:T(8,128)(2,1)S(1)} %pass_on.3.refs_1_), channel_id=1, source_target_pairs={{0,1},{1,0},{2,3},{3,2},{4,5},{5,4},{6,7},{7,6},{8,9},{9,8},{10,11... | collective-permute-start | bytes 688136 | tf_op jit(solution)/shard_map/ppermute | solution.py:24
  16.3 12.3 %collective-permute-start.9 = (bf16[64,1792]{1,0:T(8,128)(2,1)S(1)}, bf16[64,1792]{1,0:T(8,128)(2,1)S(1)}, u32[]{:S(2)}, u32[]{:S(2)}) collective-permute-start(bf16[64,1792]{1,0:T(8,128)(2,1)S(1)} %get-tuple-element.47.refs_2_), channel_id=1, source_target_pairs={{0,1},{1,0},{2,3},{3,2},{4,5},{5,4},{6,7},{7,6},{8,9},{9,8},{10,11... | collective-permute-start | bytes 688136 | tf_op jit(solution)/shard_map/ppermute | solution.py:24
  18.7 4.7 %collective-permute-start.1 = (f32[8,128]{1,0:T(8,128)S(1)}, f32[8,128]{1,0:T(8,128)S(1)}, u32[]{:S(2)}, u32[]{:S(2)}) collective-permute-start(f32[8,128]{1,0:T(8,128)S(1)} %count_rows.1.refs_0_), channel_id=1, source_target_pairs={{0,4},{4,0},{8,12},{12,8},{1,5},{5,1},{9,13},{13,9},{2,6},{6,2},{1... | collective-permute-start | bytes 12296 | tf_op jit(solution)/shard_map/ppermute | solution.py:24
  21.2 11.1 %collective-permute-start.6 = (bf16[64,1792]{1,0:T(8,128)(2,1)S(1)}, bf16[64,1792]{1,0:T(8,128)(2,1)S(1)}, u32[]{:S(2)}, u32[]{:S(2)}) collective-permute-start(bf16[64,1792]{1,0:T(8,128)(2,1)S(1)} %collective-permute-done.4.refs_0_.refs_2_), channel_id=1, source_target_pairs={{0,1},{1,0},{2,3},{3,2},{4,5},{5,4},{6,7},{7,6},{8,9},{9,8},{10,11... | collective-permute-start | bytes 688136 | tf_op jit(solution)/shard_map/ppermute | solution.py:24
  25.3 7.1 %collective-permute-start.5 = (bf16[64,1792]{1,0:T(8,128)(2,1)S(1)}, bf16[64,1792]{1,0:T(8,128)(2,1)S(1)}, u32[]{:S(2)}, u32[]{:S(2)}) collective-permute-start(bf16[64,1792]{1,0:T(8,128)(2,1)S(1)} %pass_on.2.refs_1_), channel_id=1, source_target_pairs={{0,1},{1,0},{2,3},{3,2},{4,5},{5,4},{6,7},{7,6},{8,9},{9,8},{10,11... | collective-permute-start | bytes 688136 | tf_op jit(solution)/shard_map/ppermute | solution.py:24
  27.1 5.2 %collective-permute-start.2 = (f32[8,128]{1,0:T(8,128)S(1)}, f32[8,128]{1,0:T(8,128)S(1)}, u32[]{:S(2)}, u32[]{:S(2)}) collective-permute-start(f32[8,128]{1,0:T(8,128)S(1)} %sum_rows.1.refs_0_.refs_6_), channel_id=1, source_target_pairs={{0,8},{4,12},{8,0},{12,4},{1,9},{5,13},{9,1},{13,5},{2,10},{6,14},... | collective-permute-start | bytes 12296 | tf_op jit(solution)/shard_map/ppermute | solution.py:24
  36.0 5.8 %collective-permute-start.10 = (f32[8,512]{1,0:T(8,128)S(1)}, f32[8,512]{1,0:T(8,128)S(1)}, u32[]{:S(2)}, u32[]{:S(2)}) collective-permute-start(f32[8,512]{1,0:T(8,128)S(1)} %get-tuple-element.49.refs_0_.refs_1_), channel_id=1, source_target_pairs={{0,3},{1,2},{2,1},{3,0},{4,7},{5,6},{6,5},{7,4},{8,11},{9,10},{10,... | collective-permute-start | bytes 49160 | tf_op jit(solution)/shard_map/ppermute | solution.py:24
  40.1 4.6 %collective-permute-start.11 = (f32[8,512]{1,0:T(8,128)S(1)}, f32[8,512]{1,0:T(8,128)S(1)}, u32[]{:S(2)}, u32[]{:S(2)}) collective-permute-start(f32[8,512]{1,0:T(8,128)S(1)} %get-tuple-element.49.refs_0_.refs_1_), channel_id=1, source_target_pairs={{0,2},{1,3},{2,0},{3,1},{4,6},{5,7},{6,4},{7,5},{8,10},{9,11},{10,... | collective-permute-start | bytes 49160 | tf_op jit(solution)/shard_map/ppermute | solution.py:24
  40.1 4.6 %collective-permute-start.12 = (f32[8,512]{1,0:T(8,128)S(1)}, f32[8,512]{1,0:T(8,128)S(1)}, u32[]{:S(2)}, u32[]{:S(2)}) collective-permute-start(f32[8,512]{1,0:T(8,128)S(1)} %get-tuple-element.49.refs_0_.refs_1_), channel_id=1, source_target_pairs={{0,1},{1,0},{2,3},{3,2},{4,5},{5,4},{6,7},{7,6},{8,9},{9,8},{10,11... | collective-permute-start | bytes 49160 | tf_op jit(solution)/shard_map/ppermute | solution.py:24
  48.2 3.5 %collective-permute-start.13 = (bf16[896,896]{1,0:T(8,128)(2,1)S(1)}, bf16[896,896]{1,0:T(8,128)(2,1)S(1)}, u32[]{:S(2)}, u32[]{:S(2)}) collective-permute-start(bf16[896,896]{1,0:T(8,128)(2,1)S(1)} %weight_away.3.refs_0_), channel_id=1, source_target_pairs={{0,4},{4,0},{8,12},{12,8},{16,20},{20,16},{24,28},{28,24},{1,5},{5... | collective-permute-start | bytes 4816904 | tf_op jit(solution)/shard_map/ppermute | solution.py:24
  49.1 7.9 %collective-permute-start.14 = (bf16[896,768]{1,0:T(8,128)(2,1)S(1)}, bf16[896,768]{1,0:T(8,128)(2,1)S(1)}, u32[]{:S(2)}, u32[]{:S(2)}) collective-permute-start(bf16[896,768]{1,0:T(8,128)(2,1)S(1)} %weight_away.4.refs_0_), channel_id=1, source_target_pairs={{0,4},{4,0},{8,12},{12,8},{16,20},{20,16},{24,28},{28,24},{1,5},{5... | collective-permute-start | bytes 4128776 | tf_op jit(solution)/shard_map/ppermute | solution.py:24
  50.6 8.0 %collective-permute-start.15 = (bf16[896,768]{1,0:T(8,128)(2,1)S(1)}, bf16[896,768]{1,0:T(8,128)(2,1)S(1)}, u32[]{:S(2)}, u32[]{:S(2)}) collective-permute-start(bf16[896,768]{1,0:T(8,128)(2,1)S(1)} %weight_away.5.refs_0_), channel_id=1, source_target_pairs={{0,4},{4,0},{8,12},{12,8},{16,20},{20,16},{24,28},{28,24},{1,5},{5... | collective-permute-start | bytes 4128776 | tf_op jit(solution)/shard_map/ppermute | solution.py:24
  52.8 12.8 %collective-permute-start.16 = (bf16[448,896]{1,0:T(8,128)(2,1)S(1)}, bf16[448,896]{1,0:T(8,128)(2,1)S(1)}, u32[]{:S(2)}, u32[]{:S(2)}) collective-permute-start(bf16[448,896]{1,0:T(8,128)(2,1)S(1)} %get-tuple-element.59), channel_id=1, source_target_pairs={{0,16},{4,12},{8,24},{12,4},{16,0},{20,28},{24,8},{28,20},{1,17},{... | collective-permute-start | bytes 2408456 | tf_op jit(solution)/shard_map/ppermute | solution.py:24
  57.0 13.5 %collective-permute-start.17 = (bf16[128,1792]{1,0:T(8,128)(2,1)S(1)}, bf16[128,1792]{1,0:T(8,128)(2,1)S(1)}, u32[]{:S(2)}, u32[]{:S(2)}) collective-permute-start(bf16[128,1792]{1,0:T(8,128)(2,1)S(1)} %get-tuple-element.55.refs_0_), channel_id=1, source_target_pairs={{0,1},{1,0},{2,3},{3,2},{4,5},{5,4},{6,7},{7,6},{8,9},{9,8},{10,11... | collective-permute-start | bytes 1376264 | tf_op jit(solution)/shard_map/ppermute | solution.py:24
  57.9 24.0 %collective-permute-start.19 = (bf16[448,768]{1,0:T(8,128)(2,1)S(1)}, bf16[448,768]{1,0:T(8,128)(2,1)S(1)}, u32[]{:S(2)}, u32[]{:S(2)}) collective-permute-start(bf16[448,768]{1,0:T(8,128)(2,1)S(1)} %get-tuple-element.65), channel_id=1, source_target_pairs={{0,16},{4,12},{8,24},{12,4},{16,0},{20,28},{24,8},{28,20},{1,17},{... | collective-permute-start | bytes 2064392 | tf_op jit(solution)/shard_map/ppermute | solution.py:24
  59.4 27.4 %collective-permute-start.21 = (bf16[448,768]{1,0:T(8,128)(2,1)S(1)}, bf16[448,768]{1,0:T(8,128)(2,1)S(1)}, u32[]{:S(2)}, u32[]{:S(2)}) collective-permute-start(bf16[448,768]{1,0:T(8,128)(2,1)S(1)} %get-tuple-element.69), channel_id=1, source_target_pairs={{0,16},{4,12},{8,24},{12,4},{16,0},{20,28},{24,8},{28,20},{1,17},{... | collective-permute-start | bytes 2064392 | tf_op jit(solution)/shard_map/ppermute | solution.py:24
  63.6 23.1 %collective-permute-start.20 = (bf16[128,1792]{1,0:T(8,128)(2,1)S(1)}, bf16[128,1792]{1,0:T(8,128)(2,1)S(1)}, u32[]{:S(2)}, u32[]{:S(2)}) collective-permute-start(bf16[128,1792]{1,0:T(8,128)(2,1)S(1)} %get-tuple-element.58.refs_0_), channel_id=1, source_target_pairs={{0,1},{1,0},{2,3},{3,2},{4,5},{5,4},{6,7},{7,6},{8,9},{9,8},{10,11... | collective-permute-start | bytes 1376264 | tf_op jit(solution)/shard_map/ppermute | solution.py:24
  70.5 11.4 %collective-permute-start.18 = (bf16[64,1792]{1,0:T(8,128)(2,1)S(1)}, bf16[64,1792]{1,0:T(8,128)(2,1)S(1)}, u32[]{:S(2)}, u32[]{:S(2)}) collective-permute-start(bf16[64,1792]{1,0:T(8,128)(2,1)S(1)} %get-tuple-element.63), channel_id=1, source_target_pairs={{0,2},{1,3},{2,0},{3,1},{4,6},{5,7},{6,4},{7,5},{8,10},{9,11},{10,... | collective-permute-start | bytes 688136 | tf_op jit(solution)/shard_map/ppermute | solution.py:24
  72.6 16.6 %collective-permute-start.22 = (bf16[224,896]{1,0:T(8,128)(2,1)S(1)}, bf16[224,896]{1,0:T(8,128)(2,1)S(1)}, u32[]{:S(2)}, u32[]{:S(2)}) collective-permute-start(bf16[224,896]{1,0:T(8,128)(2,1)S(1)} %get-tuple-element.71), channel_id=1, source_target_pairs={{0,8},{4,20},{8,0},{12,28},{16,24},{20,4},{24,16},{28,12},{1,9},{5... | collective-permute-start | bytes 1204232 | tf_op jit(solution)/shard_map/ppermute | solution.py:24
  82.1 9.8 %collective-permute-start.23 = (bf16[224,768]{1,0:T(8,128)(2,1)S(1)}, bf16[224,768]{1,0:T(8,128)(2,1)S(1)}, u32[]{:S(2)}, u32[]{:S(2)}) collective-permute-start(bf16[224,768]{1,0:T(8,128)(2,1)S(1)} %get-tuple-element.74), channel_id=1, source_target_pairs={{0,8},{4,20},{8,0},{12,28},{16,24},{20,4},{24,16},{28,12},{1,9},{5... | collective-permute-start | bytes 1032200 | tf_op jit(solution)/shard_map/ppermute | solution.py:24
  86.8 11.3 %collective-permute-start.24 = (bf16[64,1792]{1,0:T(8,128)(2,1)S(1)}, bf16[64,1792]{1,0:T(8,128)(2,1)S(1)}, u32[]{:S(2)}, u32[]{:S(2)}) collective-permute-start(bf16[64,1792]{1,0:T(8,128)(2,1)S(1)} %get-tuple-element.76), channel_id=1, source_target_pairs={{0,2},{1,3},{2,0},{3,1},{4,6},{5,7},{6,4},{7,5},{8,10},{9,11},{10,... | collective-permute-start | bytes 688136 | tf_op jit(solution)/shard_map/ppermute | solution.py:24
  87.0 12.7 %collective-permute-start.27 = (bf16[224,768]{1,0:T(8,128)(2,1)S(1)}, bf16[224,768]{1,0:T(8,128)(2,1)S(1)}, u32[]{:S(2)}, u32[]{:S(2)}) collective-permute-start(bf16[224,768]{1,0:T(8,128)(2,1)S(1)} %get-tuple-element.80), channel_id=1, source_target_pairs={{0,8},{4,20},{8,0},{12,28},{16,24},{20,4},{24,16},{28,12},{1,9},{5... | collective-permute-start | bytes 1032200 | tf_op jit(solution)/shard_map/ppermute | solution.py:24
  88.0 11.1 %collective-permute-start.25 = (bf16[64,1920]{1,0:T(8,128)(2,1)S(1)}, bf16[64,1920]{1,0:T(8,128)(2,1)S(1)}, u32[]{:S(2)}, u32[]{:S(2)}) collective-permute-start(bf16[64,1920]{1,0:T(8,128)(2,1)S(1)} %pack.1.refs_0_), channel_id=1, source_target_pairs={{0,16},{16,0},{1,17},{17,1},{2,18},{18,2},{3,19},{19,3},{4,20},{20... | collective-permute-start | bytes 737288 | tf_op jit(solution)/shard_map/ppermute | solution.py:24
  98.1 6.1 %collective-permute-start.26 = (bf16[64,1792]{1,0:T(8,128)(2,1)S(1)}, bf16[64,1792]{1,0:T(8,128)(2,1)S(1)}, u32[]{:S(2)}, u32[]{:S(2)}) collective-permute-start(bf16[64,1792]{1,0:T(8,128)(2,1)S(1)} %add.11.refs_0_), channel_id=1, source_target_pairs={{0,16},{16,0},{1,17},{17,1},{2,18},{18,2},{3,19},{19,3},{4,20},{20... | collective-permute-start | bytes 688136 | tf_op jit(solution)/shard_map/ppermute | solution.py:24
  (2 other events, 4.4 us)

commit v4 on v2

--- a/solution.py
+++ b/solution.py
@@ -393,20 +393,16 @@
     return top, total, gap, teacher_top, teacher_total, picked
 
 
-def join_kernel(first, second, out):
-    rows = join([[p[k : k + 1, :] for k in range(6)] for p in (first, second)])
-    out[...] = jnp.concatenate([*rows, rows[0], rows[0]])
-
-
 def over_vocab(stats, size):
-    distance = 1
-    while distance * 2 < size:
-        received = xor_swap(stats, "vocab", distance)
-        (stats,) = call(
-            join_kernel, "join_stats", [shape(stats.shape, F32)], [stats, received]
-        )
-        distance *= 2
-    return [stats, xor_swap(stats, "vocab", distance)]
+    parts, done = [stats], 1
+    while done < size:
+        if done > 1:
+            joined = join([[p[k] for k in range(6)] for p in parts])
+            parts = [jnp.stack(list(joined) + [joined[0]] * (STATS - 6))]
+        radix = min(4, size // done)
+        parts += [xor_swap(parts[0], "vocab", k * done) for k in range(1, radix)]
+        done *= radix
+    return parts
 
 
 def row_kernel(stats, side, counts, tokens, lses, shifts, weights):
@@ -657,10 +653,10 @@
 
     ids, mask = token_ids.reshape(1, rows), loss_mask.reshape(1, rows)
     pieces = []
-    for k, piece in enumerate([(0, 0), (0, 1), (1, 0), (1, 1)]):
-        pieces += pick_rows(hidden, [piece], (ids, mask) if k == 1 else (), after=pieces[-1:])
+    for k, some in enumerate([[(0, 0)], [(0, 1)], [(1, 0), (1, 1)]]):
+        pieces += pick_rows(hidden, some, (ids, mask) if k == 1 else (), after=pieces[-1:])
     direct = [xor_swap(piece, "role", 1) for piece in pieces]
-    known = teacher_stats(teacher_logits, after=pieces[3:])
+    known = teacher_stats(teacher_logits, after=pieces[1:2])
     direct[0] = pass_on(direct[0], [known])
     direct[1], side = unpack_rows(direct[1], rows)
     count = count_rows(side, mask)
@@ -783,7 +779,7 @@
         "w": weight_step,
         "t": tokens_step,
     }
-    for name in "asaanhnnhfvrfvwfwrtw":
+    for name in "asaanhnnhfvrfvfwwrtw":
         last = steps[name](last)
 
     grad_hidden = jnp.concatenate([r[:, :features] for r in returned])

time: 108 us -> 105 us (0.972)
    ppermute x27 -> x28, waiting for transfers between devices: 34.7 us -> 33.7 us  [exchange(): return lax.ppermute(array, axes, [(i, partner(i)) for i in range(size)])]
    ppermute x27 -> x28, starting transfers between devices: 37.8 us -> 36.8 us  [exchange(): return lax.ppermute(array, axes, [(i, partner(i)) for i in range(size)])]
    pallas_call x36 -> x34, Pallas kernels: 32.3 us -> 31.5 us  [call(): pl.pallas_call(lambda *refs: kernel(*refs[skip:]), in_specs=[pl.BlockSpec...]
  transfers between devices with their start and end apart: 27 -> 28, of which waited for: 12 -> 11; matrix products, arithmetic and copies ran while one was open for 0% -> 0% of each run, Pallas kernels for 24% -> 24%
where the time goes in v4:
time: 105 us; the launch traced here: 104 us
  starting transfers between devices  36.8 us (35%)
  waiting for transfers between devices  33.7 us (32%)
  Pallas kernels  31.5 us (30%)
    ppermute x28, starting transfers between devices, exchange(): return lax.ppermute(array, axes, [(i, partner(i)) for i in range(size)])  36.8 us
    ppermute x28, waiting for transfers between devices, exchange(): return lax.ppermute(array, axes, [(i, partner(i)) for i in range(size)])  33.7 us
    pallas_call x34, Pallas kernels, call(): pl.pallas_call(lambda *refs: kernel(*refs[skip:]), in_specs=[pl.BlockSpec...  31.5 us
  transfers between devices with their start and end apart: 28, of which 11 were waited for; matrix products, arithmetic and copies ran while one was open for 0% of the time, Pallas kernels for 24%

profile of v4, /device:TPU:0, one launch (start us, length us, event | category | flops | bytes accessed | tf_op | source)
XLA Modules:
  0.0 104.4 jit_solution(8409951417760614812)
XLA Ops:
  1.6 3.0 %collective-permute-start.7 = (bf16[64,1792]{1,0:T(8,128)(2,1)S(1)}, bf16[64,1792]{1,0:T(8,128)(2,1)S(1)}, u32[]{:S(2)}, u32[]{:S(2)}) collective-permute-start(bf16[64,1792]{1,0:T(8,128)(2,1)S(1)} %pick_rows.3.refs_0_), channel_id=1, source_target_pairs={{0,16},{16,0},{1,17},{17,1},{2,18},{18,2},{3,19},{19,3},{4,20},{20... | collective-permute-start | bytes 688136 | tf_op jit(solution)/shard_map/ppermute | solution.py:24
  6.9 1.9 %collective-permute-start.3 = (bf16[64,1792]{1,0:T(8,128)(2,1)S(1)}, bf16[64,1792]{1,0:T(8,128)(2,1)S(1)}, u32[]{:S(2)}, u32[]{:S(2)}) collective-permute-start(bf16[64,1792]{1,0:T(8,128)(2,1)S(1)} %get-tuple-element.48), channel_id=1, source_target_pairs={{0,16},{16,0},{1,17},{17,1},{2,18},{18,2},{3,19},{19,3},{4,20},{20... | collective-permute-start | bytes 688136 | tf_op jit(solution)/shard_map/ppermute | solution.py:24
  9.1 1.9 %teacher_stats.1.refs_0_.refs_8_ = f32[8,512]{1,0:T(8,128)S(1)} custom-call(bf16[64,1920]{1,0:T(8,128)(2,1)S(1)} %pick_rows.4.refs_0_, bf16[512,2432]{1,0:T(8,128)(2,1)S(1)} %copy-done), custom_call_target="tpu_custom_call" | custom-call | flops 20000000000 | bytes 1024 | tf_op jit(solution)/shard_map/teacher_stats/pallas_call | solution.py:39
  11.1 2.1 %collective-permute-start.8 = (bf16[64,1792]{1,0:T(8,128)(2,1)S(1)}, bf16[64,1792]{1,0:T(8,128)(2,1)S(1)}, u32[]{:S(2)}, u32[]{:S(2)}) collective-permute-start(bf16[64,1792]{1,0:T(8,128)(2,1)S(1)} %pass_on.3.refs_1_), channel_id=1, source_target_pairs={{0,1},{1,0},{2,3},{3,2},{4,5},{5,4},{6,7},{7,6},{8,9},{9,8},{10,11... | collective-permute-start | bytes 688136 | tf_op jit(solution)/shard_map/ppermute | solution.py:24
  13.2 3.1 %collective-permute-done.refs_0_ = bf16[64,1920]{1,0:T(8,128)(2,1)S(1)} collective-permute-done((bf16[64,1920]{1,0:T(8,128)(2,1)S(1)}, bf16[64,1920]{1,0:T(8,128)(2,1)S(1)}, u32[]{:S(2)}, u32[]{:S(2)}) %collective-permute-start) | collective-permute-done | bytes 245792 | tf_op jit(solution)/shard_map/ppermute | solution.py:24
  16.3 2.2 %collective-permute-start.9 = (bf16[64,1792]{1,0:T(8,128)(2,1)S(1)}, bf16[64,1792]{1,0:T(8,128)(2,1)S(1)}, u32[]{:S(2)}, u32[]{:S(2)}) collective-permute-start(bf16[64,1792]{1,0:T(8,128)(2,1)S(1)} %get-tuple-element.50.refs_2_), channel_id=1, source_target_pairs={{0,1},{1,0},{2,3},{3,2},{4,5},{5,4},{6,7},{7,6},{8,9},{9,8},{10,11... | collective-permute-start | bytes 688136 | tf_op jit(solution)/shard_map/ppermute | solution.py:24
  18.7 2.5 %collective-permute-done.3.refs_1_ = bf16[64,1792]{1,0:T(8,128)(2,1)S(1)} collective-permute-done((bf16[64,1792]{1,0:T(8,128)(2,1)S(1)}, bf16[64,1792]{1,0:T(8,128)(2,1)S(1)}, u32[]{:S(2)}, u32[]{:S(2)}) %collective-permute-start.3) | collective-permute-done | bytes 229408 | tf_op jit(solution)/shard_map/ppermute | solution.py:24
  21.2 2.1 %collective-permute-start.5 = (bf16[64,1792]{1,0:T(8,128)(2,1)S(1)}, bf16[64,1792]{1,0:T(8,128)(2,1)S(1)}, u32[]{:S(2)}, u32[]{:S(2)}) collective-permute-start(bf16[64,1792]{1,0:T(8,128)(2,1)S(1)} %collective-permute-done.3.refs_1_), channel_id=1, source_target_pairs={{0,1},{1,0},{2,3},{3,2},{4,5},{5,4},{6,7},{7,6},{8,9},{9,8},{10,11... | collective-permute-start | bytes 688136 | tf_op jit(solution)/shard_map/ppermute | solution.py:24
  23.4 1.9 %collective-permute-done.4.refs_1_ = bf16[64,1792]{1,0:T(8,128)(2,1)S(1)} collective-permute-done((bf16[64,1792]{1,0:T(8,128)(2,1)S(1)}, bf16[64,1792]{1,0:T(8,128)(2,1)S(1)}, u32[]{:S(2)}, u32[]{:S(2)}) %collective-permute-start.4) | collective-permute-done | bytes 229408 | tf_op jit(solution)/shard_map/ppermute | solution.py:24
  25.3 1.8 %collective-permute-start.6 = (bf16[64,1792]{1,0:T(8,128)(2,1)S(1)}, bf16[64,1792]{1,0:T(8,128)(2,1)S(1)}, u32[]{:S(2)}, u32[]{:S(2)}) collective-permute-start(bf16[64,1792]{1,0:T(8,128)(2,1)S(1)} %pass_on.2.refs_0_.refs_2_), channel_id=1, source_target_pairs={{0,1},{1,0},{2,3},{3,2},{4,5},{5,4},{6,7},{7,6},{8,9},{9,8},{10,11... | collective-permute-start | bytes 688136 | tf_op jit(solution)/shard_map/ppermute | solution.py:24
  27.1 1.5 %collective-permute-start.2 = (f32[8,128]{1,0:T(8,128)S(1)}, f32[8,128]{1,0:T(8,128)S(1)}, u32[]{:S(2)}, u32[]{:S(2)}) collective-permute-start(f32[8,128]{1,0:T(8,128)S(1)} %sum_rows.1.refs_0_.refs_6_), channel_id=1, source_target_pairs={{0,8},{4,12},{8,0},{12,4},{1,9},{5,13},{9,1},{13,5},{2,10},{6,14},... | collective-permute-start | bytes 12296 | tf_op jit(solution)/shard_map/ppermute | solution.py:24
  28.7 3.6 %group_logits.2 = (f32[256,2432]{1,0:T(8,128)S(1)}, f32[8,512]{1,0:T(8,128)S(1)}) custom-call(bf16[64,1792]{1,0:T(8,128)(2,1)S(1)} %pass_on.2.refs_0_.refs_2_, bf16[64,1792]{1,0:T(8,128)(2,1)S(1)} %pass_on.3.refs_1_, bf16[64,1792]{1,0:T(8,128)(2,1)S(1)} %get-tuple-element.50.refs_2_, bf16[64,1792]{1,0:T(8,128)(2,1)S(1)} %collective-permute-done.8.refs_3_, ...), custom_call_target="tpu_custom_call" | custom-call | flops 2000000000 | bytes 1024 | tf_op jit(solution)/shard_map/group_logits/pallas_call | solution.py:39
  32.5 3.6 %group_logits.3 = (f32[256,2432]{1,0:T(8,128)S(1)}, f32[8,512]{1,0:T(8,128)S(1)}) custom-call(f32[8,128]{1,0:T(8,128)S(1)} %collective-permute-done.2.refs_0_.refs_7_, bf16[64,1792]{1,0:T(8,128)(2,1)S(1)} %collective-permute-done.3.refs_1_, bf16[64,1792]{1,0:T(8,128)(2,1)S(1)} %pass_on.2.refs_0_.refs_2_, ...), custom_call_target="tpu_custom_call" | custom-call | flops 20000000000 | bytes 1024 | tf_op jit(solution)/shard_map/group_logits/pallas_call | solution.py:39
  36.1 4.0 %collective-permute-start.12 = (f32[8,512]{1,0:T(8,128)S(1)}, f32[8,512]{1,0:T(8,128)S(1)}, u32[]{:S(2)}, u32[]{:S(2)}) collective-permute-start(f32[8,512]{1,0:T(8,128)S(1)} %get-tuple-element.52.refs_0_.refs_1_), channel_id=1, source_target_pairs={{0,3},{1,2},{2,1},{3,0},{4,7},{5,6},{6,5},{7,4},{8,11},{9,10},{10,... | collective-permute-start | bytes 49160 | tf_op jit(solution)/shard_map/ppermute | solution.py:24
  41.8 2.9 %collective-permute-done.11.refs_3_ = f32[8,512]{1,0:T(8,128)S(1)} collective-permute-done((f32[8,512]{1,0:T(8,128)S(1)}, f32[8,512]{1,0:T(8,128)S(1)}, u32[]{:S(2)}, u32[]{:S(2)}) %collective-permute-start.11) | collective-permute-done | bytes 16416 | tf_op jit(solution)/shard_map/ppermute | solution.py:24
  47.0 1.4 %slopes.3 = (bf16[256,1536]{1,0:T(8,128)(2,1)S(1)}, bf16[256,1536]{1,0:T(8,128)(2,1)S(1)}) custom-call(bf16[896,896]{1,0:T(8,128)(2,1)S(1)} %weight_away.3.refs_0_, f32[512,128]{1,0:T(8,128)S(1)} %get-tuple-element.57.refs_1_, f32[512,128]{1,0:T(8,128)S(1)} %get-tuple-element.58.refs_2_, f32[512,128]{1,0:T(8,128)S(1)} %get-tuple-element.59.refs_3_, ...), custom_call_target="tpu_custom_call" | custom-call | flops 1024 | bytes 1024 | tf_op jit(solution)/shard_map/slopes/pallas_call | solution.py:39
  52.0 1.6 %collective-permute-start.16 = (bf16[448,896]{1,0:T(8,128)(2,1)S(1)}, bf16[448,896]{1,0:T(8,128)(2,1)S(1)}, u32[]{:S(2)}, u32[]{:S(2)}) collective-permute-start(bf16[448,896]{1,0:T(8,128)(2,1)S(1)} %get-tuple-element.67), channel_id=1, source_target_pairs={{0,16},{4,12},{8,24},{12,4},{16,0},{20,28},{24,8},{28,20},{1,17},{... | collective-permute-start | bytes 2408456 | tf_op jit(solution)/shard_map/ppermute | solution.py:24
  53.5 2.6 %hidden_grad.2 = (bf16[128,1792]{1,0:T(8,128)(2,1)S(1)}, f32[128,1792]{1,0:T(8,128)S(1)}) custom-call(bf16[448,896]{1,0:T(8,128)(2,1)S(1)} %get-tuple-element.62.refs_0_.refs_1_, bf16[256,896]{1,0:T(8,128)(2,1)S(1)} %get-tuple-element.56.refs_3_.refs_1_, bf16[256,1536]{1,0:T(8,128)(2,1)S(1)} %get-tuple-element.61.refs_3_.refs_2_, bf16[1792,2432]{1,0:T(8,128)(2,1)S(1)} %bitcast.5), custom_call_target="tpu_custom_call" | custom-call | flops 1024 | bytes 1024 | tf_op jit(solution)/shard_map/hidden_grad/pallas_call | solution.py:39
  58.6 1.6 %collective-permute-start.21 = (bf16[448,768]{1,0:T(8,128)(2,1)S(1)}, bf16[448,768]{1,0:T(8,128)(2,1)S(1)}, u32[]{:S(2)}, u32[]{:S(2)}) collective-permute-start(bf16[448,768]{1,0:T(8,128)(2,1)S(1)} %get-tuple-element.77), channel_id=1, source_target_pairs={{0,16},{4,12},{8,24},{12,4},{16,0},{20,28},{24,8},{28,20},{1,17},{... | collective-permute-start | bytes 2064392 | tf_op jit(solution)/shard_map/ppermute | solution.py:24
  60.2 2.6 %hidden_grad.3 = (bf16[128,1792]{1,0:T(8,128)(2,1)S(1)}, f32[128,1792]{1,0:T(8,128)S(1)}) custom-call(bf16[448,768]{1,0:T(8,128)(2,1)S(1)} %get-tuple-element.65.refs_0_.refs_1_, bf16[256,896]{1,0:T(8,128)(2,1)S(1)} %get-tuple-element.55.refs_0_.refs_4_.refs_1_, bf16[256,1536]{1,0:T(8,128)(2,1)S(1)} %get-tuple-element.60.refs_0_.refs_4_.refs_2_, ...), custom_call_target="tpu_custom_call" | custom-call | flops 1024 | bytes 1024 | tf_op jit(solution)/shard_map/hidden_grad/pallas_call | solution.py:39
  62.8 2.1 %collective-permute-start.20 = (bf16[128,1792]{1,0:T(8,128)(2,1)S(1)}, bf16[128,1792]{1,0:T(8,128)(2,1)S(1)}, u32[]{:S(2)}, u32[]{:S(2)}) collective-permute-start(bf16[128,1792]{1,0:T(8,128)(2,1)S(1)} %get-tuple-element.66.refs_0_), channel_id=1, source_target_pairs={{0,1},{1,0},{2,3},{3,2},{4,5},{5,4},{6,7},{7,6},{8,9},{9,8},{10,11... | collective-permute-start | bytes 1376264 | tf_op jit(solution)/shard_map/ppermute | solution.py:24
  65.1 4.5 %collective-permute-done.17.refs_2_ = bf16[128,1792]{1,0:T(8,128)(2,1)S(1)} collective-permute-done((bf16[128,1792]{1,0:T(8,128)(2,1)S(1)}, bf16[128,1792]{1,0:T(8,128)(2,1)S(1)}, u32[]{:S(2)}, u32[]{:S(2)}) %collective-permute-start.17) | collective-permute-done | bytes 458784 | tf_op jit(solution)/shard_map/ppermute | solution.py:24
  69.6 2.1 %collective-permute-start.18 = (bf16[64,1792]{1,0:T(8,128)(2,1)S(1)}, bf16[64,1792]{1,0:T(8,128)(2,1)S(1)}, u32[]{:S(2)}, u32[]{:S(2)}) collective-permute-start(bf16[64,1792]{1,0:T(8,128)(2,1)S(1)} %get-tuple-element.71), channel_id=1, source_target_pairs={{0,2},{1,3},{2,0},{3,1},{4,6},{5,7},{6,4},{7,5},{8,10},{9,11},{10,... | collective-permute-start | bytes 688136 | tf_op jit(solution)/shard_map/ppermute | solution.py:24
  71.7 1.6 %collective-permute-start.22 = (bf16[224,896]{1,0:T(8,128)(2,1)S(1)}, bf16[224,896]{1,0:T(8,128)(2,1)S(1)}, u32[]{:S(2)}, u32[]{:S(2)}) collective-permute-start(bf16[224,896]{1,0:T(8,128)(2,1)S(1)} %get-tuple-element.79), channel_id=1, source_target_pairs={{0,8},{4,20},{8,0},{12,28},{16,24},{20,4},{24,16},{28,12},{1,9},{5... | collective-permute-start | bytes 1204232 | tf_op jit(solution)/shard_map/ppermute | solution.py:24
  73.3 8.1 %collective-permute-done.18.refs_2_ = bf16[64,1792]{1,0:T(8,128)(2,1)S(1)} collective-permute-done((bf16[64,1792]{1,0:T(8,128)(2,1)S(1)}, bf16[64,1792]{1,0:T(8,128)(2,1)S(1)}, u32[]{:S(2)}, u32[]{:S(2)}) %collective-permute-start.18) | collective-permute-done | bytes 229408 | tf_op jit(solution)/shard_map/ppermute | solution.py:24
  82.2 1.4 %collective-permute-done.20.refs_2_ = bf16[128,1792]{1,0:T(8,128)(2,1)S(1)} collective-permute-done((bf16[128,1792]{1,0:T(8,128)(2,1)S(1)}, bf16[128,1792]{1,0:T(8,128)(2,1)S(1)}, u32[]{:S(2)}, u32[]{:S(2)}) %collective-permute-start.20) | collective-permute-done | bytes 458784 | tf_op jit(solution)/shard_map/ppermute | solution.py:24
  83.7 2.1 %collective-permute-start.24 = (bf16[64,1792]{1,0:T(8,128)(2,1)S(1)}, bf16[64,1792]{1,0:T(8,128)(2,1)S(1)}, u32[]{:S(2)}, u32[]{:S(2)}) collective-permute-start(bf16[64,1792]{1,0:T(8,128)(2,1)S(1)} %get-tuple-element.84), channel_id=1, source_target_pairs={{0,2},{1,3},{2,0},{3,1},{4,6},{5,7},{6,4},{7,5},{8,10},{9,11},{10,... | collective-permute-start | bytes 688136 | tf_op jit(solution)/shard_map/ppermute | solution.py:24
  85.9 1.6 %collective-permute-start.27 = (bf16[224,768]{1,0:T(8,128)(2,1)S(1)}, bf16[224,768]{1,0:T(8,128)(2,1)S(1)}, u32[]{:S(2)}, u32[]{:S(2)}) collective-permute-start(bf16[224,768]{1,0:T(8,128)(2,1)S(1)} %get-tuple-element.88), channel_id=1, source_target_pairs={{0,8},{4,20},{8,0},{12,28},{16,24},{20,4},{24,16},{28,12},{1,9},{5... | collective-permute-start | bytes 1032200 | tf_op jit(solution)/shard_map/ppermute | solution.py:24
  89.9 6.6 %collective-permute-done.24.refs_2_ = bf16[64,1792]{1,0:T(8,128)(2,1)S(1)} collective-permute-done((bf16[64,1792]{1,0:T(8,128)(2,1)S(1)}, bf16[64,1792]{1,0:T(8,128)(2,1)S(1)}, u32[]{:S(2)}, u32[]{:S(2)}) %collective-permute-start.24) | collective-permute-done | bytes 229408 | tf_op jit(solution)/shard_map/ppermute | solution.py:24
  96.5 1.9 %collective-permute-start.26 = (bf16[64,1792]{1,0:T(8,128)(2,1)S(1)}, bf16[64,1792]{1,0:T(8,128)(2,1)S(1)}, u32[]{:S(2)}, u32[]{:S(2)}) collective-permute-start(bf16[64,1792]{1,0:T(8,128)(2,1)S(1)} %add.11.refs_0_), channel_id=1, source_target_pairs={{0,16},{16,0},{1,17},{17,1},{2,18},{18,2},{3,19},{19,3},{4,20},{20... | collective-permute-start | bytes 688136 | tf_op jit(solution)/shard_map/ppermute | solution.py:24
  99.8 1.5 %finish.5 = (bf16[224,2432]{1,0:T(8,128)(2,1)}, f32[8,128]{1,0:T(8,128)}) custom-call(f32[1,512]{1,0:T(1,128)S(1)} %copy-done.2, bf16[224,2432]{1,0:T(8,128)(2,1)} %get-tuple-element.87.refs_1_, bf16[224,768]{1,0:T(8,128)(2,1)S(1)} %get-tuple-element.78.refs_0_.refs_2_, ...), custom_call_target="tpu_custom_call", output_to_operand_aliasing={{0}: (1, {})} | custom-call | flops 1024 | bytes 1024 | tf_op jit(solution)/shard_map/finish/pallas_call | solution.py:39
  101.2 2.4 %collective-permute-done.26 = bf16[64,1792]{1,0:T(8,128)(2,1)S(1)} collective-permute-done((bf16[64,1792]{1,0:T(8,128)(2,1)S(1)}, bf16[64,1792]{1,0:T(8,128)(2,1)S(1)}, u32[]{:S(2)}, u32[]{:S(2)}) %collective-permute-start.26) | collective-permute-done | bytes 229408 | tf_op jit(solution)/shard_map/ppermute | solution.py:24
  (73 shorter events, 19.8 us)
Async XLA Ops:
  1.6 9.5 %collective-permute-start.7 = (bf16[64,1792]{1,0:T(8,128)(2,1)S(1)}, bf16[64,1792]{1,0:T(8,128)(2,1)S(1)}, u32[]{:S(2)}, u32[]{:S(2)}) collective-permute-start(bf16[64,1792]{1,0:T(8,128)(2,1)S(1)} %pick_rows.3.refs_0_), channel_id=1, source_target_pairs={{0,16},{16,0},{1,17},{17,1},{2,18},{18,2},{3,19},{19,3},{4,20},{20... | collective-permute-start | bytes 688136 | tf_op jit(solution)/shard_map/ppermute | solution.py:24
  5.6 10.7 %collective-permute-start = (bf16[64,1920]{1,0:T(8,128)(2,1)S(1)}, bf16[64,1920]{1,0:T(8,128)(2,1)S(1)}, u32[]{:S(2)}, u32[]{:S(2)}) collective-permute-start(bf16[64,1920]{1,0:T(8,128)(2,1)S(1)} %pick_rows.4.refs_0_), channel_id=1, source_target_pairs={{0,16},{16,0},{1,17},{17,1},{2,18},{18,2},{3,19},{19,3},{4,20},{20... | collective-permute-start | bytes 737288 | tf_op jit(solution)/shard_map/ppermute | solution.py:24
  6.9 14.3 %collective-permute-start.3 = (bf16[64,1792]{1,0:T(8,128)(2,1)S(1)}, bf16[64,1792]{1,0:T(8,128)(2,1)S(1)}, u32[]{:S(2)}, u32[]{:S(2)}) collective-permute-start(bf16[64,1792]{1,0:T(8,128)(2,1)S(1)} %get-tuple-element.48), channel_id=1, source_target_pairs={{0,16},{16,0},{1,17},{17,1},{2,18},{18,2},{3,19},{19,3},{4,20},{20... | collective-permute-start | bytes 688136 | tf_op jit(solution)/shard_map/ppermute | solution.py:24
  8.8 19.8 %slice-start = ((s8[8716288]{0:T(1024)(128)(4,1)}), s8[4194304]{0:T(1024)(128)(4,1)S(1)}, s32[]{:S(2)}) async-start(s8[8716288]{0:T(1024)(128)(4,1)} %bitcast.4), calls=%async_computation | async-start | bytes 8388608
  8.9 9.7 %copy-start.1 = (s32[512]{0:T(512)S(1)}, s32[512]{0:T(512)}, u32[]{:S(2)}) copy-start(s32[512]{0:T(512)} %param.9) | copy-start | bytes 6148
  8.9 19.8 %slice-start.1 = ((s8[8716288]{0:T(1024)(128)(4,1)}), s8[4194304]{0:T(1024)(128)(4,1)S(1)}, s32[]{:S(2)}) async-start(s8[8716288]{0:T(1024)(128)(4,1)} %bitcast.4), calls=%async_computation.1 | async-start | bytes 8388608
  8.9 19.8 %slice-start.2 = ((s8[8716288]{0:T(1024)(128)(4,1)}), s8[327680]{0:T(1024)(128)(4,1)S(1)}, s32[]{:S(2)}) async-start(s8[8716288]{0:T(1024)(128)(4,1)} %bitcast.4), calls=%async_computation.2 | async-start | bytes 655360
  8.9 16.4 %collective-permute-start.4 = (bf16[64,1792]{1,0:T(8,128)(2,1)S(1)}, bf16[64,1792]{1,0:T(8,128)(2,1)S(1)}, u32[]{:S(2)}, u32[]{:S(2)}) collective-permute-start(bf16[64,1792]{1,0:T(8,128)(2,1)S(1)} %get-tuple-element.49), channel_id=1, source_target_pairs={{0,16},{16,0},{1,17},{17,1},{2,18},{18,2},{3,19},{19,3},{4,20},{20... | collective-permute-start | bytes 688136 | tf_op jit(solution)/shard_map/ppermute | solution.py:24
  11.1 17.6 %collective-permute-start.8 = (bf16[64,1792]{1,0:T(8,128)(2,1)S(1)}, bf16[64,1792]{1,0:T(8,128)(2,1)S(1)}, u32[]{:S(2)}, u32[]{:S(2)}) collective-permute-start(bf16[64,1792]{1,0:T(8,128)(2,1)S(1)} %pass_on.3.refs_1_), channel_id=1, source_target_pairs={{0,1},{1,0},{2,3},{3,2},{4,5},{5,4},{6,7},{7,6},{8,9},{9,8},{10,11... | collective-permute-start | bytes 688136 | tf_op jit(solution)/shard_map/ppermute | solution.py:24
  16.3 12.3 %collective-permute-start.9 = (bf16[64,1792]{1,0:T(8,128)(2,1)S(1)}, bf16[64,1792]{1,0:T(8,128)(2,1)S(1)}, u32[]{:S(2)}, u32[]{:S(2)}) collective-permute-start(bf16[64,1792]{1,0:T(8,128)(2,1)S(1)} %get-tuple-element.50.refs_2_), channel_id=1, source_target_pairs={{0,1},{1,0},{2,3},{3,2},{4,5},{5,4},{6,7},{7,6},{8,9},{9,8},{10,11... | collective-permute-start | bytes 688136 | tf_op jit(solution)/shard_map/ppermute | solution.py:24
  18.7 4.7 %collective-permute-start.1 = (f32[8,128]{1,0:T(8,128)S(1)}, f32[8,128]{1,0:T(8,128)S(1)}, u32[]{:S(2)}, u32[]{:S(2)}) collective-permute-start(f32[8,128]{1,0:T(8,128)S(1)} %count_rows.1.refs_0_), channel_id=1, source_target_pairs={{0,4},{4,0},{8,12},{12,8},{1,5},{5,1},{9,13},{13,9},{2,6},{6,2},{1... | collective-permute-start | bytes 12296 | tf_op jit(solution)/shard_map/ppermute | solution.py:24
  21.2 11.1 %collective-permute-start.5 = (bf16[64,1792]{1,0:T(8,128)(2,1)S(1)}, bf16[64,1792]{1,0:T(8,128)(2,1)S(1)}, u32[]{:S(2)}, u32[]{:S(2)}) collective-permute-start(bf16[64,1792]{1,0:T(8,128)(2,1)S(1)} %collective-permute-done.3.refs_1_), channel_id=1, source_target_pairs={{0,1},{1,0},{2,3},{3,2},{4,5},{5,4},{6,7},{7,6},{8,9},{9,8},{10,11... | collective-permute-start | bytes 688136 | tf_op jit(solution)/shard_map/ppermute | solution.py:24
  25.3 7.2 %collective-permute-start.6 = (bf16[64,1792]{1,0:T(8,128)(2,1)S(1)}, bf16[64,1792]{1,0:T(8,128)(2,1)S(1)}, u32[]{:S(2)}, u32[]{:S(2)}) collective-permute-start(bf16[64,1792]{1,0:T(8,128)(2,1)S(1)} %pass_on.2.refs_0_.refs_2_), channel_id=1, source_target_pairs={{0,1},{1,0},{2,3},{3,2},{4,5},{5,4},{6,7},{7,6},{8,9},{9,8},{10,11... | collective-permute-start | bytes 688136 | tf_op jit(solution)/shard_map/ppermute | solution.py:24
  27.1 5.2 %collective-permute-start.2 = (f32[8,128]{1,0:T(8,128)S(1)}, f32[8,128]{1,0:T(8,128)S(1)}, u32[]{:S(2)}, u32[]{:S(2)}) collective-permute-start(f32[8,128]{1,0:T(8,128)S(1)} %sum_rows.1.refs_0_.refs_6_), channel_id=1, source_target_pairs={{0,8},{4,12},{8,0},{12,4},{1,9},{5,13},{9,1},{13,5},{2,10},{6,14},... | collective-permute-start | bytes 12296 | tf_op jit(solution)/shard_map/ppermute | solution.py:24
  36.1 5.7 %collective-permute-start.12 = (f32[8,512]{1,0:T(8,128)S(1)}, f32[8,512]{1,0:T(8,128)S(1)}, u32[]{:S(2)}, u32[]{:S(2)}) collective-permute-start(f32[8,512]{1,0:T(8,128)S(1)} %get-tuple-element.52.refs_0_.refs_1_), channel_id=1, source_target_pairs={{0,3},{1,2},{2,1},{3,0},{4,7},{5,6},{6,5},{7,4},{8,11},{9,10},{10,... | collective-permute-start | bytes 49160 | tf_op jit(solution)/shard_map/ppermute | solution.py:24
  40.1 4.6 %collective-permute-start.11 = (f32[8,512]{1,0:T(8,128)S(1)}, f32[8,512]{1,0:T(8,128)S(1)}, u32[]{:S(2)}, u32[]{:S(2)}) collective-permute-start(f32[8,512]{1,0:T(8,128)S(1)} %get-tuple-element.52.refs_0_.refs_1_), channel_id=1, source_target_pairs={{0,2},{1,3},{2,0},{3,1},{4,6},{5,7},{6,4},{7,5},{8,10},{9,11},{10,... | collective-permute-start | bytes 49160 | tf_op jit(solution)/shard_map/ppermute | solution.py:24
  40.1 4.6 %collective-permute-start.10 = (f32[8,512]{1,0:T(8,128)S(1)}, f32[8,512]{1,0:T(8,128)S(1)}, u32[]{:S(2)}, u32[]{:S(2)}) collective-permute-start(f32[8,512]{1,0:T(8,128)S(1)} %get-tuple-element.52.refs_0_.refs_1_), channel_id=1, source_target_pairs={{0,1},{1,0},{2,3},{3,2},{4,5},{5,4},{6,7},{7,6},{8,9},{9,8},{10,11... | collective-permute-start | bytes 49160 | tf_op jit(solution)/shard_map/ppermute | solution.py:24
  47.0 3.9 %collective-permute-start.13 = (bf16[896,896]{1,0:T(8,128)(2,1)S(1)}, bf16[896,896]{1,0:T(8,128)(2,1)S(1)}, u32[]{:S(2)}, u32[]{:S(2)}) collective-permute-start(bf16[896,896]{1,0:T(8,128)(2,1)S(1)} %weight_away.3.refs_0_), channel_id=1, source_target_pairs={{0,4},{4,0},{8,12},{12,8},{16,20},{20,16},{24,28},{28,24},{1,5},{5... | collective-permute-start | bytes 4816904 | tf_op jit(solution)/shard_map/ppermute | solution.py:24
  49.3 6.9 %collective-permute-start.14 = (bf16[896,768]{1,0:T(8,128)(2,1)S(1)}, bf16[896,768]{1,0:T(8,128)(2,1)S(1)}, u32[]{:S(2)}, u32[]{:S(2)}) collective-permute-start(bf16[896,768]{1,0:T(8,128)(2,1)S(1)} %weight_away.4.refs_0_), channel_id=1, source_target_pairs={{0,4},{4,0},{8,12},{12,8},{16,20},{20,16},{24,28},{28,24},{1,5},{5... | collective-permute-start | bytes 4128776 | tf_op jit(solution)/shard_map/ppermute | solution.py:24
  50.7 7.0 %collective-permute-start.15 = (bf16[896,768]{1,0:T(8,128)(2,1)S(1)}, bf16[896,768]{1,0:T(8,128)(2,1)S(1)}, u32[]{:S(2)}, u32[]{:S(2)}) collective-permute-start(bf16[896,768]{1,0:T(8,128)(2,1)S(1)} %weight_away.5.refs_0_), channel_id=1, source_target_pairs={{0,4},{4,0},{8,12},{12,8},{16,20},{20,16},{24,28},{28,24},{1,5},{5... | collective-permute-start | bytes 4128776 | tf_op jit(solution)/shard_map/ppermute | solution.py:24
  52.0 12.9 %collective-permute-start.16 = (bf16[448,896]{1,0:T(8,128)(2,1)S(1)}, bf16[448,896]{1,0:T(8,128)(2,1)S(1)}, u32[]{:S(2)}, u32[]{:S(2)}) collective-permute-start(bf16[448,896]{1,0:T(8,128)(2,1)S(1)} %get-tuple-element.67), channel_id=1, source_target_pairs={{0,16},{4,12},{8,24},{12,4},{16,0},{20,28},{24,8},{28,20},{1,17},{... | collective-permute-start | bytes 2408456 | tf_op jit(solution)/shard_map/ppermute | solution.py:24
  56.1 13.4 %collective-permute-start.17 = (bf16[128,1792]{1,0:T(8,128)(2,1)S(1)}, bf16[128,1792]{1,0:T(8,128)(2,1)S(1)}, u32[]{:S(2)}, u32[]{:S(2)}) collective-permute-start(bf16[128,1792]{1,0:T(8,128)(2,1)S(1)} %get-tuple-element.63.refs_0_), channel_id=1, source_target_pairs={{0,1},{1,0},{2,3},{3,2},{4,5},{5,4},{6,7},{7,6},{8,9},{9,8},{10,11... | collective-permute-start | bytes 1376264 | tf_op jit(solution)/shard_map/ppermute | solution.py:24
  57.1 24.4 %collective-permute-start.19 = (bf16[448,768]{1,0:T(8,128)(2,1)S(1)}, bf16[448,768]{1,0:T(8,128)(2,1)S(1)}, u32[]{:S(2)}, u32[]{:S(2)}) collective-permute-start(bf16[448,768]{1,0:T(8,128)(2,1)S(1)} %get-tuple-element.73), channel_id=1, source_target_pairs={{0,16},{4,12},{8,24},{12,4},{16,0},{20,28},{24,8},{28,20},{1,17},{... | collective-permute-start | bytes 2064392 | tf_op jit(solution)/shard_map/ppermute | solution.py:24
  58.6 27.1 %collective-permute-start.21 = (bf16[448,768]{1,0:T(8,128)(2,1)S(1)}, bf16[448,768]{1,0:T(8,128)(2,1)S(1)}, u32[]{:S(2)}, u32[]{:S(2)}) collective-permute-start(bf16[448,768]{1,0:T(8,128)(2,1)S(1)} %get-tuple-element.77), channel_id=1, source_target_pairs={{0,16},{4,12},{8,24},{12,4},{16,0},{20,28},{24,8},{28,20},{1,17},{... | collective-permute-start | bytes 2064392 | tf_op jit(solution)/shard_map/ppermute | solution.py:24
  62.8 20.8 %collective-permute-start.20 = (bf16[128,1792]{1,0:T(8,128)(2,1)S(1)}, bf16[128,1792]{1,0:T(8,128)(2,1)S(1)}, u32[]{:S(2)}, u32[]{:S(2)}) collective-permute-start(bf16[128,1792]{1,0:T(8,128)(2,1)S(1)} %get-tuple-element.66.refs_0_), channel_id=1, source_target_pairs={{0,1},{1,0},{2,3},{3,2},{4,5},{5,4},{6,7},{7,6},{8,9},{9,8},{10,11... | collective-permute-start | bytes 1376264 | tf_op jit(solution)/shard_map/ppermute | solution.py:24
  69.6 11.8 %collective-permute-start.18 = (bf16[64,1792]{1,0:T(8,128)(2,1)S(1)}, bf16[64,1792]{1,0:T(8,128)(2,1)S(1)}, u32[]{:S(2)}, u32[]{:S(2)}) collective-permute-start(bf16[64,1792]{1,0:T(8,128)(2,1)S(1)} %get-tuple-element.71), channel_id=1, source_target_pairs={{0,2},{1,3},{2,0},{3,1},{4,6},{5,7},{6,4},{7,5},{8,10},{9,11},{10,... | collective-permute-start | bytes 688136 | tf_op jit(solution)/shard_map/ppermute | solution.py:24
  71.7 16.4 %collective-permute-start.22 = (bf16[224,896]{1,0:T(8,128)(2,1)S(1)}, bf16[224,896]{1,0:T(8,128)(2,1)S(1)}, u32[]{:S(2)}, u32[]{:S(2)}) collective-permute-start(bf16[224,896]{1,0:T(8,128)(2,1)S(1)} %get-tuple-element.79), channel_id=1, source_target_pairs={{0,8},{4,20},{8,0},{12,28},{16,24},{20,4},{24,16},{28,12},{1,9},{5... | collective-permute-start | bytes 1204232 | tf_op jit(solution)/shard_map/ppermute | solution.py:24
  81.7 7.3 %collective-permute-start.23 = (bf16[224,768]{1,0:T(8,128)(2,1)S(1)}, bf16[224,768]{1,0:T(8,128)(2,1)S(1)}, u32[]{:S(2)}, u32[]{:S(2)}) collective-permute-start(bf16[224,768]{1,0:T(8,128)(2,1)S(1)} %get-tuple-element.82), channel_id=1, source_target_pairs={{0,8},{4,20},{8,0},{12,28},{16,24},{20,4},{24,16},{28,12},{1,9},{5... | collective-permute-start | bytes 1032200 | tf_op jit(solution)/shard_map/ppermute | solution.py:24
  83.7 12.8 %collective-permute-start.24 = (bf16[64,1792]{1,0:T(8,128)(2,1)S(1)}, bf16[64,1792]{1,0:T(8,128)(2,1)S(1)}, u32[]{:S(2)}, u32[]{:S(2)}) collective-permute-start(bf16[64,1792]{1,0:T(8,128)(2,1)S(1)} %get-tuple-element.84), channel_id=1, source_target_pairs={{0,2},{1,3},{2,0},{3,1},{4,6},{5,7},{6,4},{7,5},{8,10},{9,11},{10,... | collective-permute-start | bytes 688136 | tf_op jit(solution)/shard_map/ppermute | solution.py:24
  85.9 13.1 %collective-permute-start.27 = (bf16[224,768]{1,0:T(8,128)(2,1)S(1)}, bf16[224,768]{1,0:T(8,128)(2,1)S(1)}, u32[]{:S(2)}, u32[]{:S(2)}) collective-permute-start(bf16[224,768]{1,0:T(8,128)(2,1)S(1)} %get-tuple-element.88), channel_id=1, source_target_pairs={{0,8},{4,20},{8,0},{12,28},{16,24},{20,4},{24,16},{28,12},{1,9},{5... | collective-permute-start | bytes 1032200 | tf_op jit(solution)/shard_map/ppermute | solution.py:24
  87.5 10.9 %collective-permute-start.25 = (bf16[64,1920]{1,0:T(8,128)(2,1)S(1)}, bf16[64,1920]{1,0:T(8,128)(2,1)S(1)}, u32[]{:S(2)}, u32[]{:S(2)}) collective-permute-start(bf16[64,1920]{1,0:T(8,128)(2,1)S(1)} %pack.1.refs_0_), channel_id=1, source_target_pairs={{0,16},{16,0},{1,17},{17,1},{2,18},{18,2},{3,19},{19,3},{4,20},{20... | collective-permute-start | bytes 737288 | tf_op jit(solution)/shard_map/ppermute | solution.py:24
  96.5 7.1 %collective-permute-start.26 = (bf16[64,1792]{1,0:T(8,128)(2,1)S(1)}, bf16[64,1792]{1,0:T(8,128)(2,1)S(1)}, u32[]{:S(2)}, u32[]{:S(2)}) collective-permute-start(bf16[64,1792]{1,0:T(8,128)(2,1)S(1)} %add.11.refs_0_), channel_id=1, source_target_pairs={{0,16},{16,0},{1,17},{17,1},{2,18},{18,2},{3,19},{19,3},{4,20},{20... | collective-permute-start | bytes 688136 | tf_op jit(solution)/shard_map/ppermute | solution.py:24
  (2 other events, 4.2 us)

commit v5 on v4

--- a/solution.py
+++ b/solution.py
@@ -307,7 +307,7 @@
     for ref in (total, gap, picked):
         ref[...] = jnp.zeros(ref.shape, F32)
     inside = rows // QUARTERS
-    for start, size in tiles(0, width, 2 * LANES):
+    for start, size in tiles(0, width, 4 * LANES):
         tile = jnp.dot(value, weight[:, start : start + size], preferred_element_type=F32)
         logits[:, start : start + size] = tile
         columns = range(start, start + size, LANES)
@@ -424,7 +424,7 @@
         rows, width = slope.shape
         steps = row_steps(2 * rows, group)
 
-        @pl.loop(0, rows // STEP, unroll=2)
+        @pl.loop(0, rows // STEP, unroll=4)
         def _(i):
             here, there = steps(i)
             lse, shift, weight = lses[there, :], shifts[there, :], weights[there, :]

time: 105 us -> 104 us (level)
  no operation moved by 1% of the time
where the time goes in v5:
time: 104 us
  starting transfers between devices  36.8 us (35%)
  waiting for transfers between devices  33.8 us (32%)
  Pallas kernels  31 us (30%)
    ppermute x28, starting transfers between devices, exchange(): return lax.ppermute(array, axes, [(i, partner(i)) for i in range(size)])  36.8 us
    ppermute x28, waiting for transfers between devices, exchange(): return lax.ppermute(array, axes, [(i, partner(i)) for i in range(size)])  33.8 us
    pallas_call x34, Pallas kernels, call(): pl.pallas_call(lambda *refs: kernel(*refs[skip:]), in_specs=[pl.BlockSpec...  31 us
  transfers between devices with their start and end apart: 28, of which 11 were waited for; matrix products, arithmetic and copies ran while one was open for 0% of the time, Pallas kernels for 24%

profile of v5, /device:TPU:0, one launch (start us, length us, event | category | flops | bytes accessed | tf_op | source)
XLA Modules:
  0.0 104.1 jit_solution(8445285124016459080)
XLA Ops:
  1.6 3.0 %collective-permute-start.7 = (bf16[64,1792]{1,0:T(8,128)(2,1)S(1)}, bf16[64,1792]{1,0:T(8,128)(2,1)S(1)}, u32[]{:S(2)}, u32[]{:S(2)}) collective-permute-start(bf16[64,1792]{1,0:T(8,128)(2,1)S(1)} %pick_rows.3.refs_0_), channel_id=1, source_target_pairs={{0,16},{16,0},{1,17},{17,1},{2,18},{18,2},{3,19},{19,3},{4,20},{20... | collective-permute-start | bytes 688136 | tf_op jit(solution)/shard_map/ppermute | solution.py:24
  6.9 1.9 %collective-permute-start.3 = (bf16[64,1792]{1,0:T(8,128)(2,1)S(1)}, bf16[64,1792]{1,0:T(8,128)(2,1)S(1)}, u32[]{:S(2)}, u32[]{:S(2)}) collective-permute-start(bf16[64,1792]{1,0:T(8,128)(2,1)S(1)} %get-tuple-element.48), channel_id=1, source_target_pairs={{0,16},{16,0},{1,17},{17,1},{2,18},{18,2},{3,19},{19,3},{4,20},{20... | collective-permute-start | bytes 688136 | tf_op jit(solution)/shard_map/ppermute | solution.py:24
  9.1 1.9 %teacher_stats.1.refs_0_.refs_8_ = f32[8,512]{1,0:T(8,128)S(1)} custom-call(bf16[64,1920]{1,0:T(8,128)(2,1)S(1)} %pick_rows.4.refs_0_, bf16[512,2432]{1,0:T(8,128)(2,1)S(1)} %copy-done), custom_call_target="tpu_custom_call" | custom-call | flops 20000000000 | bytes 1024 | tf_op jit(solution)/shard_map/teacher_stats/pallas_call | solution.py:39
  11.1 2.1 %collective-permute-start.8 = (bf16[64,1792]{1,0:T(8,128)(2,1)S(1)}, bf16[64,1792]{1,0:T(8,128)(2,1)S(1)}, u32[]{:S(2)}, u32[]{:S(2)}) collective-permute-start(bf16[64,1792]{1,0:T(8,128)(2,1)S(1)} %pass_on.3.refs_1_), channel_id=1, source_target_pairs={{0,1},{1,0},{2,3},{3,2},{4,5},{5,4},{6,7},{7,6},{8,9},{9,8},{10,11... | collective-permute-start | bytes 688136 | tf_op jit(solution)/shard_map/ppermute | solution.py:24
  13.2 3.1 %collective-permute-done.refs_0_ = bf16[64,1920]{1,0:T(8,128)(2,1)S(1)} collective-permute-done((bf16[64,1920]{1,0:T(8,128)(2,1)S(1)}, bf16[64,1920]{1,0:T(8,128)(2,1)S(1)}, u32[]{:S(2)}, u32[]{:S(2)}) %collective-permute-start) | collective-permute-done | bytes 245792 | tf_op jit(solution)/shard_map/ppermute | solution.py:24
  16.3 2.2 %collective-permute-start.9 = (bf16[64,1792]{1,0:T(8,128)(2,1)S(1)}, bf16[64,1792]{1,0:T(8,128)(2,1)S(1)}, u32[]{:S(2)}, u32[]{:S(2)}) collective-permute-start(bf16[64,1792]{1,0:T(8,128)(2,1)S(1)} %get-tuple-element.50.refs_2_), channel_id=1, source_target_pairs={{0,1},{1,0},{2,3},{3,2},{4,5},{5,4},{6,7},{7,6},{8,9},{9,8},{10,11... | collective-permute-start | bytes 688136 | tf_op jit(solution)/shard_map/ppermute | solution.py:24
  18.7 2.5 %collective-permute-done.3.refs_1_ = bf16[64,1792]{1,0:T(8,128)(2,1)S(1)} collective-permute-done((bf16[64,1792]{1,0:T(8,128)(2,1)S(1)}, bf16[64,1792]{1,0:T(8,128)(2,1)S(1)}, u32[]{:S(2)}, u32[]{:S(2)}) %collective-permute-start.3) | collective-permute-done | bytes 229408 | tf_op jit(solution)/shard_map/ppermute | solution.py:24
  21.2 2.1 %collective-permute-start.5 = (bf16[64,1792]{1,0:T(8,128)(2,1)S(1)}, bf16[64,1792]{1,0:T(8,128)(2,1)S(1)}, u32[]{:S(2)}, u32[]{:S(2)}) collective-permute-start(bf16[64,1792]{1,0:T(8,128)(2,1)S(1)} %collective-permute-done.3.refs_1_), channel_id=1, source_target_pairs={{0,1},{1,0},{2,3},{3,2},{4,5},{5,4},{6,7},{7,6},{8,9},{9,8},{10,11... | collective-permute-start | bytes 688136 | tf_op jit(solution)/shard_map/ppermute | solution.py:24
  23.4 1.9 %collective-permute-done.4.refs_1_ = bf16[64,1792]{1,0:T(8,128)(2,1)S(1)} collective-permute-done((bf16[64,1792]{1,0:T(8,128)(2,1)S(1)}, bf16[64,1792]{1,0:T(8,128)(2,1)S(1)}, u32[]{:S(2)}, u32[]{:S(2)}) %collective-permute-start.4) | collective-permute-done | bytes 229408 | tf_op jit(solution)/shard_map/ppermute | solution.py:24
  25.3 1.8 %collective-permute-start.6 = (bf16[64,1792]{1,0:T(8,128)(2,1)S(1)}, bf16[64,1792]{1,0:T(8,128)(2,1)S(1)}, u32[]{:S(2)}, u32[]{:S(2)}) collective-permute-start(bf16[64,1792]{1,0:T(8,128)(2,1)S(1)} %pass_on.2.refs_0_.refs_2_), channel_id=1, source_target_pairs={{0,1},{1,0},{2,3},{3,2},{4,5},{5,4},{6,7},{7,6},{8,9},{9,8},{10,11... | collective-permute-start | bytes 688136 | tf_op jit(solution)/shard_map/ppermute | solution.py:24
  27.1 1.5 %collective-permute-start.2 = (f32[8,128]{1,0:T(8,128)S(1)}, f32[8,128]{1,0:T(8,128)S(1)}, u32[]{:S(2)}, u32[]{:S(2)}) collective-permute-start(f32[8,128]{1,0:T(8,128)S(1)} %sum_rows.1.refs_0_.refs_6_), channel_id=1, source_target_pairs={{0,8},{4,12},{8,0},{12,4},{1,9},{5,13},{9,1},{13,5},{2,10},{6,14},... | collective-permute-start | bytes 12296 | tf_op jit(solution)/shard_map/ppermute | solution.py:24
  28.7 3.5 %group_logits.2 = (f32[256,2432]{1,0:T(8,128)S(1)}, f32[8,512]{1,0:T(8,128)S(1)}) custom-call(bf16[64,1792]{1,0:T(8,128)(2,1)S(1)} %pass_on.2.refs_0_.refs_2_, bf16[64,1792]{1,0:T(8,128)(2,1)S(1)} %pass_on.3.refs_1_, bf16[64,1792]{1,0:T(8,128)(2,1)S(1)} %get-tuple-element.50.refs_2_, bf16[64,1792]{1,0:T(8,128)(2,1)S(1)} %collective-permute-done.8.refs_3_, ...), custom_call_target="tpu_custom_call" | custom-call | flops 2000000000 | bytes 1024 | tf_op jit(solution)/shard_map/group_logits/pallas_call | solution.py:39
  32.5 3.4 %group_logits.3 = (f32[256,2432]{1,0:T(8,128)S(1)}, f32[8,512]{1,0:T(8,128)S(1)}) custom-call(f32[8,128]{1,0:T(8,128)S(1)} %collective-permute-done.2.refs_0_.refs_7_, bf16[64,1792]{1,0:T(8,128)(2,1)S(1)} %collective-permute-done.3.refs_1_, bf16[64,1792]{1,0:T(8,128)(2,1)S(1)} %pass_on.2.refs_0_.refs_2_, ...), custom_call_target="tpu_custom_call" | custom-call | flops 20000000000 | bytes 1024 | tf_op jit(solution)/shard_map/group_logits/pallas_call | solution.py:39
  35.9 4.0 %collective-permute-start.12 = (f32[8,512]{1,0:T(8,128)S(1)}, f32[8,512]{1,0:T(8,128)S(1)}, u32[]{:S(2)}, u32[]{:S(2)}) collective-permute-start(f32[8,512]{1,0:T(8,128)S(1)} %get-tuple-element.52.refs_0_.refs_1_), channel_id=1, source_target_pairs={{0,3},{1,2},{2,1},{3,0},{4,7},{5,6},{6,5},{7,4},{8,11},{9,10},{10,... | collective-permute-start | bytes 49160 | tf_op jit(solution)/shard_map/ppermute | solution.py:24
  41.6 2.9 %collective-permute-done.11.refs_3_ = f32[8,512]{1,0:T(8,128)S(1)} collective-permute-done((f32[8,512]{1,0:T(8,128)S(1)}, f32[8,512]{1,0:T(8,128)S(1)}, u32[]{:S(2)}, u32[]{:S(2)}) %collective-permute-start.11) | collective-permute-done | bytes 16416 | tf_op jit(solution)/shard_map/ppermute | solution.py:24
  46.8 1.3 %slopes.3 = (bf16[256,1536]{1,0:T(8,128)(2,1)S(1)}, bf16[256,1536]{1,0:T(8,128)(2,1)S(1)}) custom-call(bf16[896,896]{1,0:T(8,128)(2,1)S(1)} %weight_away.3.refs_0_, f32[512,128]{1,0:T(8,128)S(1)} %get-tuple-element.57.refs_1_, f32[512,128]{1,0:T(8,128)S(1)} %get-tuple-element.58.refs_2_, f32[512,128]{1,0:T(8,128)S(1)} %get-tuple-element.59.refs_3_, ...), custom_call_target="tpu_custom_call" | custom-call | flops 1024 | bytes 1024 | tf_op jit(solution)/shard_map/slopes/pallas_call | solution.py:39
  51.7 1.6 %collective-permute-start.16 = (bf16[448,896]{1,0:T(8,128)(2,1)S(1)}, bf16[448,896]{1,0:T(8,128)(2,1)S(1)}, u32[]{:S(2)}, u32[]{:S(2)}) collective-permute-start(bf16[448,896]{1,0:T(8,128)(2,1)S(1)} %get-tuple-element.67), channel_id=1, source_target_pairs={{0,16},{4,12},{8,24},{12,4},{16,0},{20,28},{24,8},{28,20},{1,17},{... | collective-permute-start | bytes 2408456 | tf_op jit(solution)/shard_map/ppermute | solution.py:24
  53.2 2.6 %hidden_grad.2 = (bf16[128,1792]{1,0:T(8,128)(2,1)S(1)}, f32[128,1792]{1,0:T(8,128)S(1)}) custom-call(bf16[448,896]{1,0:T(8,128)(2,1)S(1)} %get-tuple-element.62.refs_0_.refs_1_, bf16[256,896]{1,0:T(8,128)(2,1)S(1)} %get-tuple-element.56.refs_3_.refs_1_, bf16[256,1536]{1,0:T(8,128)(2,1)S(1)} %get-tuple-element.61.refs_3_.refs_2_, bf16[1792,2432]{1,0:T(8,128)(2,1)S(1)} %bitcast.5), custom_call_target="tpu_custom_call" | custom-call | flops 1024 | bytes 1024 | tf_op jit(solution)/shard_map/hidden_grad/pallas_call | solution.py:39
  58.3 1.6 %collective-permute-start.21 = (bf16[448,768]{1,0:T(8,128)(2,1)S(1)}, bf16[448,768]{1,0:T(8,128)(2,1)S(1)}, u32[]{:S(2)}, u32[]{:S(2)}) collective-permute-start(bf16[448,768]{1,0:T(8,128)(2,1)S(1)} %get-tuple-element.77), channel_id=1, source_target_pairs={{0,16},{4,12},{8,24},{12,4},{16,0},{20,28},{24,8},{28,20},{1,17},{... | collective-permute-start | bytes 2064392 | tf_op jit(solution)/shard_map/ppermute | solution.py:24
  59.9 2.6 %hidden_grad.3 = (bf16[128,1792]{1,0:T(8,128)(2,1)S(1)}, f32[128,1792]{1,0:T(8,128)S(1)}) custom-call(bf16[448,768]{1,0:T(8,128)(2,1)S(1)} %get-tuple-element.65.refs_0_.refs_1_, bf16[256,896]{1,0:T(8,128)(2,1)S(1)} %get-tuple-element.55.refs_0_.refs_4_.refs_1_, bf16[256,1536]{1,0:T(8,128)(2,1)S(1)} %get-tuple-element.60.refs_0_.refs_4_.refs_2_, ...), custom_call_target="tpu_custom_call" | custom-call | flops 1024 | bytes 1024 | tf_op jit(solution)/shard_map/hidden_grad/pallas_call | solution.py:39
  62.5 2.1 %collective-permute-start.20 = (bf16[128,1792]{1,0:T(8,128)(2,1)S(1)}, bf16[128,1792]{1,0:T(8,128)(2,1)S(1)}, u32[]{:S(2)}, u32[]{:S(2)}) collective-permute-start(bf16[128,1792]{1,0:T(8,128)(2,1)S(1)} %get-tuple-element.66.refs_0_), channel_id=1, source_target_pairs={{0,1},{1,0},{2,3},{3,2},{4,5},{5,4},{6,7},{7,6},{8,9},{9,8},{10,11... | collective-permute-start | bytes 1376264 | tf_op jit(solution)/shard_map/ppermute | solution.py:24
  64.8 4.5 %collective-permute-done.17.refs_2_ = bf16[128,1792]{1,0:T(8,128)(2,1)S(1)} collective-permute-done((bf16[128,1792]{1,0:T(8,128)(2,1)S(1)}, bf16[128,1792]{1,0:T(8,128)(2,1)S(1)}, u32[]{:S(2)}, u32[]{:S(2)}) %collective-permute-start.17) | collective-permute-done | bytes 458784 | tf_op jit(solution)/shard_map/ppermute | solution.py:24
  69.3 2.1 %collective-permute-start.18 = (bf16[64,1792]{1,0:T(8,128)(2,1)S(1)}, bf16[64,1792]{1,0:T(8,128)(2,1)S(1)}, u32[]{:S(2)}, u32[]{:S(2)}) collective-permute-start(bf16[64,1792]{1,0:T(8,128)(2,1)S(1)} %get-tuple-element.71), channel_id=1, source_target_pairs={{0,2},{1,3},{2,0},{3,1},{4,6},{5,7},{6,4},{7,5},{8,10},{9,11},{10,... | collective-permute-start | bytes 688136 | tf_op jit(solution)/shard_map/ppermute | solution.py:24
  71.4 1.6 %collective-permute-start.22 = (bf16[224,896]{1,0:T(8,128)(2,1)S(1)}, bf16[224,896]{1,0:T(8,128)(2,1)S(1)}, u32[]{:S(2)}, u32[]{:S(2)}) collective-permute-start(bf16[224,896]{1,0:T(8,128)(2,1)S(1)} %get-tuple-element.79), channel_id=1, source_target_pairs={{0,8},{4,20},{8,0},{12,28},{16,24},{20,4},{24,16},{28,12},{1,9},{5... | collective-permute-start | bytes 1204232 | tf_op jit(solution)/shard_map/ppermute | solution.py:24
  73.0 8.1 %collective-permute-done.18.refs_2_ = bf16[64,1792]{1,0:T(8,128)(2,1)S(1)} collective-permute-done((bf16[64,1792]{1,0:T(8,128)(2,1)S(1)}, bf16[64,1792]{1,0:T(8,128)(2,1)S(1)}, u32[]{:S(2)}, u32[]{:S(2)}) %collective-permute-start.18) | collective-permute-done | bytes 229408 | tf_op jit(solution)/shard_map/ppermute | solution.py:24
  81.9 1.4 %collective-permute-done.20.refs_2_ = bf16[128,1792]{1,0:T(8,128)(2,1)S(1)} collective-permute-done((bf16[128,1792]{1,0:T(8,128)(2,1)S(1)}, bf16[128,1792]{1,0:T(8,128)(2,1)S(1)}, u32[]{:S(2)}, u32[]{:S(2)}) %collective-permute-start.20) | collective-permute-done | bytes 458784 | tf_op jit(solution)/shard_map/ppermute | solution.py:24
  83.4 2.1 %collective-permute-start.24 = (bf16[64,1792]{1,0:T(8,128)(2,1)S(1)}, bf16[64,1792]{1,0:T(8,128)(2,1)S(1)}, u32[]{:S(2)}, u32[]{:S(2)}) collective-permute-start(bf16[64,1792]{1,0:T(8,128)(2,1)S(1)} %get-tuple-element.84), channel_id=1, source_target_pairs={{0,2},{1,3},{2,0},{3,1},{4,6},{5,7},{6,4},{7,5},{8,10},{9,11},{10,... | collective-permute-start | bytes 688136 | tf_op jit(solution)/shard_map/ppermute | solution.py:24
  85.6 1.6 %collective-permute-start.27 = (bf16[224,768]{1,0:T(8,128)(2,1)S(1)}, bf16[224,768]{1,0:T(8,128)(2,1)S(1)}, u32[]{:S(2)}, u32[]{:S(2)}) collective-permute-start(bf16[224,768]{1,0:T(8,128)(2,1)S(1)} %get-tuple-element.88), channel_id=1, source_target_pairs={{0,8},{4,20},{8,0},{12,28},{16,24},{20,4},{24,16},{28,12},{1,9},{5... | collective-permute-start | bytes 1032200 | tf_op jit(solution)/shard_map/ppermute | solution.py:24
  89.6 6.6 %collective-permute-done.24.refs_2_ = bf16[64,1792]{1,0:T(8,128)(2,1)S(1)} collective-permute-done((bf16[64,1792]{1,0:T(8,128)(2,1)S(1)}, bf16[64,1792]{1,0:T(8,128)(2,1)S(1)}, u32[]{:S(2)}, u32[]{:S(2)}) %collective-permute-start.24) | collective-permute-done | bytes 229408 | tf_op jit(solution)/shard_map/ppermute | solution.py:24
  96.2 1.9 %collective-permute-start.26 = (bf16[64,1792]{1,0:T(8,128)(2,1)S(1)}, bf16[64,1792]{1,0:T(8,128)(2,1)S(1)}, u32[]{:S(2)}, u32[]{:S(2)}) collective-permute-start(bf16[64,1792]{1,0:T(8,128)(2,1)S(1)} %add.11.refs_0_), channel_id=1, source_target_pairs={{0,16},{16,0},{1,17},{17,1},{2,18},{18,2},{3,19},{19,3},{4,20},{20... | collective-permute-start | bytes 688136 | tf_op jit(solution)/shard_map/ppermute | solution.py:24
  99.4 1.5 %finish.5 = (bf16[224,2432]{1,0:T(8,128)(2,1)}, f32[8,128]{1,0:T(8,128)}) custom-call(f32[1,512]{1,0:T(1,128)S(1)} %copy-done.2, bf16[224,2432]{1,0:T(8,128)(2,1)} %get-tuple-element.87.refs_1_, bf16[224,768]{1,0:T(8,128)(2,1)S(1)} %get-tuple-element.78.refs_0_.refs_2_, ...), custom_call_target="tpu_custom_call", output_to_operand_aliasing={{0}: (1, {})} | custom-call | flops 1024 | bytes 1024 | tf_op jit(solution)/shard_map/finish/pallas_call | solution.py:39
  100.9 2.4 %collective-permute-done.26 = bf16[64,1792]{1,0:T(8,128)(2,1)S(1)} collective-permute-done((bf16[64,1792]{1,0:T(8,128)(2,1)S(1)}, bf16[64,1792]{1,0:T(8,128)(2,1)S(1)}, u32[]{:S(2)}, u32[]{:S(2)}) %collective-permute-start.26) | collective-permute-done | bytes 229408 | tf_op jit(solution)/shard_map/ppermute | solution.py:24
  (73 shorter events, 19.8 us)
Async XLA Ops:
  1.6 9.5 %collective-permute-start.7 = (bf16[64,1792]{1,0:T(8,128)(2,1)S(1)}, bf16[64,1792]{1,0:T(8,128)(2,1)S(1)}, u32[]{:S(2)}, u32[]{:S(2)}) collective-permute-start(bf16[64,1792]{1,0:T(8,128)(2,1)S(1)} %pick_rows.3.refs_0_), channel_id=1, source_target_pairs={{0,16},{16,0},{1,17},{17,1},{2,18},{18,2},{3,19},{19,3},{4,20},{20... | collective-permute-start | bytes 688136 | tf_op jit(solution)/shard_map/ppermute | solution.py:24
  5.6 10.7 %collective-permute-start = (bf16[64,1920]{1,0:T(8,128)(2,1)S(1)}, bf16[64,1920]{1,0:T(8,128)(2,1)S(1)}, u32[]{:S(2)}, u32[]{:S(2)}) collective-permute-start(bf16[64,1920]{1,0:T(8,128)(2,1)S(1)} %pick_rows.4.refs_0_), channel_id=1, source_target_pairs={{0,16},{16,0},{1,17},{17,1},{2,18},{18,2},{3,19},{19,3},{4,20},{20... | collective-permute-start | bytes 737288 | tf_op jit(solution)/shard_map/ppermute | solution.py:24
  6.9 14.3 %collective-permute-start.3 = (bf16[64,1792]{1,0:T(8,128)(2,1)S(1)}, bf16[64,1792]{1,0:T(8,128)(2,1)S(1)}, u32[]{:S(2)}, u32[]{:S(2)}) collective-permute-start(bf16[64,1792]{1,0:T(8,128)(2,1)S(1)} %get-tuple-element.48), channel_id=1, source_target_pairs={{0,16},{16,0},{1,17},{17,1},{2,18},{18,2},{3,19},{19,3},{4,20},{20... | collective-permute-start | bytes 688136 | tf_op jit(solution)/shard_map/ppermute | solution.py:24
  8.8 19.8 %slice-start = ((s8[8716288]{0:T(1024)(128)(4,1)}), s8[4194304]{0:T(1024)(128)(4,1)S(1)}, s32[]{:S(2)}) async-start(s8[8716288]{0:T(1024)(128)(4,1)} %bitcast.4), calls=%async_computation | async-start | bytes 8388608
  8.9 9.7 %copy-start.1 = (s32[512]{0:T(512)S(1)}, s32[512]{0:T(512)}, u32[]{:S(2)}) copy-start(s32[512]{0:T(512)} %param.9) | copy-start | bytes 6148
  8.9 19.8 %slice-start.1 = ((s8[8716288]{0:T(1024)(128)(4,1)}), s8[4194304]{0:T(1024)(128)(4,1)S(1)}, s32[]{:S(2)}) async-start(s8[8716288]{0:T(1024)(128)(4,1)} %bitcast.4), calls=%async_computation.1 | async-start | bytes 8388608
  8.9 19.8 %slice-start.2 = ((s8[8716288]{0:T(1024)(128)(4,1)}), s8[327680]{0:T(1024)(128)(4,1)S(1)}, s32[]{:S(2)}) async-start(s8[8716288]{0:T(1024)(128)(4,1)} %bitcast.4), calls=%async_computation.2 | async-start | bytes 655360
  8.9 16.4 %collective-permute-start.4 = (bf16[64,1792]{1,0:T(8,128)(2,1)S(1)}, bf16[64,1792]{1,0:T(8,128)(2,1)S(1)}, u32[]{:S(2)}, u32[]{:S(2)}) collective-permute-start(bf16[64,1792]{1,0:T(8,128)(2,1)S(1)} %get-tuple-element.49), channel_id=1, source_target_pairs={{0,16},{16,0},{1,17},{17,1},{2,18},{18,2},{3,19},{19,3},{4,20},{20... | collective-permute-start | bytes 688136 | tf_op jit(solution)/shard_map/ppermute | solution.py:24
  11.1 17.6 %collective-permute-start.8 = (bf16[64,1792]{1,0:T(8,128)(2,1)S(1)}, bf16[64,1792]{1,0:T(8,128)(2,1)S(1)}, u32[]{:S(2)}, u32[]{:S(2)}) collective-permute-start(bf16[64,1792]{1,0:T(8,128)(2,1)S(1)} %pass_on.3.refs_1_), channel_id=1, source_target_pairs={{0,1},{1,0},{2,3},{3,2},{4,5},{5,4},{6,7},{7,6},{8,9},{9,8},{10,11... | collective-permute-start | bytes 688136 | tf_op jit(solution)/shard_map/ppermute | solution.py:24
  16.3 12.3 %collective-permute-start.9 = (bf16[64,1792]{1,0:T(8,128)(2,1)S(1)}, bf16[64,1792]{1,0:T(8,128)(2,1)S(1)}, u32[]{:S(2)}, u32[]{:S(2)}) collective-permute-start(bf16[64,1792]{1,0:T(8,128)(2,1)S(1)} %get-tuple-element.50.refs_2_), channel_id=1, source_target_pairs={{0,1},{1,0},{2,3},{3,2},{4,5},{5,4},{6,7},{7,6},{8,9},{9,8},{10,11... | collective-permute-start | bytes 688136 | tf_op jit(solution)/shard_map/ppermute | solution.py:24
  18.7 4.7 %collective-permute-start.1 = (f32[8,128]{1,0:T(8,128)S(1)}, f32[8,128]{1,0:T(8,128)S(1)}, u32[]{:S(2)}, u32[]{:S(2)}) collective-permute-start(f32[8,128]{1,0:T(8,128)S(1)} %count_rows.1.refs_0_), channel_id=1, source_target_pairs={{0,4},{4,0},{8,12},{12,8},{1,5},{5,1},{9,13},{13,9},{2,6},{6,2},{1... | collective-permute-start | bytes 12296 | tf_op jit(solution)/shard_map/ppermute | solution.py:24
  21.2 10.9 %collective-permute-start.5 = (bf16[64,1792]{1,0:T(8,128)(2,1)S(1)}, bf16[64,1792]{1,0:T(8,128)(2,1)S(1)}, u32[]{:S(2)}, u32[]{:S(2)}) collective-permute-start(bf16[64,1792]{1,0:T(8,128)(2,1)S(1)} %collective-permute-done.3.refs_1_), channel_id=1, source_target_pairs={{0,1},{1,0},{2,3},{3,2},{4,5},{5,4},{6,7},{7,6},{8,9},{9,8},{10,11... | collective-permute-start | bytes 688136 | tf_op jit(solution)/shard_map/ppermute | solution.py:24
  25.3 7.2 %collective-permute-start.6 = (bf16[64,1792]{1,0:T(8,128)(2,1)S(1)}, bf16[64,1792]{1,0:T(8,128)(2,1)S(1)}, u32[]{:S(2)}, u32[]{:S(2)}) collective-permute-start(bf16[64,1792]{1,0:T(8,128)(2,1)S(1)} %pass_on.2.refs_0_.refs_2_), channel_id=1, source_target_pairs={{0,1},{1,0},{2,3},{3,2},{4,5},{5,4},{6,7},{7,6},{8,9},{9,8},{10,11... | collective-permute-start | bytes 688136 | tf_op jit(solution)/shard_map/ppermute | solution.py:24
  27.1 5.0 %collective-permute-start.2 = (f32[8,128]{1,0:T(8,128)S(1)}, f32[8,128]{1,0:T(8,128)S(1)}, u32[]{:S(2)}, u32[]{:S(2)}) collective-permute-start(f32[8,128]{1,0:T(8,128)S(1)} %sum_rows.1.refs_0_.refs_6_), channel_id=1, source_target_pairs={{0,8},{4,12},{8,0},{12,4},{1,9},{5,13},{9,1},{13,5},{2,10},{6,14},... | collective-permute-start | bytes 12296 | tf_op jit(solution)/shard_map/ppermute | solution.py:24
  35.9 5.7 %collective-permute-start.12 = (f32[8,512]{1,0:T(8,128)S(1)}, f32[8,512]{1,0:T(8,128)S(1)}, u32[]{:S(2)}, u32[]{:S(2)}) collective-permute-start(f32[8,512]{1,0:T(8,128)S(1)} %get-tuple-element.52.refs_0_.refs_1_), channel_id=1, source_target_pairs={{0,3},{1,2},{2,1},{3,0},{4,7},{5,6},{6,5},{7,4},{8,11},{9,10},{10,... | collective-permute-start | bytes 49160 | tf_op jit(solution)/shard_map/ppermute | solution.py:24
  39.9 4.6 %collective-permute-start.11 = (f32[8,512]{1,0:T(8,128)S(1)}, f32[8,512]{1,0:T(8,128)S(1)}, u32[]{:S(2)}, u32[]{:S(2)}) collective-permute-start(f32[8,512]{1,0:T(8,128)S(1)} %get-tuple-element.52.refs_0_.refs_1_), channel_id=1, source_target_pairs={{0,2},{1,3},{2,0},{3,1},{4,6},{5,7},{6,4},{7,5},{8,10},{9,11},{10,... | collective-permute-start | bytes 49160 | tf_op jit(solution)/shard_map/ppermute | solution.py:24
  39.9 4.6 %collective-permute-start.10 = (f32[8,512]{1,0:T(8,128)S(1)}, f32[8,512]{1,0:T(8,128)S(1)}, u32[]{:S(2)}, u32[]{:S(2)}) collective-permute-start(f32[8,512]{1,0:T(8,128)S(1)} %get-tuple-element.52.refs_0_.refs_1_), channel_id=1, source_target_pairs={{0,1},{1,0},{2,3},{3,2},{4,5},{5,4},{6,7},{7,6},{8,9},{9,8},{10,11... | collective-permute-start | bytes 49160 | tf_op jit(solution)/shard_map/ppermute | solution.py:24
  46.7 3.8 %collective-permute-start.13 = (bf16[896,896]{1,0:T(8,128)(2,1)S(1)}, bf16[896,896]{1,0:T(8,128)(2,1)S(1)}, u32[]{:S(2)}, u32[]{:S(2)}) collective-permute-start(bf16[896,896]{1,0:T(8,128)(2,1)S(1)} %weight_away.3.refs_0_), channel_id=1, source_target_pairs={{0,4},{4,0},{8,12},{12,8},{16,20},{20,16},{24,28},{28,24},{1,5},{5... | collective-permute-start | bytes 4816904 | tf_op jit(solution)/shard_map/ppermute | solution.py:24
  49.0 6.9 %collective-permute-start.14 = (bf16[896,768]{1,0:T(8,128)(2,1)S(1)}, bf16[896,768]{1,0:T(8,128)(2,1)S(1)}, u32[]{:S(2)}, u32[]{:S(2)}) collective-permute-start(bf16[896,768]{1,0:T(8,128)(2,1)S(1)} %weight_away.4.refs_0_), channel_id=1, source_target_pairs={{0,4},{4,0},{8,12},{12,8},{16,20},{20,16},{24,28},{28,24},{1,5},{5... | collective-permute-start | bytes 4128776 | tf_op jit(solution)/shard_map/ppermute | solution.py:24
  50.4 7.0 %collective-permute-start.15 = (bf16[896,768]{1,0:T(8,128)(2,1)S(1)}, bf16[896,768]{1,0:T(8,128)(2,1)S(1)}, u32[]{:S(2)}, u32[]{:S(2)}) collective-permute-start(bf16[896,768]{1,0:T(8,128)(2,1)S(1)} %weight_away.5.refs_0_), channel_id=1, source_target_pairs={{0,4},{4,0},{8,12},{12,8},{16,20},{20,16},{24,28},{28,24},{1,5},{5... | collective-permute-start | bytes 4128776 | tf_op jit(solution)/shard_map/ppermute | solution.py:24
  51.7 12.9 %collective-permute-start.16 = (bf16[448,896]{1,0:T(8,128)(2,1)S(1)}, bf16[448,896]{1,0:T(8,128)(2,1)S(1)}, u32[]{:S(2)}, u32[]{:S(2)}) collective-permute-start(bf16[448,896]{1,0:T(8,128)(2,1)S(1)} %get-tuple-element.67), channel_id=1, source_target_pairs={{0,16},{4,12},{8,24},{12,4},{16,0},{20,28},{24,8},{28,20},{1,17},{... | collective-permute-start | bytes 2408456 | tf_op jit(solution)/shard_map/ppermute | solution.py:24
  55.8 13.4 %collective-permute-start.17 = (bf16[128,1792]{1,0:T(8,128)(2,1)S(1)}, bf16[128,1792]{1,0:T(8,128)(2,1)S(1)}, u32[]{:S(2)}, u32[]{:S(2)}) collective-permute-start(bf16[128,1792]{1,0:T(8,128)(2,1)S(1)} %get-tuple-element.63.refs_0_), channel_id=1, source_target_pairs={{0,1},{1,0},{2,3},{3,2},{4,5},{5,4},{6,7},{7,6},{8,9},{9,8},{10,11... | collective-permute-start | bytes 1376264 | tf_op jit(solution)/shard_map/ppermute | solution.py:24
  56.8 24.3 %collective-permute-start.19 = (bf16[448,768]{1,0:T(8,128)(2,1)S(1)}, bf16[448,768]{1,0:T(8,128)(2,1)S(1)}, u32[]{:S(2)}, u32[]{:S(2)}) collective-permute-start(bf16[448,768]{1,0:T(8,128)(2,1)S(1)} %get-tuple-element.73), channel_id=1, source_target_pairs={{0,16},{4,12},{8,24},{12,4},{16,0},{20,28},{24,8},{28,20},{1,17},{... | collective-permute-start | bytes 2064392 | tf_op jit(solution)/shard_map/ppermute | solution.py:24
  58.3 27.1 %collective-permute-start.21 = (bf16[448,768]{1,0:T(8,128)(2,1)S(1)}, bf16[448,768]{1,0:T(8,128)(2,1)S(1)}, u32[]{:S(2)}, u32[]{:S(2)}) collective-permute-start(bf16[448,768]{1,0:T(8,128)(2,1)S(1)} %get-tuple-element.77), channel_id=1, source_target_pairs={{0,16},{4,12},{8,24},{12,4},{16,0},{20,28},{24,8},{28,20},{1,17},{... | collective-permute-start | bytes 2064392 | tf_op jit(solution)/shard_map/ppermute | solution.py:24
  62.5 20.8 %collective-permute-start.20 = (bf16[128,1792]{1,0:T(8,128)(2,1)S(1)}, bf16[128,1792]{1,0:T(8,128)(2,1)S(1)}, u32[]{:S(2)}, u32[]{:S(2)}) collective-permute-start(bf16[128,1792]{1,0:T(8,128)(2,1)S(1)} %get-tuple-element.66.refs_0_), channel_id=1, source_target_pairs={{0,1},{1,0},{2,3},{3,2},{4,5},{5,4},{6,7},{7,6},{8,9},{9,8},{10,11... | collective-permute-start | bytes 1376264 | tf_op jit(solution)/shard_map/ppermute | solution.py:24
  69.3 11.8 %collective-permute-start.18 = (bf16[64,1792]{1,0:T(8,128)(2,1)S(1)}, bf16[64,1792]{1,0:T(8,128)(2,1)S(1)}, u32[]{:S(2)}, u32[]{:S(2)}) collective-permute-start(bf16[64,1792]{1,0:T(8,128)(2,1)S(1)} %get-tuple-element.71), channel_id=1, source_target_pairs={{0,2},{1,3},{2,0},{3,1},{4,6},{5,7},{6,4},{7,5},{8,10},{9,11},{10,... | collective-permute-start | bytes 688136 | tf_op jit(solution)/shard_map/ppermute | solution.py:24
  71.4 16.4 %collective-permute-start.22 = (bf16[224,896]{1,0:T(8,128)(2,1)S(1)}, bf16[224,896]{1,0:T(8,128)(2,1)S(1)}, u32[]{:S(2)}, u32[]{:S(2)}) collective-permute-start(bf16[224,896]{1,0:T(8,128)(2,1)S(1)} %get-tuple-element.79), channel_id=1, source_target_pairs={{0,8},{4,20},{8,0},{12,28},{16,24},{20,4},{24,16},{28,12},{1,9},{5... | collective-permute-start | bytes 1204232 | tf_op jit(solution)/shard_map/ppermute | solution.py:24
  81.3 7.3 %collective-permute-start.23 = (bf16[224,768]{1,0:T(8,128)(2,1)S(1)}, bf16[224,768]{1,0:T(8,128)(2,1)S(1)}, u32[]{:S(2)}, u32[]{:S(2)}) collective-permute-start(bf16[224,768]{1,0:T(8,128)(2,1)S(1)} %get-tuple-element.82), channel_id=1, source_target_pairs={{0,8},{4,20},{8,0},{12,28},{16,24},{20,4},{24,16},{28,12},{1,9},{5... | collective-permute-start | bytes 1032200 | tf_op jit(solution)/shard_map/ppermute | solution.py:24
  83.4 12.8 %collective-permute-start.24 = (bf16[64,1792]{1,0:T(8,128)(2,1)S(1)}, bf16[64,1792]{1,0:T(8,128)(2,1)S(1)}, u32[]{:S(2)}, u32[]{:S(2)}) collective-permute-start(bf16[64,1792]{1,0:T(8,128)(2,1)S(1)} %get-tuple-element.84), channel_id=1, source_target_pairs={{0,2},{1,3},{2,0},{3,1},{4,6},{5,7},{6,4},{7,5},{8,10},{9,11},{10,... | collective-permute-start | bytes 688136 | tf_op jit(solution)/shard_map/ppermute | solution.py:24
  85.6 13.1 %collective-permute-start.27 = (bf16[224,768]{1,0:T(8,128)(2,1)S(1)}, bf16[224,768]{1,0:T(8,128)(2,1)S(1)}, u32[]{:S(2)}, u32[]{:S(2)}) collective-permute-start(bf16[224,768]{1,0:T(8,128)(2,1)S(1)} %get-tuple-element.88), channel_id=1, source_target_pairs={{0,8},{4,20},{8,0},{12,28},{16,24},{20,4},{24,16},{28,12},{1,9},{5... | collective-permute-start | bytes 1032200 | tf_op jit(solution)/shard_map/ppermute | solution.py:24
  87.2 10.9 %collective-permute-start.25 = (bf16[64,1920]{1,0:T(8,128)(2,1)S(1)}, bf16[64,1920]{1,0:T(8,128)(2,1)S(1)}, u32[]{:S(2)}, u32[]{:S(2)}) collective-permute-start(bf16[64,1920]{1,0:T(8,128)(2,1)S(1)} %pack.1.refs_0_), channel_id=1, source_target_pairs={{0,16},{16,0},{1,17},{17,1},{2,18},{18,2},{3,19},{19,3},{4,20},{20... | collective-permute-start | bytes 737288 | tf_op jit(solution)/shard_map/ppermute | solution.py:24
  96.2 7.1 %collective-permute-start.26 = (bf16[64,1792]{1,0:T(8,128)(2,1)S(1)}, bf16[64,1792]{1,0:T(8,128)(2,1)S(1)}, u32[]{:S(2)}, u32[]{:S(2)}) collective-permute-start(bf16[64,1792]{1,0:T(8,128)(2,1)S(1)} %add.11.refs_0_), channel_id=1, source_target_pairs={{0,16},{16,0},{1,17},{17,1},{2,18},{18,2},{3,19},{19,3},{4,20},{20... | collective-permute-start | bytes 688136 | tf_op jit(solution)/shard_map/ppermute | solution.py:24
  (2 other events, 4.2 us)

commit v6 on v5

--- a/solution.py
+++ b/solution.py
@@ -435,27 +435,28 @@
                 slope[here, at : at + size] = value.astype(BF16)
 
 
-def first_slopes(stats, side, counts, teacher, logits, size, after=()):
+def first_slopes(stats, side, counts, teacher, logits, hidden_t, size):
     rows = teacher.shape[0]
+    features = hidden_t[0].shape[0]
     parts = len(stats)
 
     def kernel(*refs):
-        before, (slope_0, slope_1, *after) = refs[: parts + 6], refs[parts + 6 :]
-        side, first, second, teacher, *logits = before[parts:]
+        before, (away, slope_0, slope_1, *after) = refs[: parts + 8], refs[parts + 8 :]
+        side, first, second, teacher, *logits = before[parts : parts + 6]
         row_kernel(before[:parts], side, (first, second), *after)
         slope_kernel(*after[1:], teacher, *logits, slope_0, slope_1, start=0)
-
-    *slopes, tokens, lses, shifts, weights = call(
+        weight_away_kernel(*before[parts + 6 :], slope_0, slope_1, away, start=0)
+
+    away, *slopes, tokens, lses, shifts, weights = call(
         kernel,
         "slopes",
-        [shape((rows // 2, size), BF16)] * 2
+        [shape((features // 2, size), BF16)]
+        + [shape((rows // 2, size), BF16)] * 2
         + [shape((2, rows), F32)]
         + [shape((rows, LANES), F32)] * 3,
-        [*stats, side, *counts, teacher, *logits],
-        (),
-        after,
-    )
-    return slopes, tokens, (lses, shifts, weights)
+        [*stats, side, *counts, teacher, *logits, *hidden_t],
+    )
+    return away, slopes, tokens, (lses, shifts, weights)
 
 
 def more_slopes(columns, teacher, logits, start, size, after=()):
@@ -683,11 +684,10 @@
         hidden_t.append(turn_rows(direct[pair], other[pair], after=stats[group:]))
     chunks = column_chunks(width, (7, 6, 6))
     split = chunks[1][0]
-    slopes, tokens, columns = first_slopes(
-        over_vocab(stats[1], vocab_size), side, counts, teacher_logits, logits, split, hidden_t[1:]
+    last, slopes, tokens, columns = first_slopes(
+        over_vocab(stats[1], vocab_size), side, counts, teacher_logits, logits, hidden_t, split
     )
     ranges = [(0, list(slopes))]
-    last = slopes[1]
 
     def slope_step(last):
         slopes = more_slopes(columns, teacher_logits, logits, split, width - split, after=[last])
@@ -714,7 +714,8 @@
         return slopes, start - begin, size
 
     def away_step(last):
-        last = weight_away(hidden_t, *chunk_of(len(arrived)), after=[last])
+        if arrived:
+            last = weight_away(hidden_t, *chunk_of(len(arrived)), after=[last])
         arrived.append(exchange(last, group_axes, group_size, lambda i: i ^ 1))
         return last
 

time: 104 us -> 104 us (level)
    pallas_call x34 -> x33, Pallas kernels: 31 us -> 31 us  [call(): pl.pallas_call(lambda *refs: kernel(*refs[skip:]), in_specs=[pl.BlockSpec...]
where the time goes in v6:
time: 104 us
  starting transfers between devices  36.8 us (35%)
  waiting for transfers between devices  33.8 us (32%)
  Pallas kernels  31 us (30%)
    ppermute x28, starting transfers between devices, exchange(): return lax.ppermute(array, axes, [(i, partner(i)) for i in range(size)])  36.8 us
    ppermute x28, waiting for transfers between devices, exchange(): return lax.ppermute(array, axes, [(i, partner(i)) for i in range(size)])  33.8 us
    pallas_call x33, Pallas kernels, call(): pl.pallas_call(lambda *refs: kernel(*refs[skip:]), in_specs=[pl.BlockSpec...  31 us
  transfers between devices with their start and end apart: 28, of which 11 were waited for; matrix products, arithmetic and copies ran while one was open for 0% of the time, Pallas kernels for 24%

profile of v6, /device:TPU:0, one launch (start us, length us, event | category | flops | bytes accessed | tf_op | source)
XLA Modules:
  0.0 104.1 jit_solution(9422213248972335794)
XLA Ops:
  1.6 3.0 %collective-permute-start.7 = (bf16[64,1792]{1,0:T(8,128)(2,1)S(1)}, bf16[64,1792]{1,0:T(8,128)(2,1)S(1)}, u32[]{:S(2)}, u32[]{:S(2)}) collective-permute-start(bf16[64,1792]{1,0:T(8,128)(2,1)S(1)} %pick_rows.3.refs_0_), channel_id=1, source_target_pairs={{0,16},{16,0},{1,17},{17,1},{2,18},{18,2},{3,19},{19,3},{4,20},{20... | collective-permute-start | bytes 688136 | tf_op jit(solution)/shard_map/ppermute | solution.py:24
  6.9 1.9 %collective-permute-start.3 = (bf16[64,1792]{1,0:T(8,128)(2,1)S(1)}, bf16[64,1792]{1,0:T(8,128)(2,1)S(1)}, u32[]{:S(2)}, u32[]{:S(2)}) collective-permute-start(bf16[64,1792]{1,0:T(8,128)(2,1)S(1)} %get-tuple-element.49), channel_id=1, source_target_pairs={{0,16},{16,0},{1,17},{17,1},{2,18},{18,2},{3,19},{19,3},{4,20},{20... | collective-permute-start | bytes 688136 | tf_op jit(solution)/shard_map/ppermute | solution.py:24
  9.1 1.9 %teacher_stats.1.refs_0_.refs_8_ = f32[8,512]{1,0:T(8,128)S(1)} custom-call(bf16[64,1920]{1,0:T(8,128)(2,1)S(1)} %pick_rows.4.refs_0_, bf16[512,2432]{1,0:T(8,128)(2,1)S(1)} %copy-done), custom_call_target="tpu_custom_call" | custom-call | flops 20000000000 | bytes 1024 | tf_op jit(solution)/shard_map/teacher_stats/pallas_call | solution.py:39
  11.1 2.1 %collective-permute-start.8 = (bf16[64,1792]{1,0:T(8,128)(2,1)S(1)}, bf16[64,1792]{1,0:T(8,128)(2,1)S(1)}, u32[]{:S(2)}, u32[]{:S(2)}) collective-permute-start(bf16[64,1792]{1,0:T(8,128)(2,1)S(1)} %pass_on.3.refs_1_), channel_id=1, source_target_pairs={{0,1},{1,0},{2,3},{3,2},{4,5},{5,4},{6,7},{7,6},{8,9},{9,8},{10,11... | collective-permute-start | bytes 688136 | tf_op jit(solution)/shard_map/ppermute | solution.py:24
  13.2 3.1 %collective-permute-done.refs_0_ = bf16[64,1920]{1,0:T(8,128)(2,1)S(1)} collective-permute-done((bf16[64,1920]{1,0:T(8,128)(2,1)S(1)}, bf16[64,1920]{1,0:T(8,128)(2,1)S(1)}, u32[]{:S(2)}, u32[]{:S(2)}) %collective-permute-start) | collective-permute-done | bytes 245792 | tf_op jit(solution)/shard_map/ppermute | solution.py:24
  16.3 2.2 %collective-permute-start.9 = (bf16[64,1792]{1,0:T(8,128)(2,1)S(1)}, bf16[64,1792]{1,0:T(8,128)(2,1)S(1)}, u32[]{:S(2)}, u32[]{:S(2)}) collective-permute-start(bf16[64,1792]{1,0:T(8,128)(2,1)S(1)} %get-tuple-element.51.refs_2_), channel_id=1, source_target_pairs={{0,1},{1,0},{2,3},{3,2},{4,5},{5,4},{6,7},{7,6},{8,9},{9,8},{10,11... | collective-permute-start | bytes 688136 | tf_op jit(solution)/shard_map/ppermute | solution.py:24
  18.7 2.5 %collective-permute-done.3.refs_1_ = bf16[64,1792]{1,0:T(8,128)(2,1)S(1)} collective-permute-done((bf16[64,1792]{1,0:T(8,128)(2,1)S(1)}, bf16[64,1792]{1,0:T(8,128)(2,1)S(1)}, u32[]{:S(2)}, u32[]{:S(2)}) %collective-permute-start.3) | collective-permute-done | bytes 229408 | tf_op jit(solution)/shard_map/ppermute | solution.py:24
  21.2 2.1 %collective-permute-start.5 = (bf16[64,1792]{1,0:T(8,128)(2,1)S(1)}, bf16[64,1792]{1,0:T(8,128)(2,1)S(1)}, u32[]{:S(2)}, u32[]{:S(2)}) collective-permute-start(bf16[64,1792]{1,0:T(8,128)(2,1)S(1)} %collective-permute-done.3.refs_1_), channel_id=1, source_target_pairs={{0,1},{1,0},{2,3},{3,2},{4,5},{5,4},{6,7},{7,6},{8,9},{9,8},{10,11... | collective-permute-start | bytes 688136 | tf_op jit(solution)/shard_map/ppermute | solution.py:24
  23.4 1.9 %collective-permute-done.4.refs_1_ = bf16[64,1792]{1,0:T(8,128)(2,1)S(1)} collective-permute-done((bf16[64,1792]{1,0:T(8,128)(2,1)S(1)}, bf16[64,1792]{1,0:T(8,128)(2,1)S(1)}, u32[]{:S(2)}, u32[]{:S(2)}) %collective-permute-start.4) | collective-permute-done | bytes 229408 | tf_op jit(solution)/shard_map/ppermute | solution.py:24
  25.3 1.8 %collective-permute-start.6 = (bf16[64,1792]{1,0:T(8,128)(2,1)S(1)}, bf16[64,1792]{1,0:T(8,128)(2,1)S(1)}, u32[]{:S(2)}, u32[]{:S(2)}) collective-permute-start(bf16[64,1792]{1,0:T(8,128)(2,1)S(1)} %pass_on.2.refs_0_.refs_2_), channel_id=1, source_target_pairs={{0,1},{1,0},{2,3},{3,2},{4,5},{5,4},{6,7},{7,6},{8,9},{9,8},{10,11... | collective-permute-start | bytes 688136 | tf_op jit(solution)/shard_map/ppermute | solution.py:24
  27.1 1.5 %collective-permute-start.2 = (f32[8,128]{1,0:T(8,128)S(1)}, f32[8,128]{1,0:T(8,128)S(1)}, u32[]{:S(2)}, u32[]{:S(2)}) collective-permute-start(f32[8,128]{1,0:T(8,128)S(1)} %sum_rows.1.refs_0_.refs_5_), channel_id=1, source_target_pairs={{0,8},{4,12},{8,0},{12,4},{1,9},{5,13},{9,1},{13,5},{2,10},{6,14},... | collective-permute-start | bytes 12296 | tf_op jit(solution)/shard_map/ppermute | solution.py:24
  28.7 3.5 %group_logits.2 = (f32[256,2432]{1,0:T(8,128)S(1)}, f32[8,512]{1,0:T(8,128)S(1)}) custom-call(bf16[64,1792]{1,0:T(8,128)(2,1)S(1)} %pass_on.2.refs_0_.refs_2_, bf16[64,1792]{1,0:T(8,128)(2,1)S(1)} %pass_on.3.refs_1_, bf16[64,1792]{1,0:T(8,128)(2,1)S(1)} %get-tuple-element.51.refs_2_, bf16[64,1792]{1,0:T(8,128)(2,1)S(1)} %collective-permute-done.8.refs_3_, ...), custom_call_target="tpu_custom_call" | custom-call | flops 2000000000 | bytes 1024 | tf_op jit(solution)/shard_map/group_logits/pallas_call | solution.py:39
  32.5 3.4 %group_logits.3 = (f32[256,2432]{1,0:T(8,128)S(1)}, f32[8,512]{1,0:T(8,128)S(1)}) custom-call(f32[8,128]{1,0:T(8,128)S(1)} %collective-permute-done.2.refs_0_.refs_6_, bf16[64,1792]{1,0:T(8,128)(2,1)S(1)} %collective-permute-done.3.refs_1_, bf16[64,1792]{1,0:T(8,128)(2,1)S(1)} %pass_on.2.refs_0_.refs_2_, ...), custom_call_target="tpu_custom_call" | custom-call | flops 20000000000 | bytes 1024 | tf_op jit(solution)/shard_map/group_logits/pallas_call | solution.py:39
  35.9 4.0 %collective-permute-start.12 = (f32[8,512]{1,0:T(8,128)S(1)}, f32[8,512]{1,0:T(8,128)S(1)}, u32[]{:S(2)}, u32[]{:S(2)}) collective-permute-start(f32[8,512]{1,0:T(8,128)S(1)} %get-tuple-element.53.refs_0_), channel_id=1, source_target_pairs={{0,3},{1,2},{2,1},{3,0},{4,7},{5,6},{6,5},{7,4},{8,11},{9,10},{10,... | collective-permute-start | bytes 49160 | tf_op jit(solution)/shard_map/ppermute | solution.py:24
  41.6 2.9 %collective-permute-done.11.refs_2_ = f32[8,512]{1,0:T(8,128)S(1)} collective-permute-done((f32[8,512]{1,0:T(8,128)S(1)}, f32[8,512]{1,0:T(8,128)S(1)}, u32[]{:S(2)}, u32[]{:S(2)}) %collective-permute-start.11) | collective-permute-done | bytes 16416 | tf_op jit(solution)/shard_map/ppermute | solution.py:24
  44.6 2.1 %slopes.2 = (bf16[896,896]{1,0:T(8,128)(2,1)S(1)}, bf16[256,896]{1,0:T(8,128)(2,1)S(1)}, bf16[256,896]{1,0:T(8,128)(2,1)S(1)}, f32[2,512]{1,0:T(2,128)S(1)}, f32...) custom-call(f32[8,512]{1,0:T(8,128)S(1)} %get-tuple-element.53.refs_0_, ...), custom_call_target="tpu_custom_call" | custom-call | flops 1024 | bytes 1024 | tf_op jit(solution)/shard_map/slopes/pallas_call | solution.py:39
  51.6 1.6 %collective-permute-start.16 = (bf16[448,896]{1,0:T(8,128)(2,1)S(1)}, bf16[448,896]{1,0:T(8,128)(2,1)S(1)}, u32[]{:S(2)}, u32[]{:S(2)}) collective-permute-start(bf16[448,896]{1,0:T(8,128)(2,1)S(1)} %get-tuple-element.69), channel_id=1, source_target_pairs={{0,16},{4,12},{8,24},{12,4},{16,0},{20,28},{24,8},{28,20},{1,17},{... | collective-permute-start | bytes 2408456 | tf_op jit(solution)/shard_map/ppermute | solution.py:24
  53.2 2.6 %hidden_grad.2 = (bf16[128,1792]{1,0:T(8,128)(2,1)S(1)}, f32[128,1792]{1,0:T(8,128)S(1)}) custom-call(bf16[448,896]{1,0:T(8,128)(2,1)S(1)} %get-tuple-element.64.refs_0_.refs_1_, bf16[256,896]{1,0:T(8,128)(2,1)S(1)} %get-tuple-element.62.refs_3_.refs_1_, bf16[256,1536]{1,0:T(8,128)(2,1)S(1)} %get-tuple-element.61.refs_3_.refs_2_, bf16[1792,2432]{1,0:T(8,128)(2,1)S(1)} %bitcast.5), custom_call_target="tpu_custom_call" | custom-call | flops 1024 | bytes 1024 | tf_op jit(solution)/shard_map/hidden_grad/pallas_call | solution.py:39
  58.3 1.6 %collective-permute-start.21 = (bf16[448,768]{1,0:T(8,128)(2,1)S(1)}, bf16[448,768]{1,0:T(8,128)(2,1)S(1)}, u32[]{:S(2)}, u32[]{:S(2)}) collective-permute-start(bf16[448,768]{1,0:T(8,128)(2,1)S(1)} %get-tuple-element.79), channel_id=1, source_target_pairs={{0,16},{4,12},{8,24},{12,4},{16,0},{20,28},{24,8},{28,20},{1,17},{... | collective-permute-start | bytes 2064392 | tf_op jit(solution)/shard_map/ppermute | solution.py:24
  59.9 2.6 %hidden_grad.3 = (bf16[128,1792]{1,0:T(8,128)(2,1)S(1)}, f32[128,1792]{1,0:T(8,128)S(1)}) custom-call(bf16[448,768]{1,0:T(8,128)(2,1)S(1)} %get-tuple-element.67.refs_0_.refs_1_, bf16[256,896]{1,0:T(8,128)(2,1)S(1)} %get-tuple-element.63.refs_4_.refs_1_, bf16[256,1536]{1,0:T(8,128)(2,1)S(1)} %get-tuple-element.60.refs_0_.refs_4_.refs_2_, ...), custom_call_target="tpu_custom_call" | custom-call | flops 1024 | bytes 1024 | tf_op jit(solution)/shard_map/hidden_grad/pallas_call | solution.py:39
  62.5 2.1 %collective-permute-start.20 = (bf16[128,1792]{1,0:T(8,128)(2,1)S(1)}, bf16[128,1792]{1,0:T(8,128)(2,1)S(1)}, u32[]{:S(2)}, u32[]{:S(2)}) collective-permute-start(bf16[128,1792]{1,0:T(8,128)(2,1)S(1)} %get-tuple-element.68.refs_0_), channel_id=1, source_target_pairs={{0,1},{1,0},{2,3},{3,2},{4,5},{5,4},{6,7},{7,6},{8,9},{9,8},{10,11... | collective-permute-start | bytes 1376264 | tf_op jit(solution)/shard_map/ppermute | solution.py:24
  64.8 4.5 %collective-permute-done.17.refs_2_ = bf16[128,1792]{1,0:T(8,128)(2,1)S(1)} collective-permute-done((bf16[128,1792]{1,0:T(8,128)(2,1)S(1)}, bf16[128,1792]{1,0:T(8,128)(2,1)S(1)}, u32[]{:S(2)}, u32[]{:S(2)}) %collective-permute-start.17) | collective-permute-done | bytes 458784 | tf_op jit(solution)/shard_map/ppermute | solution.py:24
  69.3 2.1 %collective-permute-start.18 = (bf16[64,1792]{1,0:T(8,128)(2,1)S(1)}, bf16[64,1792]{1,0:T(8,128)(2,1)S(1)}, u32[]{:S(2)}, u32[]{:S(2)}) collective-permute-start(bf16[64,1792]{1,0:T(8,128)(2,1)S(1)} %get-tuple-element.73), channel_id=1, source_target_pairs={{0,2},{1,3},{2,0},{3,1},{4,6},{5,7},{6,4},{7,5},{8,10},{9,11},{10,... | collective-permute-start | bytes 688136 | tf_op jit(solution)/shard_map/ppermute | solution.py:24
  71.4 1.6 %collective-permute-start.22 = (bf16[224,896]{1,0:T(8,128)(2,1)S(1)}, bf16[224,896]{1,0:T(8,128)(2,1)S(1)}, u32[]{:S(2)}, u32[]{:S(2)}) collective-permute-start(bf16[224,896]{1,0:T(8,128)(2,1)S(1)} %get-tuple-element.81), channel_id=1, source_target_pairs={{0,8},{4,20},{8,0},{12,28},{16,24},{20,4},{24,16},{28,12},{1,9},{5... | collective-permute-start | bytes 1204232 | tf_op jit(solution)/shard_map/ppermute | solution.py:24
  73.0 8.1 %collective-permute-done.18.refs_2_ = bf16[64,1792]{1,0:T(8,128)(2,1)S(1)} collective-permute-done((bf16[64,1792]{1,0:T(8,128)(2,1)S(1)}, bf16[64,1792]{1,0:T(8,128)(2,1)S(1)}, u32[]{:S(2)}, u32[]{:S(2)}) %collective-permute-start.18) | collective-permute-done | bytes 229408 | tf_op jit(solution)/shard_map/ppermute | solution.py:24
  81.9 1.3 %collective-permute-done.20.refs_2_ = bf16[128,1792]{1,0:T(8,128)(2,1)S(1)} collective-permute-done((bf16[128,1792]{1,0:T(8,128)(2,1)S(1)}, bf16[128,1792]{1,0:T(8,128)(2,1)S(1)}, u32[]{:S(2)}, u32[]{:S(2)}) %collective-permute-start.20) | collective-permute-done | bytes 458784 | tf_op jit(solution)/shard_map/ppermute | solution.py:24
  83.4 2.1 %collective-permute-start.24 = (bf16[64,1792]{1,0:T(8,128)(2,1)S(1)}, bf16[64,1792]{1,0:T(8,128)(2,1)S(1)}, u32[]{:S(2)}, u32[]{:S(2)}) collective-permute-start(bf16[64,1792]{1,0:T(8,128)(2,1)S(1)} %get-tuple-element.86), channel_id=1, source_target_pairs={{0,2},{1,3},{2,0},{3,1},{4,6},{5,7},{6,4},{7,5},{8,10},{9,11},{10,... | collective-permute-start | bytes 688136 | tf_op jit(solution)/shard_map/ppermute | solution.py:24
  85.6 1.6 %collective-permute-start.27 = (bf16[224,768]{1,0:T(8,128)(2,1)S(1)}, bf16[224,768]{1,0:T(8,128)(2,1)S(1)}, u32[]{:S(2)}, u32[]{:S(2)}) collective-permute-start(bf16[224,768]{1,0:T(8,128)(2,1)S(1)} %get-tuple-element.90), channel_id=1, source_target_pairs={{0,8},{4,20},{8,0},{12,28},{16,24},{20,4},{24,16},{28,12},{1,9},{5... | collective-permute-start | bytes 1032200 | tf_op jit(solution)/shard_map/ppermute | solution.py:24
  89.6 6.6 %collective-permute-done.24.refs_2_ = bf16[64,1792]{1,0:T(8,128)(2,1)S(1)} collective-permute-done((bf16[64,1792]{1,0:T(8,128)(2,1)S(1)}, bf16[64,1792]{1,0:T(8,128)(2,1)S(1)}, u32[]{:S(2)}, u32[]{:S(2)}) %collective-permute-start.24) | collective-permute-done | bytes 229408 | tf_op jit(solution)/shard_map/ppermute | solution.py:24
  96.2 1.9 %collective-permute-start.26 = (bf16[64,1792]{1,0:T(8,128)(2,1)S(1)}, bf16[64,1792]{1,0:T(8,128)(2,1)S(1)}, u32[]{:S(2)}, u32[]{:S(2)}) collective-permute-start(bf16[64,1792]{1,0:T(8,128)(2,1)S(1)} %add.11.refs_0_), channel_id=1, source_target_pairs={{0,16},{16,0},{1,17},{17,1},{2,18},{18,2},{3,19},{19,3},{4,20},{20... | collective-permute-start | bytes 688136 | tf_op jit(solution)/shard_map/ppermute | solution.py:24
  99.4 1.5 %finish.5 = (bf16[224,2432]{1,0:T(8,128)(2,1)}, f32[8,128]{1,0:T(8,128)}) custom-call(f32[1,512]{1,0:T(1,128)S(1)} %copy-done.2, bf16[224,2432]{1,0:T(8,128)(2,1)} %get-tuple-element.89.refs_1_, bf16[224,768]{1,0:T(8,128)(2,1)S(1)} %get-tuple-element.80.refs_0_.refs_2_, ...), custom_call_target="tpu_custom_call", output_to_operand_aliasing={{0}: (1, {})} | custom-call | flops 1024 | bytes 1024 | tf_op jit(solution)/shard_map/finish/pallas_call | solution.py:39
  100.9 2.4 %collective-permute-done.26 = bf16[64,1792]{1,0:T(8,128)(2,1)S(1)} collective-permute-done((bf16[64,1792]{1,0:T(8,128)(2,1)S(1)}, bf16[64,1792]{1,0:T(8,128)(2,1)S(1)}, u32[]{:S(2)}, u32[]{:S(2)}) %collective-permute-start.26) | collective-permute-done | bytes 229408 | tf_op jit(solution)/shard_map/ppermute | solution.py:24
  (72 shorter events, 19.0 us)
Async XLA Ops:
  1.6 9.5 %collective-permute-start.7 = (bf16[64,1792]{1,0:T(8,128)(2,1)S(1)}, bf16[64,1792]{1,0:T(8,128)(2,1)S(1)}, u32[]{:S(2)}, u32[]{:S(2)}) collective-permute-start(bf16[64,1792]{1,0:T(8,128)(2,1)S(1)} %pick_rows.3.refs_0_), channel_id=1, source_target_pairs={{0,16},{16,0},{1,17},{17,1},{2,18},{18,2},{3,19},{19,3},{4,20},{20... | collective-permute-start | bytes 688136 | tf_op jit(solution)/shard_map/ppermute | solution.py:24
  5.6 10.7 %collective-permute-start = (bf16[64,1920]{1,0:T(8,128)(2,1)S(1)}, bf16[64,1920]{1,0:T(8,128)(2,1)S(1)}, u32[]{:S(2)}, u32[]{:S(2)}) collective-permute-start(bf16[64,1920]{1,0:T(8,128)(2,1)S(1)} %pick_rows.4.refs_0_), channel_id=1, source_target_pairs={{0,16},{16,0},{1,17},{17,1},{2,18},{18,2},{3,19},{19,3},{4,20},{20... | collective-permute-start | bytes 737288 | tf_op jit(solution)/shard_map/ppermute | solution.py:24
  6.9 14.3 %collective-permute-start.3 = (bf16[64,1792]{1,0:T(8,128)(2,1)S(1)}, bf16[64,1792]{1,0:T(8,128)(2,1)S(1)}, u32[]{:S(2)}, u32[]{:S(2)}) collective-permute-start(bf16[64,1792]{1,0:T(8,128)(2,1)S(1)} %get-tuple-element.49), channel_id=1, source_target_pairs={{0,16},{16,0},{1,17},{17,1},{2,18},{18,2},{3,19},{19,3},{4,20},{20... | collective-permute-start | bytes 688136 | tf_op jit(solution)/shard_map/ppermute | solution.py:24
  8.8 19.8 %slice-start = ((s8[8716288]{0:T(1024)(128)(4,1)}), s8[4194304]{0:T(1024)(128)(4,1)S(1)}, s32[]{:S(2)}) async-start(s8[8716288]{0:T(1024)(128)(4,1)} %bitcast.4), calls=%async_computation | async-start | bytes 8388608
  8.9 9.7 %copy-start.1 = (s32[512]{0:T(512)S(1)}, s32[512]{0:T(512)}, u32[]{:S(2)}) copy-start(s32[512]{0:T(512)} %param.9) | copy-start | bytes 6148
  8.9 19.8 %slice-start.1 = ((s8[8716288]{0:T(1024)(128)(4,1)}), s8[4194304]{0:T(1024)(128)(4,1)S(1)}, s32[]{:S(2)}) async-start(s8[8716288]{0:T(1024)(128)(4,1)} %bitcast.4), calls=%async_computation.1 | async-start | bytes 8388608
  8.9 19.8 %slice-start.2 = ((s8[8716288]{0:T(1024)(128)(4,1)}), s8[327680]{0:T(1024)(128)(4,1)S(1)}, s32[]{:S(2)}) async-start(s8[8716288]{0:T(1024)(128)(4,1)} %bitcast.4), calls=%async_computation.2 | async-start | bytes 655360
  8.9 16.4 %collective-permute-start.4 = (bf16[64,1792]{1,0:T(8,128)(2,1)S(1)}, bf16[64,1792]{1,0:T(8,128)(2,1)S(1)}, u32[]{:S(2)}, u32[]{:S(2)}) collective-permute-start(bf16[64,1792]{1,0:T(8,128)(2,1)S(1)} %get-tuple-element.50), channel_id=1, source_target_pairs={{0,16},{16,0},{1,17},{17,1},{2,18},{18,2},{3,19},{19,3},{4,20},{20... | collective-permute-start | bytes 688136 | tf_op jit(solution)/shard_map/ppermute | solution.py:24
  11.1 17.6 %collective-permute-start.8 = (bf16[64,1792]{1,0:T(8,128)(2,1)S(1)}, bf16[64,1792]{1,0:T(8,128)(2,1)S(1)}, u32[]{:S(2)}, u32[]{:S(2)}) collective-permute-start(bf16[64,1792]{1,0:T(8,128)(2,1)S(1)} %pass_on.3.refs_1_), channel_id=1, source_target_pairs={{0,1},{1,0},{2,3},{3,2},{4,5},{5,4},{6,7},{7,6},{8,9},{9,8},{10,11... | collective-permute-start | bytes 688136 | tf_op jit(solution)/shard_map/ppermute | solution.py:24
  16.3 12.3 %collective-permute-start.9 = (bf16[64,1792]{1,0:T(8,128)(2,1)S(1)}, bf16[64,1792]{1,0:T(8,128)(2,1)S(1)}, u32[]{:S(2)}, u32[]{:S(2)}) collective-permute-start(bf16[64,1792]{1,0:T(8,128)(2,1)S(1)} %get-tuple-element.51.refs_2_), channel_id=1, source_target_pairs={{0,1},{1,0},{2,3},{3,2},{4,5},{5,4},{6,7},{7,6},{8,9},{9,8},{10,11... | collective-permute-start | bytes 688136 | tf_op jit(solution)/shard_map/ppermute | solution.py:24
  18.7 4.7 %collective-permute-start.1 = (f32[8,128]{1,0:T(8,128)S(1)}, f32[8,128]{1,0:T(8,128)S(1)}, u32[]{:S(2)}, u32[]{:S(2)}) collective-permute-start(f32[8,128]{1,0:T(8,128)S(1)} %count_rows.1.refs_0_), channel_id=1, source_target_pairs={{0,4},{4,0},{8,12},{12,8},{1,5},{5,1},{9,13},{13,9},{2,6},{6,2},{1... | collective-permute-start | bytes 12296 | tf_op jit(solution)/shard_map/ppermute | solution.py:24
  21.2 11.0 %collective-permute-start.5 = (bf16[64,1792]{1,0:T(8,128)(2,1)S(1)}, bf16[64,1792]{1,0:T(8,128)(2,1)S(1)}, u32[]{:S(2)}, u32[]{:S(2)}) collective-permute-start(bf16[64,1792]{1,0:T(8,128)(2,1)S(1)} %collective-permute-done.3.refs_1_), channel_id=1, source_target_pairs={{0,1},{1,0},{2,3},{3,2},{4,5},{5,4},{6,7},{7,6},{8,9},{9,8},{10,11... | collective-permute-start | bytes 688136 | tf_op jit(solution)/shard_map/ppermute | solution.py:24
  25.3 7.2 %collective-permute-start.6 = (bf16[64,1792]{1,0:T(8,128)(2,1)S(1)}, bf16[64,1792]{1,0:T(8,128)(2,1)S(1)}, u32[]{:S(2)}, u32[]{:S(2)}) collective-permute-start(bf16[64,1792]{1,0:T(8,128)(2,1)S(1)} %pass_on.2.refs_0_.refs_2_), channel_id=1, source_target_pairs={{0,1},{1,0},{2,3},{3,2},{4,5},{5,4},{6,7},{7,6},{8,9},{9,8},{10,11... | collective-permute-start | bytes 688136 | tf_op jit(solution)/shard_map/ppermute | solution.py:24
  27.1 5.0 %collective-permute-start.2 = (f32[8,128]{1,0:T(8,128)S(1)}, f32[8,128]{1,0:T(8,128)S(1)}, u32[]{:S(2)}, u32[]{:S(2)}) collective-permute-start(f32[8,128]{1,0:T(8,128)S(1)} %sum_rows.1.refs_0_.refs_5_), channel_id=1, source_target_pairs={{0,8},{4,12},{8,0},{12,4},{1,9},{5,13},{9,1},{13,5},{2,10},{6,14},... | collective-permute-start | bytes 12296 | tf_op jit(solution)/shard_map/ppermute | solution.py:24
  35.9 5.7 %collective-permute-start.12 = (f32[8,512]{1,0:T(8,128)S(1)}, f32[8,512]{1,0:T(8,128)S(1)}, u32[]{:S(2)}, u32[]{:S(2)}) collective-permute-start(f32[8,512]{1,0:T(8,128)S(1)} %get-tuple-element.53.refs_0_), channel_id=1, source_target_pairs={{0,3},{1,2},{2,1},{3,0},{4,7},{5,6},{6,5},{7,4},{8,11},{9,10},{10,... | collective-permute-start | bytes 49160 | tf_op jit(solution)/shard_map/ppermute | solution.py:24
  39.9 4.6 %collective-permute-start.11 = (f32[8,512]{1,0:T(8,128)S(1)}, f32[8,512]{1,0:T(8,128)S(1)}, u32[]{:S(2)}, u32[]{:S(2)}) collective-permute-start(f32[8,512]{1,0:T(8,128)S(1)} %get-tuple-element.53.refs_0_), channel_id=1, source_target_pairs={{0,2},{1,3},{2,0},{3,1},{4,6},{5,7},{6,4},{7,5},{8,10},{9,11},{10,... | collective-permute-start | bytes 49160 | tf_op jit(solution)/shard_map/ppermute | solution.py:24
  39.9 4.6 %collective-permute-start.10 = (f32[8,512]{1,0:T(8,128)S(1)}, f32[8,512]{1,0:T(8,128)S(1)}, u32[]{:S(2)}, u32[]{:S(2)}) collective-permute-start(f32[8,512]{1,0:T(8,128)S(1)} %get-tuple-element.53.refs_0_), channel_id=1, source_target_pairs={{0,1},{1,0},{2,3},{3,2},{4,5},{5,4},{6,7},{7,6},{8,9},{9,8},{10,11... | collective-permute-start | bytes 49160 | tf_op jit(solution)/shard_map/ppermute | solution.py:24
  46.7 3.8 %collective-permute-start.13 = (bf16[896,896]{1,0:T(8,128)(2,1)S(1)}, bf16[896,896]{1,0:T(8,128)(2,1)S(1)}, u32[]{:S(2)}, u32[]{:S(2)}) collective-permute-start(bf16[896,896]{1,0:T(8,128)(2,1)S(1)} %get-tuple-element.56.refs_0_), channel_id=1, source_target_pairs={{0,4},{4,0},{8,12},{12,8},{16,20},{20,16},{24,28},{28,24},{1,5},{5... | collective-permute-start | bytes 4816904 | tf_op jit(solution)/shard_map/ppermute | solution.py:24
  49.0 6.9 %collective-permute-start.14 = (bf16[896,768]{1,0:T(8,128)(2,1)S(1)}, bf16[896,768]{1,0:T(8,128)(2,1)S(1)}, u32[]{:S(2)}, u32[]{:S(2)}) collective-permute-start(bf16[896,768]{1,0:T(8,128)(2,1)S(1)} %weight_away.2.refs_0_), channel_id=1, source_target_pairs={{0,4},{4,0},{8,12},{12,8},{16,20},{20,16},{24,28},{28,24},{1,5},{5... | collective-permute-start | bytes 4128776 | tf_op jit(solution)/shard_map/ppermute | solution.py:24
  50.4 7.0 %collective-permute-start.15 = (bf16[896,768]{1,0:T(8,128)(2,1)S(1)}, bf16[896,768]{1,0:T(8,128)(2,1)S(1)}, u32[]{:S(2)}, u32[]{:S(2)}) collective-permute-start(bf16[896,768]{1,0:T(8,128)(2,1)S(1)} %weight_away.3.refs_0_), channel_id=1, source_target_pairs={{0,4},{4,0},{8,12},{12,8},{16,20},{20,16},{24,28},{28,24},{1,5},{5... | collective-permute-start | bytes 4128776 | tf_op jit(solution)/shard_map/ppermute | solution.py:24
  51.6 12.9 %collective-permute-start.16 = (bf16[448,896]{1,0:T(8,128)(2,1)S(1)}, bf16[448,896]{1,0:T(8,128)(2,1)S(1)}, u32[]{:S(2)}, u32[]{:S(2)}) collective-permute-start(bf16[448,896]{1,0:T(8,128)(2,1)S(1)} %get-tuple-element.69), channel_id=1, source_target_pairs={{0,16},{4,12},{8,24},{12,4},{16,0},{20,28},{24,8},{28,20},{1,17},{... | collective-permute-start | bytes 2408456 | tf_op jit(solution)/shard_map/ppermute | solution.py:24
  55.8 13.4 %collective-permute-start.17 = (bf16[128,1792]{1,0:T(8,128)(2,1)S(1)}, bf16[128,1792]{1,0:T(8,128)(2,1)S(1)}, u32[]{:S(2)}, u32[]{:S(2)}) collective-permute-start(bf16[128,1792]{1,0:T(8,128)(2,1)S(1)} %get-tuple-element.65.refs_0_), channel_id=1, source_target_pairs={{0,1},{1,0},{2,3},{3,2},{4,5},{5,4},{6,7},{7,6},{8,9},{9,8},{10,11... | collective-permute-start | bytes 1376264 | tf_op jit(solution)/shard_map/ppermute | solution.py:24
  56.8 24.4 %collective-permute-start.19 = (bf16[448,768]{1,0:T(8,128)(2,1)S(1)}, bf16[448,768]{1,0:T(8,128)(2,1)S(1)}, u32[]{:S(2)}, u32[]{:S(2)}) collective-permute-start(bf16[448,768]{1,0:T(8,128)(2,1)S(1)} %get-tuple-element.75), channel_id=1, source_target_pairs={{0,16},{4,12},{8,24},{12,4},{16,0},{20,28},{24,8},{28,20},{1,17},{... | collective-permute-start | bytes 2064392 | tf_op jit(solution)/shard_map/ppermute | solution.py:24
  58.3 27.1 %collective-permute-start.21 = (bf16[448,768]{1,0:T(8,128)(2,1)S(1)}, bf16[448,768]{1,0:T(8,128)(2,1)S(1)}, u32[]{:S(2)}, u32[]{:S(2)}) collective-permute-start(bf16[448,768]{1,0:T(8,128)(2,1)S(1)} %get-tuple-element.79), channel_id=1, source_target_pairs={{0,16},{4,12},{8,24},{12,4},{16,0},{20,28},{24,8},{28,20},{1,17},{... | collective-permute-start | bytes 2064392 | tf_op jit(solution)/shard_map/ppermute | solution.py:24
  62.5 20.8 %collective-permute-start.20 = (bf16[128,1792]{1,0:T(8,128)(2,1)S(1)}, bf16[128,1792]{1,0:T(8,128)(2,1)S(1)}, u32[]{:S(2)}, u32[]{:S(2)}) collective-permute-start(bf16[128,1792]{1,0:T(8,128)(2,1)S(1)} %get-tuple-element.68.refs_0_), channel_id=1, source_target_pairs={{0,1},{1,0},{2,3},{3,2},{4,5},{5,4},{6,7},{7,6},{8,9},{9,8},{10,11... | collective-permute-start | bytes 1376264 | tf_op jit(solution)/shard_map/ppermute | solution.py:24
  69.3 11.8 %collective-permute-start.18 = (bf16[64,1792]{1,0:T(8,128)(2,1)S(1)}, bf16[64,1792]{1,0:T(8,128)(2,1)S(1)}, u32[]{:S(2)}, u32[]{:S(2)}) collective-permute-start(bf16[64,1792]{1,0:T(8,128)(2,1)S(1)} %get-tuple-element.73), channel_id=1, source_target_pairs={{0,2},{1,3},{2,0},{3,1},{4,6},{5,7},{6,4},{7,5},{8,10},{9,11},{10,... | collective-permute-start | bytes 688136 | tf_op jit(solution)/shard_map/ppermute | solution.py:24
  71.4 16.4 %collective-permute-start.22 = (bf16[224,896]{1,0:T(8,128)(2,1)S(1)}, bf16[224,896]{1,0:T(8,128)(2,1)S(1)}, u32[]{:S(2)}, u32[]{:S(2)}) collective-permute-start(bf16[224,896]{1,0:T(8,128)(2,1)S(1)} %get-tuple-element.81), channel_id=1, source_target_pairs={{0,8},{4,20},{8,0},{12,28},{16,24},{20,4},{24,16},{28,12},{1,9},{5... | collective-permute-start | bytes 1204232 | tf_op jit(solution)/shard_map/ppermute | solution.py:24
  81.4 7.3 %collective-permute-start.23 = (bf16[224,768]{1,0:T(8,128)(2,1)S(1)}, bf16[224,768]{1,0:T(8,128)(2,1)S(1)}, u32[]{:S(2)}, u32[]{:S(2)}) collective-permute-start(bf16[224,768]{1,0:T(8,128)(2,1)S(1)} %get-tuple-element.84), channel_id=1, source_target_pairs={{0,8},{4,20},{8,0},{12,28},{16,24},{20,4},{24,16},{28,12},{1,9},{5... | collective-permute-start | bytes 1032200 | tf_op jit(solution)/shard_map/ppermute | solution.py:24
  83.4 12.8 %collective-permute-start.24 = (bf16[64,1792]{1,0:T(8,128)(2,1)S(1)}, bf16[64,1792]{1,0:T(8,128)(2,1)S(1)}, u32[]{:S(2)}, u32[]{:S(2)}) collective-permute-start(bf16[64,1792]{1,0:T(8,128)(2,1)S(1)} %get-tuple-element.86), channel_id=1, source_target_pairs={{0,2},{1,3},{2,0},{3,1},{4,6},{5,7},{6,4},{7,5},{8,10},{9,11},{10,... | collective-permute-start | bytes 688136 | tf_op jit(solution)/shard_map/ppermute | solution.py:24
  85.6 13.1 %collective-permute-start.27 = (bf16[224,768]{1,0:T(8,128)(2,1)S(1)}, bf16[224,768]{1,0:T(8,128)(2,1)S(1)}, u32[]{:S(2)}, u32[]{:S(2)}) collective-permute-start(bf16[224,768]{1,0:T(8,128)(2,1)S(1)} %get-tuple-element.90), channel_id=1, source_target_pairs={{0,8},{4,20},{8,0},{12,28},{16,24},{20,4},{24,16},{28,12},{1,9},{5... | collective-permute-start | bytes 1032200 | tf_op jit(solution)/shard_map/ppermute | solution.py:24
  87.2 10.9 %collective-permute-start.25 = (bf16[64,1920]{1,0:T(8,128)(2,1)S(1)}, bf16[64,1920]{1,0:T(8,128)(2,1)S(1)}, u32[]{:S(2)}, u32[]{:S(2)}) collective-permute-start(bf16[64,1920]{1,0:T(8,128)(2,1)S(1)} %pack.1.refs_0_), channel_id=1, source_target_pairs={{0,16},{16,0},{1,17},{17,1},{2,18},{18,2},{3,19},{19,3},{4,20},{20... | collective-permute-start | bytes 737288 | tf_op jit(solution)/shard_map/ppermute | solution.py:24
  96.2 7.1 %collective-permute-start.26 = (bf16[64,1792]{1,0:T(8,128)(2,1)S(1)}, bf16[64,1792]{1,0:T(8,128)(2,1)S(1)}, u32[]{:S(2)}, u32[]{:S(2)}) collective-permute-start(bf16[64,1792]{1,0:T(8,128)(2,1)S(1)} %add.11.refs_0_), channel_id=1, source_target_pairs={{0,16},{16,0},{1,17},{17,1},{2,18},{18,2},{3,19},{19,3},{4,20},{20... | collective-permute-start | bytes 688136 | tf_op jit(solution)/shard_map/ppermute | solution.py:24
  (2 other events, 4.2 us)

commit v7 on v6

--- a/solution.py
+++ b/solution.py
@@ -307,7 +307,7 @@
     for ref in (total, gap, picked):
         ref[...] = jnp.zeros(ref.shape, F32)
     inside = rows // QUARTERS
-    for start, size in tiles(0, width, 4 * LANES):
+    for start, size in tiles(0, width, 5 * LANES):
         tile = jnp.dot(value, weight[:, start : start + size], preferred_element_type=F32)
         logits[:, start : start + size] = tile
         columns = range(start, start + size, LANES)

time: 104 us -> 105 us (level)
  transfers between devices with their start and end apart: 28 -> 28, of which waited for: 11 -> 10; matrix products, arithmetic and copies ran while one was open for 0% -> 0% of each run, Pallas kernels for 24% -> 24%
where the time goes in v7:
time: 105 us; the launch traced here: 104 us
  starting transfers between devices  36.7 us (35%)
  waiting for transfers between devices  33.5 us (32%)
  Pallas kernels  31.9 us (30%)
    ppermute x28, starting transfers between devices, exchange(): return lax.ppermute(array, axes, [(i, partner(i)) for i in range(size)])  36.7 us
    ppermute x28, waiting for transfers between devices, exchange(): return lax.ppermute(array, axes, [(i, partner(i)) for i in range(size)])  33.5 us
    pallas_call x33, Pallas kernels, call(): pl.pallas_call(lambda *refs: kernel(*refs[skip:]), in_specs=[pl.BlockSpec...  31.9 us
  transfers between devices with their start and end apart: 28, of which 10 were waited for; matrix products, arithmetic and copies ran while one was open for 0% of the time, Pallas kernels for 24%

profile of v7, /device:TPU:0, one launch (start us, length us, event | category | flops | bytes accessed | tf_op | source)
XLA Modules:
  0.0 104.5 jit_solution(4045248254234340984)
XLA Ops:
  1.6 3.0 %collective-permute-start.7 = (bf16[64,1792]{1,0:T(8,128)(2,1)S(1)}, bf16[64,1792]{1,0:T(8,128)(2,1)S(1)}, u32[]{:S(2)}, u32[]{:S(2)}) collective-permute-start(bf16[64,1792]{1,0:T(8,128)(2,1)S(1)} %pick_rows.3.refs_0_), channel_id=1, source_target_pairs={{0,16},{16,0},{1,17},{17,1},{2,18},{18,2},{3,19},{19,3},{4,20},{20... | collective-permute-start | bytes 688136 | tf_op jit(solution)/shard_map/ppermute | solution.py:24
  6.9 1.9 %collective-permute-start.3 = (bf16[64,1792]{1,0:T(8,128)(2,1)S(1)}, bf16[64,1792]{1,0:T(8,128)(2,1)S(1)}, u32[]{:S(2)}, u32[]{:S(2)}) collective-permute-start(bf16[64,1792]{1,0:T(8,128)(2,1)S(1)} %get-tuple-element.49), channel_id=1, source_target_pairs={{0,16},{16,0},{1,17},{17,1},{2,18},{18,2},{3,19},{19,3},{4,20},{20... | collective-permute-start | bytes 688136 | tf_op jit(solution)/shard_map/ppermute | solution.py:24
  9.1 1.9 %teacher_stats.1.refs_0_.refs_8_ = f32[8,512]{1,0:T(8,128)S(1)} custom-call(bf16[64,1920]{1,0:T(8,128)(2,1)S(1)} %pick_rows.4.refs_0_, bf16[512,2432]{1,0:T(8,128)(2,1)S(1)} %copy-done), custom_call_target="tpu_custom_call" | custom-call | flops 20000000000 | bytes 1024 | tf_op jit(solution)/shard_map/teacher_stats/pallas_call | solution.py:39
  11.1 2.1 %collective-permute-start.8 = (bf16[64,1792]{1,0:T(8,128)(2,1)S(1)}, bf16[64,1792]{1,0:T(8,128)(2,1)S(1)}, u32[]{:S(2)}, u32[]{:S(2)}) collective-permute-start(bf16[64,1792]{1,0:T(8,128)(2,1)S(1)} %pass_on.3.refs_1_), channel_id=1, source_target_pairs={{0,1},{1,0},{2,3},{3,2},{4,5},{5,4},{6,7},{7,6},{8,9},{9,8},{10,11... | collective-permute-start | bytes 688136 | tf_op jit(solution)/shard_map/ppermute | solution.py:24
  13.2 3.1 %collective-permute-done.refs_0_ = bf16[64,1920]{1,0:T(8,128)(2,1)S(1)} collective-permute-done((bf16[64,1920]{1,0:T(8,128)(2,1)S(1)}, bf16[64,1920]{1,0:T(8,128)(2,1)S(1)}, u32[]{:S(2)}, u32[]{:S(2)}) %collective-permute-start) | collective-permute-done | bytes 245792 | tf_op jit(solution)/shard_map/ppermute | solution.py:24
  16.3 2.2 %collective-permute-start.9 = (bf16[64,1792]{1,0:T(8,128)(2,1)S(1)}, bf16[64,1792]{1,0:T(8,128)(2,1)S(1)}, u32[]{:S(2)}, u32[]{:S(2)}) collective-permute-start(bf16[64,1792]{1,0:T(8,128)(2,1)S(1)} %get-tuple-element.51.refs_2_), channel_id=1, source_target_pairs={{0,1},{1,0},{2,3},{3,2},{4,5},{5,4},{6,7},{7,6},{8,9},{9,8},{10,11... | collective-permute-start | bytes 688136 | tf_op jit(solution)/shard_map/ppermute | solution.py:24
  18.7 2.5 %collective-permute-done.3.refs_1_ = bf16[64,1792]{1,0:T(8,128)(2,1)S(1)} collective-permute-done((bf16[64,1792]{1,0:T(8,128)(2,1)S(1)}, bf16[64,1792]{1,0:T(8,128)(2,1)S(1)}, u32[]{:S(2)}, u32[]{:S(2)}) %collective-permute-start.3) | collective-permute-done | bytes 229408 | tf_op jit(solution)/shard_map/ppermute | solution.py:24
  21.2 2.1 %collective-permute-start.5 = (bf16[64,1792]{1,0:T(8,128)(2,1)S(1)}, bf16[64,1792]{1,0:T(8,128)(2,1)S(1)}, u32[]{:S(2)}, u32[]{:S(2)}) collective-permute-start(bf16[64,1792]{1,0:T(8,128)(2,1)S(1)} %collective-permute-done.3.refs_1_), channel_id=1, source_target_pairs={{0,1},{1,0},{2,3},{3,2},{4,5},{5,4},{6,7},{7,6},{8,9},{9,8},{10,11... | collective-permute-start | bytes 688136 | tf_op jit(solution)/shard_map/ppermute | solution.py:24
  23.4 1.9 %collective-permute-done.4.refs_1_ = bf16[64,1792]{1,0:T(8,128)(2,1)S(1)} collective-permute-done((bf16[64,1792]{1,0:T(8,128)(2,1)S(1)}, bf16[64,1792]{1,0:T(8,128)(2,1)S(1)}, u32[]{:S(2)}, u32[]{:S(2)}) %collective-permute-start.4) | collective-permute-done | bytes 229408 | tf_op jit(solution)/shard_map/ppermute | solution.py:24
  25.3 1.8 %collective-permute-start.6 = (bf16[64,1792]{1,0:T(8,128)(2,1)S(1)}, bf16[64,1792]{1,0:T(8,128)(2,1)S(1)}, u32[]{:S(2)}, u32[]{:S(2)}) collective-permute-start(bf16[64,1792]{1,0:T(8,128)(2,1)S(1)} %pass_on.2.refs_0_.refs_2_), channel_id=1, source_target_pairs={{0,1},{1,0},{2,3},{3,2},{4,5},{5,4},{6,7},{7,6},{8,9},{9,8},{10,11... | collective-permute-start | bytes 688136 | tf_op jit(solution)/shard_map/ppermute | solution.py:24
  27.1 1.5 %collective-permute-start.2 = (f32[8,128]{1,0:T(8,128)S(1)}, f32[8,128]{1,0:T(8,128)S(1)}, u32[]{:S(2)}, u32[]{:S(2)}) collective-permute-start(f32[8,128]{1,0:T(8,128)S(1)} %sum_rows.1.refs_0_.refs_5_), channel_id=1, source_target_pairs={{0,8},{4,12},{8,0},{12,4},{1,9},{5,13},{9,1},{13,5},{2,10},{6,14},... | collective-permute-start | bytes 12296 | tf_op jit(solution)/shard_map/ppermute | solution.py:24
  28.7 3.9 %group_logits.2 = (f32[256,2432]{1,0:T(8,128)S(1)}, f32[8,512]{1,0:T(8,128)S(1)}) custom-call(bf16[64,1792]{1,0:T(8,128)(2,1)S(1)} %pass_on.2.refs_0_.refs_2_, bf16[64,1792]{1,0:T(8,128)(2,1)S(1)} %pass_on.3.refs_1_, bf16[64,1792]{1,0:T(8,128)(2,1)S(1)} %get-tuple-element.51.refs_2_, bf16[64,1792]{1,0:T(8,128)(2,1)S(1)} %collective-permute-done.8.refs_3_, ...), custom_call_target="tpu_custom_call" | custom-call | flops 2000000000 | bytes 1024 | tf_op jit(solution)/shard_map/group_logits/pallas_call | solution.py:39
  32.6 3.8 %group_logits.3 = (f32[256,2432]{1,0:T(8,128)S(1)}, f32[8,512]{1,0:T(8,128)S(1)}) custom-call(f32[8,128]{1,0:T(8,128)S(1)} %collective-permute-done.2.refs_0_.refs_6_, bf16[64,1792]{1,0:T(8,128)(2,1)S(1)} %collective-permute-done.3.refs_1_, bf16[64,1792]{1,0:T(8,128)(2,1)S(1)} %pass_on.2.refs_0_.refs_2_, ...), custom_call_target="tpu_custom_call" | custom-call | flops 20000000000 | bytes 1024 | tf_op jit(solution)/shard_map/group_logits/pallas_call | solution.py:39
  36.4 3.9 %collective-permute-start.12 = (f32[8,512]{1,0:T(8,128)S(1)}, f32[8,512]{1,0:T(8,128)S(1)}, u32[]{:S(2)}, u32[]{:S(2)}) collective-permute-start(f32[8,512]{1,0:T(8,128)S(1)} %get-tuple-element.53.refs_0_), channel_id=1, source_target_pairs={{0,3},{1,2},{2,1},{3,0},{4,7},{5,6},{6,5},{7,4},{8,11},{9,10},{10,... | collective-permute-start | bytes 49160 | tf_op jit(solution)/shard_map/ppermute | solution.py:24
  42.0 2.9 %collective-permute-done.11.refs_2_ = f32[8,512]{1,0:T(8,128)S(1)} collective-permute-done((f32[8,512]{1,0:T(8,128)S(1)}, f32[8,512]{1,0:T(8,128)S(1)}, u32[]{:S(2)}, u32[]{:S(2)}) %collective-permute-start.11) | collective-permute-done | bytes 16416 | tf_op jit(solution)/shard_map/ppermute | solution.py:24
  44.9 2.1 %slopes.2 = (bf16[896,896]{1,0:T(8,128)(2,1)S(1)}, bf16[256,896]{1,0:T(8,128)(2,1)S(1)}, bf16[256,896]{1,0:T(8,128)(2,1)S(1)}, f32[2,512]{1,0:T(2,128)S(1)}, f32...) custom-call(f32[8,512]{1,0:T(8,128)S(1)} %get-tuple-element.53.refs_0_, ...), custom_call_target="tpu_custom_call" | custom-call | flops 1024 | bytes 1024 | tf_op jit(solution)/shard_map/slopes/pallas_call | solution.py:39
  52.0 1.6 %collective-permute-start.16 = (bf16[448,896]{1,0:T(8,128)(2,1)S(1)}, bf16[448,896]{1,0:T(8,128)(2,1)S(1)}, u32[]{:S(2)}, u32[]{:S(2)}) collective-permute-start(bf16[448,896]{1,0:T(8,128)(2,1)S(1)} %get-tuple-element.69), channel_id=1, source_target_pairs={{0,16},{4,12},{8,24},{12,4},{16,0},{20,28},{24,8},{28,20},{1,17},{... | collective-permute-start | bytes 2408456 | tf_op jit(solution)/shard_map/ppermute | solution.py:24
  53.6 2.6 %hidden_grad.2 = (bf16[128,1792]{1,0:T(8,128)(2,1)S(1)}, f32[128,1792]{1,0:T(8,128)S(1)}) custom-call(bf16[448,896]{1,0:T(8,128)(2,1)S(1)} %get-tuple-element.64.refs_0_.refs_1_, bf16[256,896]{1,0:T(8,128)(2,1)S(1)} %get-tuple-element.62.refs_3_.refs_1_, bf16[256,1536]{1,0:T(8,128)(2,1)S(1)} %get-tuple-element.61.refs_3_.refs_2_, bf16[1792,2432]{1,0:T(8,128)(2,1)S(1)} %bitcast.5), custom_call_target="tpu_custom_call" | custom-call | flops 1024 | bytes 1024 | tf_op jit(solution)/shard_map/hidden_grad/pallas_call | solution.py:39
  58.7 1.6 %collective-permute-start.21 = (bf16[448,768]{1,0:T(8,128)(2,1)S(1)}, bf16[448,768]{1,0:T(8,128)(2,1)S(1)}, u32[]{:S(2)}, u32[]{:S(2)}) collective-permute-start(bf16[448,768]{1,0:T(8,128)(2,1)S(1)} %get-tuple-element.79), channel_id=1, source_target_pairs={{0,16},{4,12},{8,24},{12,4},{16,0},{20,28},{24,8},{28,20},{1,17},{... | collective-permute-start | bytes 2064392 | tf_op jit(solution)/shard_map/ppermute | solution.py:24
  60.3 2.6 %hidden_grad.3 = (bf16[128,1792]{1,0:T(8,128)(2,1)S(1)}, f32[128,1792]{1,0:T(8,128)S(1)}) custom-call(bf16[448,768]{1,0:T(8,128)(2,1)S(1)} %get-tuple-element.67.refs_0_.refs_1_, bf16[256,896]{1,0:T(8,128)(2,1)S(1)} %get-tuple-element.63.refs_4_.refs_1_, bf16[256,1536]{1,0:T(8,128)(2,1)S(1)} %get-tuple-element.60.refs_0_.refs_4_.refs_2_, ...), custom_call_target="tpu_custom_call" | custom-call | flops 1024 | bytes 1024 | tf_op jit(solution)/shard_map/hidden_grad/pallas_call | solution.py:39
  62.9 2.1 %collective-permute-start.20 = (bf16[128,1792]{1,0:T(8,128)(2,1)S(1)}, bf16[128,1792]{1,0:T(8,128)(2,1)S(1)}, u32[]{:S(2)}, u32[]{:S(2)}) collective-permute-start(bf16[128,1792]{1,0:T(8,128)(2,1)S(1)} %get-tuple-element.68.refs_0_), channel_id=1, source_target_pairs={{0,1},{1,0},{2,3},{3,2},{4,5},{5,4},{6,7},{7,6},{8,9},{9,8},{10,11... | collective-permute-start | bytes 1376264 | tf_op jit(solution)/shard_map/ppermute | solution.py:24
  65.1 4.5 %collective-permute-done.17.refs_2_ = bf16[128,1792]{1,0:T(8,128)(2,1)S(1)} collective-permute-done((bf16[128,1792]{1,0:T(8,128)(2,1)S(1)}, bf16[128,1792]{1,0:T(8,128)(2,1)S(1)}, u32[]{:S(2)}, u32[]{:S(2)}) %collective-permute-start.17) | collective-permute-done | bytes 458784 | tf_op jit(solution)/shard_map/ppermute | solution.py:24
  69.7 2.1 %collective-permute-start.18 = (bf16[64,1792]{1,0:T(8,128)(2,1)S(1)}, bf16[64,1792]{1,0:T(8,128)(2,1)S(1)}, u32[]{:S(2)}, u32[]{:S(2)}) collective-permute-start(bf16[64,1792]{1,0:T(8,128)(2,1)S(1)} %get-tuple-element.73), channel_id=1, source_target_pairs={{0,2},{1,3},{2,0},{3,1},{4,6},{5,7},{6,4},{7,5},{8,10},{9,11},{10,... | collective-permute-start | bytes 688136 | tf_op jit(solution)/shard_map/ppermute | solution.py:24
  71.8 1.6 %collective-permute-start.22 = (bf16[224,896]{1,0:T(8,128)(2,1)S(1)}, bf16[224,896]{1,0:T(8,128)(2,1)S(1)}, u32[]{:S(2)}, u32[]{:S(2)}) collective-permute-start(bf16[224,896]{1,0:T(8,128)(2,1)S(1)} %get-tuple-element.81), channel_id=1, source_target_pairs={{0,8},{4,20},{8,0},{12,28},{16,24},{20,4},{24,16},{28,12},{1,9},{5... | collective-permute-start | bytes 1204232 | tf_op jit(solution)/shard_map/ppermute | solution.py:24
  73.4 8.1 %collective-permute-done.18.refs_2_ = bf16[64,1792]{1,0:T(8,128)(2,1)S(1)} collective-permute-done((bf16[64,1792]{1,0:T(8,128)(2,1)S(1)}, bf16[64,1792]{1,0:T(8,128)(2,1)S(1)}, u32[]{:S(2)}, u32[]{:S(2)}) %collective-permute-start.18) | collective-permute-done | bytes 229408 | tf_op jit(solution)/shard_map/ppermute | solution.py:24
  82.3 1.3 %collective-permute-done.20.refs_2_ = bf16[128,1792]{1,0:T(8,128)(2,1)S(1)} collective-permute-done((bf16[128,1792]{1,0:T(8,128)(2,1)S(1)}, bf16[128,1792]{1,0:T(8,128)(2,1)S(1)}, u32[]{:S(2)}, u32[]{:S(2)}) %collective-permute-start.20) | collective-permute-done | bytes 458784 | tf_op jit(solution)/shard_map/ppermute | solution.py:24
  83.7 2.1 %collective-permute-start.24 = (bf16[64,1792]{1,0:T(8,128)(2,1)S(1)}, bf16[64,1792]{1,0:T(8,128)(2,1)S(1)}, u32[]{:S(2)}, u32[]{:S(2)}) collective-permute-start(bf16[64,1792]{1,0:T(8,128)(2,1)S(1)} %get-tuple-element.86), channel_id=1, source_target_pairs={{0,2},{1,3},{2,0},{3,1},{4,6},{5,7},{6,4},{7,5},{8,10},{9,11},{10,... | collective-permute-start | bytes 688136 | tf_op jit(solution)/shard_map/ppermute | solution.py:24
  86.0 1.6 %collective-permute-start.27 = (bf16[224,768]{1,0:T(8,128)(2,1)S(1)}, bf16[224,768]{1,0:T(8,128)(2,1)S(1)}, u32[]{:S(2)}, u32[]{:S(2)}) collective-permute-start(bf16[224,768]{1,0:T(8,128)(2,1)S(1)} %get-tuple-element.90), channel_id=1, source_target_pairs={{0,8},{4,20},{8,0},{12,28},{16,24},{20,4},{24,16},{28,12},{1,9},{5... | collective-permute-start | bytes 1032200 | tf_op jit(solution)/shard_map/ppermute | solution.py:24
  90.0 6.6 %collective-permute-done.24.refs_2_ = bf16[64,1792]{1,0:T(8,128)(2,1)S(1)} collective-permute-done((bf16[64,1792]{1,0:T(8,128)(2,1)S(1)}, bf16[64,1792]{1,0:T(8,128)(2,1)S(1)}, u32[]{:S(2)}, u32[]{:S(2)}) %collective-permute-start.24) | collective-permute-done | bytes 229408 | tf_op jit(solution)/shard_map/ppermute | solution.py:24
  96.6 1.9 %collective-permute-start.26 = (bf16[64,1792]{1,0:T(8,128)(2,1)S(1)}, bf16[64,1792]{1,0:T(8,128)(2,1)S(1)}, u32[]{:S(2)}, u32[]{:S(2)}) collective-permute-start(bf16[64,1792]{1,0:T(8,128)(2,1)S(1)} %add.11.refs_0_), channel_id=1, source_target_pairs={{0,16},{16,0},{1,17},{17,1},{2,18},{18,2},{3,19},{19,3},{4,20},{20... | collective-permute-start | bytes 688136 | tf_op jit(solution)/shard_map/ppermute | solution.py:24
  99.8 1.5 %finish.5 = (bf16[224,2432]{1,0:T(8,128)(2,1)}, f32[8,128]{1,0:T(8,128)}) custom-call(f32[1,512]{1,0:T(1,128)S(1)} %copy-done.2, bf16[224,2432]{1,0:T(8,128)(2,1)} %get-tuple-element.89.refs_1_, bf16[224,768]{1,0:T(8,128)(2,1)S(1)} %get-tuple-element.80.refs_0_.refs_2_, ...), custom_call_target="tpu_custom_call", output_to_operand_aliasing={{0}: (1, {})} | custom-call | flops 1024 | bytes 1024 | tf_op jit(solution)/shard_map/finish/pallas_call | solution.py:39
  101.3 2.4 %collective-permute-done.26 = bf16[64,1792]{1,0:T(8,128)(2,1)S(1)} collective-permute-done((bf16[64,1792]{1,0:T(8,128)(2,1)S(1)}, bf16[64,1792]{1,0:T(8,128)(2,1)S(1)}, u32[]{:S(2)}, u32[]{:S(2)}) %collective-permute-start.26) | collective-permute-done | bytes 229408 | tf_op jit(solution)/shard_map/ppermute | solution.py:24
  (72 shorter events, 18.8 us)
Async XLA Ops:
  1.6 9.5 %collective-permute-start.7 = (bf16[64,1792]{1,0:T(8,128)(2,1)S(1)}, bf16[64,1792]{1,0:T(8,128)(2,1)S(1)}, u32[]{:S(2)}, u32[]{:S(2)}) collective-permute-start(bf16[64,1792]{1,0:T(8,128)(2,1)S(1)} %pick_rows.3.refs_0_), channel_id=1, source_target_pairs={{0,16},{16,0},{1,17},{17,1},{2,18},{18,2},{3,19},{19,3},{4,20},{20... | collective-permute-start | bytes 688136 | tf_op jit(solution)/shard_map/ppermute | solution.py:24
  5.6 10.7 %collective-permute-start = (bf16[64,1920]{1,0:T(8,128)(2,1)S(1)}, bf16[64,1920]{1,0:T(8,128)(2,1)S(1)}, u32[]{:S(2)}, u32[]{:S(2)}) collective-permute-start(bf16[64,1920]{1,0:T(8,128)(2,1)S(1)} %pick_rows.4.refs_0_), channel_id=1, source_target_pairs={{0,16},{16,0},{1,17},{17,1},{2,18},{18,2},{3,19},{19,3},{4,20},{20... | collective-permute-start | bytes 737288 | tf_op jit(solution)/shard_map/ppermute | solution.py:24
  6.9 14.3 %collective-permute-start.3 = (bf16[64,1792]{1,0:T(8,128)(2,1)S(1)}, bf16[64,1792]{1,0:T(8,128)(2,1)S(1)}, u32[]{:S(2)}, u32[]{:S(2)}) collective-permute-start(bf16[64,1792]{1,0:T(8,128)(2,1)S(1)} %get-tuple-element.49), channel_id=1, source_target_pairs={{0,16},{16,0},{1,17},{17,1},{2,18},{18,2},{3,19},{19,3},{4,20},{20... | collective-permute-start | bytes 688136 | tf_op jit(solution)/shard_map/ppermute | solution.py:24
  8.8 19.8 %slice-start = ((s8[8716288]{0:T(1024)(128)(4,1)}), s8[4194304]{0:T(1024)(128)(4,1)S(1)}, s32[]{:S(2)}) async-start(s8[8716288]{0:T(1024)(128)(4,1)} %bitcast.4), calls=%async_computation | async-start | bytes 8388608
  8.9 9.7 %copy-start.1 = (s32[512]{0:T(512)S(1)}, s32[512]{0:T(512)}, u32[]{:S(2)}) copy-start(s32[512]{0:T(512)} %param.9) | copy-start | bytes 6148
  8.9 19.8 %slice-start.1 = ((s8[8716288]{0:T(1024)(128)(4,1)}), s8[4194304]{0:T(1024)(128)(4,1)S(1)}, s32[]{:S(2)}) async-start(s8[8716288]{0:T(1024)(128)(4,1)} %bitcast.4), calls=%async_computation.1 | async-start | bytes 8388608
  8.9 19.8 %slice-start.2 = ((s8[8716288]{0:T(1024)(128)(4,1)}), s8[327680]{0:T(1024)(128)(4,1)S(1)}, s32[]{:S(2)}) async-start(s8[8716288]{0:T(1024)(128)(4,1)} %bitcast.4), calls=%async_computation.2 | async-start | bytes 655360
  8.9 16.4 %collective-permute-start.4 = (bf16[64,1792]{1,0:T(8,128)(2,1)S(1)}, bf16[64,1792]{1,0:T(8,128)(2,1)S(1)}, u32[]{:S(2)}, u32[]{:S(2)}) collective-permute-start(bf16[64,1792]{1,0:T(8,128)(2,1)S(1)} %get-tuple-element.50), channel_id=1, source_target_pairs={{0,16},{16,0},{1,17},{17,1},{2,18},{18,2},{3,19},{19,3},{4,20},{20... | collective-permute-start | bytes 688136 | tf_op jit(solution)/shard_map/ppermute | solution.py:24
  11.1 17.6 %collective-permute-start.8 = (bf16[64,1792]{1,0:T(8,128)(2,1)S(1)}, bf16[64,1792]{1,0:T(8,128)(2,1)S(1)}, u32[]{:S(2)}, u32[]{:S(2)}) collective-permute-start(bf16[64,1792]{1,0:T(8,128)(2,1)S(1)} %pass_on.3.refs_1_), channel_id=1, source_target_pairs={{0,1},{1,0},{2,3},{3,2},{4,5},{5,4},{6,7},{7,6},{8,9},{9,8},{10,11... | collective-permute-start | bytes 688136 | tf_op jit(solution)/shard_map/ppermute | solution.py:24
  16.3 12.3 %collective-permute-start.9 = (bf16[64,1792]{1,0:T(8,128)(2,1)S(1)}, bf16[64,1792]{1,0:T(8,128)(2,1)S(1)}, u32[]{:S(2)}, u32[]{:S(2)}) collective-permute-start(bf16[64,1792]{1,0:T(8,128)(2,1)S(1)} %get-tuple-element.51.refs_2_), channel_id=1, source_target_pairs={{0,1},{1,0},{2,3},{3,2},{4,5},{5,4},{6,7},{7,6},{8,9},{9,8},{10,11... | collective-permute-start | bytes 688136 | tf_op jit(solution)/shard_map/ppermute | solution.py:24
  18.7 4.7 %collective-permute-start.1 = (f32[8,128]{1,0:T(8,128)S(1)}, f32[8,128]{1,0:T(8,128)S(1)}, u32[]{:S(2)}, u32[]{:S(2)}) collective-permute-start(f32[8,128]{1,0:T(8,128)S(1)} %count_rows.1.refs_0_), channel_id=1, source_target_pairs={{0,4},{4,0},{8,12},{12,8},{1,5},{5,1},{9,13},{13,9},{2,6},{6,2},{1... | collective-permute-start | bytes 12296 | tf_op jit(solution)/shard_map/ppermute | solution.py:24
  21.2 11.4 %collective-permute-start.5 = (bf16[64,1792]{1,0:T(8,128)(2,1)S(1)}, bf16[64,1792]{1,0:T(8,128)(2,1)S(1)}, u32[]{:S(2)}, u32[]{:S(2)}) collective-permute-start(bf16[64,1792]{1,0:T(8,128)(2,1)S(1)} %collective-permute-done.3.refs_1_), channel_id=1, source_target_pairs={{0,1},{1,0},{2,3},{3,2},{4,5},{5,4},{6,7},{7,6},{8,9},{9,8},{10,11... | collective-permute-start | bytes 688136 | tf_op jit(solution)/shard_map/ppermute | solution.py:24
  25.3 7.3 %collective-permute-start.6 = (bf16[64,1792]{1,0:T(8,128)(2,1)S(1)}, bf16[64,1792]{1,0:T(8,128)(2,1)S(1)}, u32[]{:S(2)}, u32[]{:S(2)}) collective-permute-start(bf16[64,1792]{1,0:T(8,128)(2,1)S(1)} %pass_on.2.refs_0_.refs_2_), channel_id=1, source_target_pairs={{0,1},{1,0},{2,3},{3,2},{4,5},{5,4},{6,7},{7,6},{8,9},{9,8},{10,11... | collective-permute-start | bytes 688136 | tf_op jit(solution)/shard_map/ppermute | solution.py:24
  27.1 5.4 %collective-permute-start.2 = (f32[8,128]{1,0:T(8,128)S(1)}, f32[8,128]{1,0:T(8,128)S(1)}, u32[]{:S(2)}, u32[]{:S(2)}) collective-permute-start(f32[8,128]{1,0:T(8,128)S(1)} %sum_rows.1.refs_0_.refs_5_), channel_id=1, source_target_pairs={{0,8},{4,12},{8,0},{12,4},{1,9},{5,13},{9,1},{13,5},{2,10},{6,14},... | collective-permute-start | bytes 12296 | tf_op jit(solution)/shard_map/ppermute | solution.py:24
  36.4 5.6 %collective-permute-start.12 = (f32[8,512]{1,0:T(8,128)S(1)}, f32[8,512]{1,0:T(8,128)S(1)}, u32[]{:S(2)}, u32[]{:S(2)}) collective-permute-start(f32[8,512]{1,0:T(8,128)S(1)} %get-tuple-element.53.refs_0_), channel_id=1, source_target_pairs={{0,3},{1,2},{2,1},{3,0},{4,7},{5,6},{6,5},{7,4},{8,11},{9,10},{10,... | collective-permute-start | bytes 49160 | tf_op jit(solution)/shard_map/ppermute | solution.py:24
  40.3 4.6 %collective-permute-start.11 = (f32[8,512]{1,0:T(8,128)S(1)}, f32[8,512]{1,0:T(8,128)S(1)}, u32[]{:S(2)}, u32[]{:S(2)}) collective-permute-start(f32[8,512]{1,0:T(8,128)S(1)} %get-tuple-element.53.refs_0_), channel_id=1, source_target_pairs={{0,2},{1,3},{2,0},{3,1},{4,6},{5,7},{6,4},{7,5},{8,10},{9,11},{10,... | collective-permute-start | bytes 49160 | tf_op jit(solution)/shard_map/ppermute | solution.py:24
  40.3 4.6 %collective-permute-start.10 = (f32[8,512]{1,0:T(8,128)S(1)}, f32[8,512]{1,0:T(8,128)S(1)}, u32[]{:S(2)}, u32[]{:S(2)}) collective-permute-start(f32[8,512]{1,0:T(8,128)S(1)} %get-tuple-element.53.refs_0_), channel_id=1, source_target_pairs={{0,1},{1,0},{2,3},{3,2},{4,5},{5,4},{6,7},{7,6},{8,9},{9,8},{10,11... | collective-permute-start | bytes 49160 | tf_op jit(solution)/shard_map/ppermute | solution.py:24
  47.1 3.8 %collective-permute-start.13 = (bf16[896,896]{1,0:T(8,128)(2,1)S(1)}, bf16[896,896]{1,0:T(8,128)(2,1)S(1)}, u32[]{:S(2)}, u32[]{:S(2)}) collective-permute-start(bf16[896,896]{1,0:T(8,128)(2,1)S(1)} %get-tuple-element.56.refs_0_), channel_id=1, source_target_pairs={{0,4},{4,0},{8,12},{12,8},{16,20},{20,16},{24,28},{28,24},{1,5},{5... | collective-permute-start | bytes 4816904 | tf_op jit(solution)/shard_map/ppermute | solution.py:24
  49.4 6.9 %collective-permute-start.14 = (bf16[896,768]{1,0:T(8,128)(2,1)S(1)}, bf16[896,768]{1,0:T(8,128)(2,1)S(1)}, u32[]{:S(2)}, u32[]{:S(2)}) collective-permute-start(bf16[896,768]{1,0:T(8,128)(2,1)S(1)} %weight_away.2.refs_0_), channel_id=1, source_target_pairs={{0,4},{4,0},{8,12},{12,8},{16,20},{20,16},{24,28},{28,24},{1,5},{5... | collective-permute-start | bytes 4128776 | tf_op jit(solution)/shard_map/ppermute | solution.py:24
  50.8 7.0 %collective-permute-start.15 = (bf16[896,768]{1,0:T(8,128)(2,1)S(1)}, bf16[896,768]{1,0:T(8,128)(2,1)S(1)}, u32[]{:S(2)}, u32[]{:S(2)}) collective-permute-start(bf16[896,768]{1,0:T(8,128)(2,1)S(1)} %weight_away.3.refs_0_), channel_id=1, source_target_pairs={{0,4},{4,0},{8,12},{12,8},{16,20},{20,16},{24,28},{28,24},{1,5},{5... | collective-permute-start | bytes 4128776 | tf_op jit(solution)/shard_map/ppermute | solution.py:24
  52.0 12.9 %collective-permute-start.16 = (bf16[448,896]{1,0:T(8,128)(2,1)S(1)}, bf16[448,896]{1,0:T(8,128)(2,1)S(1)}, u32[]{:S(2)}, u32[]{:S(2)}) collective-permute-start(bf16[448,896]{1,0:T(8,128)(2,1)S(1)} %get-tuple-element.69), channel_id=1, source_target_pairs={{0,16},{4,12},{8,24},{12,4},{16,0},{20,28},{24,8},{28,20},{1,17},{... | collective-permute-start | bytes 2408456 | tf_op jit(solution)/shard_map/ppermute | solution.py:24
  56.2 13.4 %collective-permute-start.17 = (bf16[128,1792]{1,0:T(8,128)(2,1)S(1)}, bf16[128,1792]{1,0:T(8,128)(2,1)S(1)}, u32[]{:S(2)}, u32[]{:S(2)}) collective-permute-start(bf16[128,1792]{1,0:T(8,128)(2,1)S(1)} %get-tuple-element.65.refs_0_), channel_id=1, source_target_pairs={{0,1},{1,0},{2,3},{3,2},{4,5},{5,4},{6,7},{7,6},{8,9},{9,8},{10,11... | collective-permute-start | bytes 1376264 | tf_op jit(solution)/shard_map/ppermute | solution.py:24
  57.2 24.4 %collective-permute-start.19 = (bf16[448,768]{1,0:T(8,128)(2,1)S(1)}, bf16[448,768]{1,0:T(8,128)(2,1)S(1)}, u32[]{:S(2)}, u32[]{:S(2)}) collective-permute-start(bf16[448,768]{1,0:T(8,128)(2,1)S(1)} %get-tuple-element.75), channel_id=1, source_target_pairs={{0,16},{4,12},{8,24},{12,4},{16,0},{20,28},{24,8},{28,20},{1,17},{... | collective-permute-start | bytes 2064392 | tf_op jit(solution)/shard_map/ppermute | solution.py:24
  58.7 27.1 %collective-permute-start.21 = (bf16[448,768]{1,0:T(8,128)(2,1)S(1)}, bf16[448,768]{1,0:T(8,128)(2,1)S(1)}, u32[]{:S(2)}, u32[]{:S(2)}) collective-permute-start(bf16[448,768]{1,0:T(8,128)(2,1)S(1)} %get-tuple-element.79), channel_id=1, source_target_pairs={{0,16},{4,12},{8,24},{12,4},{16,0},{20,28},{24,8},{28,20},{1,17},{... | collective-permute-start | bytes 2064392 | tf_op jit(solution)/shard_map/ppermute | solution.py:24
  62.9 20.8 %collective-permute-start.20 = (bf16[128,1792]{1,0:T(8,128)(2,1)S(1)}, bf16[128,1792]{1,0:T(8,128)(2,1)S(1)}, u32[]{:S(2)}, u32[]{:S(2)}) collective-permute-start(bf16[128,1792]{1,0:T(8,128)(2,1)S(1)} %get-tuple-element.68.refs_0_), channel_id=1, source_target_pairs={{0,1},{1,0},{2,3},{3,2},{4,5},{5,4},{6,7},{7,6},{8,9},{9,8},{10,11... | collective-permute-start | bytes 1376264 | tf_op jit(solution)/shard_map/ppermute | solution.py:24
  69.7 11.8 %collective-permute-start.18 = (bf16[64,1792]{1,0:T(8,128)(2,1)S(1)}, bf16[64,1792]{1,0:T(8,128)(2,1)S(1)}, u32[]{:S(2)}, u32[]{:S(2)}) collective-permute-start(bf16[64,1792]{1,0:T(8,128)(2,1)S(1)} %get-tuple-element.73), channel_id=1, source_target_pairs={{0,2},{1,3},{2,0},{3,1},{4,6},{5,7},{6,4},{7,5},{8,10},{9,11},{10,... | collective-permute-start | bytes 688136 | tf_op jit(solution)/shard_map/ppermute | solution.py:24
  71.8 16.4 %collective-permute-start.22 = (bf16[224,896]{1,0:T(8,128)(2,1)S(1)}, bf16[224,896]{1,0:T(8,128)(2,1)S(1)}, u32[]{:S(2)}, u32[]{:S(2)}) collective-permute-start(bf16[224,896]{1,0:T(8,128)(2,1)S(1)} %get-tuple-element.81), channel_id=1, source_target_pairs={{0,8},{4,20},{8,0},{12,28},{16,24},{20,4},{24,16},{28,12},{1,9},{5... | collective-permute-start | bytes 1204232 | tf_op jit(solution)/shard_map/ppermute | solution.py:24
  81.7 7.3 %collective-permute-start.23 = (bf16[224,768]{1,0:T(8,128)(2,1)S(1)}, bf16[224,768]{1,0:T(8,128)(2,1)S(1)}, u32[]{:S(2)}, u32[]{:S(2)}) collective-permute-start(bf16[224,768]{1,0:T(8,128)(2,1)S(1)} %get-tuple-element.84), channel_id=1, source_target_pairs={{0,8},{4,20},{8,0},{12,28},{16,24},{20,4},{24,16},{28,12},{1,9},{5... | collective-permute-start | bytes 1032200 | tf_op jit(solution)/shard_map/ppermute | solution.py:24
  83.7 12.8 %collective-permute-start.24 = (bf16[64,1792]{1,0:T(8,128)(2,1)S(1)}, bf16[64,1792]{1,0:T(8,128)(2,1)S(1)}, u32[]{:S(2)}, u32[]{:S(2)}) collective-permute-start(bf16[64,1792]{1,0:T(8,128)(2,1)S(1)} %get-tuple-element.86), channel_id=1, source_target_pairs={{0,2},{1,3},{2,0},{3,1},{4,6},{5,7},{6,4},{7,5},{8,10},{9,11},{10,... | collective-permute-start | bytes 688136 | tf_op jit(solution)/shard_map/ppermute | solution.py:24
  86.0 13.1 %collective-permute-start.27 = (bf16[224,768]{1,0:T(8,128)(2,1)S(1)}, bf16[224,768]{1,0:T(8,128)(2,1)S(1)}, u32[]{:S(2)}, u32[]{:S(2)}) collective-permute-start(bf16[224,768]{1,0:T(8,128)(2,1)S(1)} %get-tuple-element.90), channel_id=1, source_target_pairs={{0,8},{4,20},{8,0},{12,28},{16,24},{20,4},{24,16},{28,12},{1,9},{5... | collective-permute-start | bytes 1032200 | tf_op jit(solution)/shard_map/ppermute | solution.py:24
  87.6 10.9 %collective-permute-start.25 = (bf16[64,1920]{1,0:T(8,128)(2,1)S(1)}, bf16[64,1920]{1,0:T(8,128)(2,1)S(1)}, u32[]{:S(2)}, u32[]{:S(2)}) collective-permute-start(bf16[64,1920]{1,0:T(8,128)(2,1)S(1)} %pack.1.refs_0_), channel_id=1, source_target_pairs={{0,16},{16,0},{1,17},{17,1},{2,18},{18,2},{3,19},{19,3},{4,20},{20... | collective-permute-start | bytes 737288 | tf_op jit(solution)/shard_map/ppermute | solution.py:24
  96.6 7.1 %collective-permute-start.26 = (bf16[64,1792]{1,0:T(8,128)(2,1)S(1)}, bf16[64,1792]{1,0:T(8,128)(2,1)S(1)}, u32[]{:S(2)}, u32[]{:S(2)}) collective-permute-start(bf16[64,1792]{1,0:T(8,128)(2,1)S(1)} %add.11.refs_0_), channel_id=1, source_target_pairs={{0,16},{16,0},{1,17},{17,1},{2,18},{18,2},{3,19},{19,3},{4,20},{20... | collective-permute-start | bytes 688136 | tf_op jit(solution)/shard_map/ppermute | solution.py:24
  (2 other events, 4.2 us)
